TPU v7x, 32 devices: a whole 2x2x4 slice. The times are simulated.
32 devices in a mesh: groups: 2 (over y), row: 4 (over z), col: 2 (over x), chan: 2 (over core).
Axes of the slice: x: 2, y: 2, z: 4, core: 2. Of those that a mesh axis runs over, the one named last changes fastest.
Arguments:
- pair_input: bfloat16 [512, 256, 128], P(('groups', 'row'), ('col', 'chan')), parts along dimension 0, may hold values from -6 to 6
- alignment_features: bfloat16 [128, 512, 64], P('row', ('groups', 'col', 'chan')), parts along dimension 1, may hold values from -6 to 6
- alignment_mask: int32 [128, 512], P('row', ('groups', 'col', 'chan')), parts along dimension 1, may hold values from 0 to 1
- token_valid: int32 [512], P('groups'), parts along dimension 0, may hold values from 0 to 1, as said below
- left_weight: bfloat16 [64, 32], replicated, may hold values from -0.75 to 0.75
- right_weight: bfloat16 [64, 32], replicated, may hold values from -0.75 to 0.75
- output_weight: bfloat16 [1024, 128], replicated, may hold values from -1.75 to 1.75
- gate_weight: bfloat16 [128, 512], replicated, may hold values from -0.5 to 0.5
- up_weight: bfloat16 [128, 512], replicated, may hold values from -0.5 to 0.5
- down_weight: bfloat16 [512, 128], replicated, may hold values from -0.25 to 0.25
- kernel_weight: bfloat16 [3, 3, 128, 128], replicated, may hold values from -0.1875 to 0.1875
Outputs:
- pair_out: bfloat16 [512, 256, 128], P(('groups', 'row'), ('col', 'chan')), parts along dimension 0
There are 2 independent parts, one for each index of `groups`. A program takes and returns all parts, laid end to end along the dimension named above; an argument that names none is the same for every part. Nothing has to cross between parts.
Inputs may be any that keep to these rules, and one draw needn't show every extreme that they name: `token_valid`: the ones come first.
All inputs are finite; a program needn't handle non-finite values.
Results may differ from a plain program's by a relative error of at most 0.014.
Values may be sent and summed in bfloat16 or wider, within the bound.
No kernel may reach another device: no remote copies, remote signals or barrier semaphores. Data moves between devices by JAX's collectives and lax.ppermute only.
A program may use at most 64 MiB of HBM per device.

v0:
```python
import math

import jax
import jax.numpy as jnp
from jax import lax
from jax.sharding import PartitionSpec as P

epsilon = 1e-05


def with_halo(value, sides, width):
    for axis, dim in sides:
        size, length = (lax.axis_size(axis), value.shape[dim])
        up = [(i, (i + 1) % size) for i in range(size - 1)]
        down = [(j, i) for i, j in up]
        last = lax.slice_in_dim(value, length - width, length, axis=dim)
        initial = lax.slice_in_dim(value, 0, width, axis=dim)
        before = lax.ppermute(last, axis, up)
        after = lax.ppermute(initial, axis, down)
        value = jnp.concatenate([before, value, after], axis=dim)
    return value


def transition(pair_rows, gate_weight, up_weight, down_weight):
    values = pair_rows.astype(jnp.float32)
    centre = jnp.mean(values, axis=-1, keepdims=True)
    spread = jnp.mean(jnp.square(values - centre), axis=-1, keepdims=True)
    normed = ((values - centre) * lax.rsqrt(spread + epsilon)).astype(jnp.bfloat16)
    gate_act = jnp.dot(normed, gate_weight, preferred_element_type=jnp.float32)
    up_act = jnp.dot(normed, up_weight, preferred_element_type=jnp.float32)
    hidden = (jax.nn.silu(gate_act) * up_act).astype(jnp.bfloat16)
    return (values + jnp.dot(hidden, down_weight, preferred_element_type=jnp.float32)).astype(
        jnp.bfloat16
    )


def on_device(
    pair_input,
    alignment_features,
    alignment_mask,
    token_valid,
    left_weight,
    right_weight,
    output_weight,
    gate_weight,
    up_weight,
    down_weight,
    kernel_weight,
):
    rows_dev, cols_dev, channels = pair_input.shape
    local_row_count, local_token_count, alignment_width = alignment_features.shape
    opm_width = left_weight.shape[1]
    row_count = lax.axis_size("row")
    col_count = lax.axis_size(("col", "chan"))
    fold_ratio = row_count // col_count
    row_index = lax.axis_index("row")
    col_index = lax.axis_index(("col", "chan"))
    halved_mask = alignment_mask.astype(jnp.bfloat16)
    column_mask = alignment_mask.reshape(local_row_count * local_token_count, 1).astype(jnp.float32)
    alignment_flat = alignment_features.reshape(
        local_row_count * local_token_count, alignment_width
    )
    left_local = (
        jnp.dot(alignment_flat, left_weight, preferred_element_type=jnp.float32) * column_mask
    ).astype(jnp.bfloat16)
    left_local = left_local.reshape(local_row_count, local_token_count, opm_width)
    right_local = (
        jnp.dot(alignment_flat, right_weight, preferred_element_type=jnp.float32) * column_mask
    ).astype(jnp.bfloat16)
    right_local = right_local.reshape(local_row_count, local_token_count, opm_width)
    right_projected, right_mask = (
        lax.all_gather(right_local, "row", axis=0, tiled=True),
        lax.all_gather(halved_mask, "row", axis=0, tiled=True),
    )
    wide_left, wide_mask = (
        lax.all_gather(left_local, ("col", "chan"), axis=1, tiled=True),
        lax.all_gather(halved_mask, ("col", "chan"), axis=1, tiled=True),
    )
    left_projected, left_mask = (
        lax.all_to_all(wide_left, "row", split_axis=1, concat_axis=0, tiled=True),
        lax.all_to_all(wide_mask, "row", split_axis=1, concat_axis=0, tiled=True),
    )
    depth_all = left_projected.shape[0]
    counts = lax.dot_general(
        left_mask, right_mask, (((0,), (0,)), ((), ())), preferred_element_type=jnp.float32
    )
    right_flat = right_projected.reshape(depth_all, cols_dev * opm_width)
    strip_rows = math.gcd(16, rows_dev)

    def outer_rows(first_row):
        left_part = lax.dynamic_slice_in_dim(left_projected, first_row, strip_rows, 1).reshape(
            depth_all, strip_rows * opm_width
        )
        products = lax.dot_general(
            left_part, right_flat, (((0,), (0,)), ((), ())), preferred_element_type=jnp.float32
        )
        products = products.reshape(strip_rows, opm_width, cols_dev, opm_width).transpose(
            0, 2, 1, 3
        )
        products = products.reshape(strip_rows * cols_dev, opm_width * opm_width).astype(
            jnp.bfloat16
        )
        update = jnp.dot(products, output_weight, preferred_element_type=jnp.float32).reshape(
            strip_rows, cols_dev, channels
        )
        pair_count = lax.dynamic_slice_in_dim(counts, first_row, strip_rows, 0)
        update = update / jnp.maximum(pair_count, 1.0)[:, :, None]
        base_pair = lax.dynamic_slice_in_dim(pair_input, first_row, strip_rows, 0).astype(
            jnp.float32
        )
        return (base_pair + update).astype(jnp.bfloat16)

    starts = jnp.arange(rows_dev // strip_rows, dtype=jnp.int32) * strip_rows
    pair_one = lax.map(outer_rows, starts).reshape(rows_dev, cols_dev, channels)

    def apply_transition(pair_tile):
        total_rows = rows_dev * cols_dev
        slab_size = math.gcd(1024, total_rows)
        pair_slabs = pair_tile.reshape(total_rows // slab_size, slab_size, channels)

        def one_slab(pair_slab):
            return transition(pair_slab, gate_weight, up_weight, down_weight)

        return lax.map(one_slab, pair_slabs).reshape(rows_dev, cols_dev, channels)

    share_rows = rows_dev // col_count
    second_step = lax.all_to_all(
        lax.all_to_all(pair_one, ("col", "chan"), split_axis=0, concat_axis=1, tiled=True),
        "row",
        split_axis=1,
        concat_axis=0,
        tiled=True,
    )
    flipped = jnp.swapaxes(second_step, 0, 1)
    third_step = lax.all_to_all(flipped, ("col", "chan"), split_axis=1, concat_axis=1, tiled=True)
    arranged = third_step.reshape(rows_dev, col_count, fold_ratio, share_rows, channels).transpose(
        0, 2, 1, 3, 4
    )
    mirrored_one = arranged.reshape(rows_dev, cols_dev, channels)
    pair_two = apply_transition(pair_one)
    pair_mirror = apply_transition(mirrored_one)
    pad_real = token_valid.astype(jnp.float32)
    pad_rows = lax.dynamic_slice_in_dim(pad_real, row_index * rows_dev, rows_dev)
    pad_cols = lax.dynamic_slice_in_dim(pad_real, col_index * cols_dev, cols_dev)
    symmetric = (pair_two.astype(jnp.float32) + pair_mirror.astype(jnp.float32)) * 0.5
    masked = (symmetric * pad_rows[:, None, None] * pad_cols[None, :, None]).astype(jnp.bfloat16)
    padded = with_halo(masked, (("row", 0), (("col", "chan"), 1)), 1)
    summed = jnp.zeros((rows_dev * cols_dev, channels), jnp.float32)
    for shift_row in range(3):
        for shift_col in range(3):
            shifted = padded[
                shift_row : shift_row + rows_dev, shift_col : shift_col + cols_dev
            ].reshape(rows_dev * cols_dev, channels)
            summed = summed + jnp.dot(
                shifted, kernel_weight[shift_row, shift_col], preferred_element_type=jnp.float32
            )
    result = symmetric.reshape(rows_dev * cols_dev, channels) + summed
    return result.astype(jnp.bfloat16).reshape(rows_dev, cols_dev, channels)


def solution(mesh):
    placed = (
        P(("groups", "row"), ("col", "chan"), None),
        P("row", ("groups", "col", "chan"), None),
        P("row", ("groups", "col", "chan")),
        P("groups"),
        P(),
        P(),
        P(),
        P(),
        P(),
        P(),
        P(),
    )
    return jax.shard_map(
        on_device,
        mesh=mesh,
        in_specs=placed,
        out_specs=P(("groups", "row"), ("col", "chan"), None),
        check_vma=False,
    )
```

profile of v0, /device:TPU:1, one launch (start us, length us, event | category | flops | bytes accessed | tf_op | source)
XLA Modules:
  0.0 240.0 jit_solution(9252353414318188215)
XLA Ops:
  0.8 6.0 %all-gather = bf16[4,64,32]{1,2,0:T(8,128)(2,1)S(1)} all-gather(bf16[1,64,32]{1,2,0:T(8,128)(2,1)S(1)} %bitcast.246), channel_id=1, replica_groups=mesh['groups'=2,'row'=4,'col'=2,'chan'=2] {'col','chan'}, dimensions={0}, use_global_device_ids=true | all-gather | bytes 20480 | tf_op jit(solution)/shard_map/all_gather | solution.py:77
  7.8 5.1 %all-to-all-start.1 = ((bf16[4,2,1024]{2,1,0:T(2,128)(2,1)}), bf16[4,2,1024]{2,1,0:T(2,128)(2,1)S(1)}, u32[]{:S(2)}, u32[]{:S(2)}) async-start(bf16[4,2,1024]{2,1,0:T(2,128)(2,1)} %reshape.147), calls=%async_computation.1 | async-start | bytes 32768 | tf_op jit(solution)/shard_map/all_to_all | solution.py:81
  15.0 16.0 %all_gather.12 = bf16[32,256,32]{2,0,1:T(8,128)(2,1)S(1)} all-gather(bf16[32,64,32]{2,0,1:T(8,128)(2,1)S(1)} %copy.48), channel_id=1, replica_groups=mesh['groups'=2,'row'=4,'col'=2,'chan'=2] {'col','chan'}, dimensions={1}, use_global_device_ids=true | all-gather | bytes 655360 | tf_op jit(solution)/shard_map/all_gather | solution.py:76
  31.1 2.9 %reshape.145 = bf16[4,2,32768]{2,1,0:T(2,128)(2,1)} reshape(bf16[256,32,32]{2,1,0:T(8,128)(2,1)S(1)} %bitcast.227) | data formatting | bytes 1048576
  34.0 4.8 %all-to-all-start = ((bf16[4,2,32768]{2,1,0:T(2,128)(2,1)}), bf16[4,2,32768]{2,1,0:T(2,128)(2,1)S(1)}, u32[]{:S(2)}, u32[]{:S(2)}) async-start(bf16[4,2,32768]{2,1,0:T(2,128)(2,1)} %reshape.145), calls=%async_computation | async-start | bytes 1048576 | tf_op jit(solution)/shard_map/all_to_all | solution.py:80
  39.4 28.4 %all_gather.13 = bf16[128,64,32]{1,2,0:T(8,128)(2,1)S(1)} all-gather(bf16[32,64,32]{1,2,0:T(8,128)(2,1)S(1)} %copy.51), channel_id=1, replica_groups=mesh['groups'=2,'row'=4,'col'=2,'chan'=2] {'row'}, dimensions={0}, use_global_device_ids=true | all-gather | bytes 655360 | tf_op jit(solution)/shard_map/all_gather | solution.py:72
  69.4 10.2 %all_gather.15 = bf16[128,64]{1,0:T(8,128)(2,1)S(1)} all-gather(bf16[32,64]{1,0:T(8,128)(2,1)S(1)} %get-tuple-element.203), channel_id=1, replica_groups=mesh['groups'=2,'row'=4,'col'=2,'chan'=2] {'row'}, dimensions={0}, use_global_device_ids=true | all-gather | bytes 20480 | tf_op jit(solution)/shard_map/all_gather | solution.py:73
  82.3 3.5 %copy.63 = bf16[32,4,64,32]{2,1,3,0:T(4,128)(2,1)S(1)} copy(bf16[32,4,64,32]{3,0,2,1:T(8,128)(2,1)} %bitcast.228) | data formatting | bytes 1048576 | tf_op jit(solution)/shard_map/all_to_all | solution.py:80
  87.0 2.8 %copy.55 = bf16[128,64,32]{0,2,1:T(8,128)(2,1)S(1)} copy(bf16[128,64,32]{1,2,0:T(8,128)(2,1)} %bitcast.240) | data formatting | bytes 1048576 | tf_op jit(solution)/shard_map/while | solution.py:114
  89.8 31.8 %while.30 = (s32[]{:T(128)}, bf16[4,16,64,128]{3,2,1,0:T(8,128)(2,1)S(1)}, s32[4]{0:T(128)S(1)}, bf16[64,64,128]{2,1,0:T(8,128)(2,1)}, bf16[128,64,32]{0,2,1:T(8...) while((s32[]{:T(128)}, ...), condition=%wide.region_1.2_spmd, body=%wide.region_0.1_spmd.sunk | while | flops 538444800 | bytes 11944115 | solution.py:114
  121.7 21.9 %all_to_all.78 = bf16[64,64,128]{2,1,0:T(8,128)(2,1)S(1)} all-to-all(bf16[64,64,128]{2,1,0:T(8,128)(2,1)S(1)} %bitcast.222), channel_id=1, replica_groups=mesh['groups'=2,'row'=4,'col'=2,'chan'=2] {'col','chan'}, dimensions={0} | all-to-all | bytes 2097152 | tf_op jit(solution)/shard_map/all_to_all | solution.py:128
  145.3 3.5 %all-to-all-start.3 = ((bf16[16,256,128]{2,0,1:T(8,128)(2,1)}), bf16[16,256,128]{2,0,1:T(8,128)(2,1)S(1)}, u32[]{:S(2)}, u32[]{:S(2)}) async-start(bf16[16,256,128]{2,0,1:T(8,128)(2,1)} %copy.57), calls=%async_computation.3 | async-start | bytes 2097152 | tf_op jit(solution)/shard_map/all_to_all | solution.py:127
  149.3 24.7 %all-to-all-done.3 = bf16[16,256,128]{2,0,1:T(8,128)(2,1)S(1)} async-done(((bf16[16,256,128]{2,0,1:T(8,128)(2,1)}), bf16[16,256,128]{2,0,1:T(8,128)(2,1)S(1)}, u32[]{:S(2)}, u32[]{:S(2)}) %all-to-all-start.3) | async-done | bytes 1048608 | tf_op jit(solution)/shard_map/all_to_all | solution.py:127
  175.3 5.8 %all-to-all-start.4 = ((bf16[64,64,128]{2,0,1:T(8,128)(2,1)}), bf16[64,64,128]{2,0,1:T(8,128)(2,1)}, u32[]{:S(2)}, u32[]{:S(2)}) async-start(bf16[64,64,128]{2,0,1:T(8,128)(2,1)} %bitcast.36), calls=%async_computation.4 | async-start | bytes 2097152 | tf_op jit(solution)/shard_map/all_to_all | solution.py:135
  182.2 14.7 %while.31 = (s32[]{:T(128)}, bf16[4,1024,128]{2,1,0:T(8,128)(2,1)}, bf16[4,1024,128]{2,1,0:T(8,128)(2,1)S(1)}, bf16[128,512]{1,0:T(8,128)(2,1)S(1)}, bf16[128,51...) while((s32[]{:T(128)}, bf16[4,1024,128]{2,1,0:T(8,128)(2,1)}, ...), condition=%wide.region_5.6_spmd, body=%wide.region_2.5_spmd.sunk | while | flops 408028160 | bytes 6206561 | solution.py:124
  183.2 2.7 %fusion.151 = bf16[4,1024,128]{2,1,0:T(8,128)(2,1)} fusion(bf16[4,1024,128]{2,1,0:T(8,128)(2,1)} %get-tuple-element.395, s32[]{:T(128)S(6)} %copy.92, bf16[512,128]{1,0:T(8,128)(2,1)} %get-tuple-element.406, f32[1024,512]{1,0:T(8,128)S(1)} %fusion.150, bf16[128,512]{1,0:T(8,128)(2,1)S(1)} %get-tuple-element.404, f32[1024]{0:T(1024)S(1)} %add_rsqrt_fusion.4, ...), kind=kOutput, calls=%fused_computation.18.clone.1 | convolution fusion | flops 272498688 | bytes 3154944 | tf_op jit(solution)/shard_map/while/body/eval_jaxpr/dot_general | solution.py:32
  186.9 2.6 %fusion.151 = bf16[4,1024,128]{2,1,0:T(8,128)(2,1)} fusion(bf16[4,1024,128]{2,1,0:T(8,128)(2,1)} %get-tuple-element.395, s32[]{:T(128)S(6)} %copy.92, bf16[512,128]{1,0:T(8,128)(2,1)} %get-tuple-element.406, f32[1024,512]{1,0:T(8,128)S(1)} %fusion.150, bf16[128,512]{1,0:T(8,128)(2,1)S(1)} %get-tuple-element.404, f32[1024]{0:T(1024)S(1)} %add_rsqrt_fusion.4, ...), kind=kOutput, calls=%fused_computation.18.clone.1 | convolution fusion | flops 272498688 | bytes 3154944 | tf_op jit(solution)/shard_map/while/body/eval_jaxpr/dot_general | solution.py:32
  190.6 2.6 %fusion.151 = bf16[4,1024,128]{2,1,0:T(8,128)(2,1)} fusion(bf16[4,1024,128]{2,1,0:T(8,128)(2,1)} %get-tuple-element.395, s32[]{:T(128)S(6)} %copy.92, bf16[512,128]{1,0:T(8,128)(2,1)} %get-tuple-element.406, f32[1024,512]{1,0:T(8,128)S(1)} %fusion.150, bf16[128,512]{1,0:T(8,128)(2,1)S(1)} %get-tuple-element.404, f32[1024]{0:T(1024)S(1)} %add_rsqrt_fusion.4, ...), kind=kOutput, calls=%fused_computation.18.clone.1 | convolution fusion | flops 272498688 | bytes 3154944 | tf_op jit(solution)/shard_map/while/body/eval_jaxpr/dot_general | solution.py:32
  194.2 2.7 %fusion.151 = bf16[4,1024,128]{2,1,0:T(8,128)(2,1)} fusion(bf16[4,1024,128]{2,1,0:T(8,128)(2,1)} %get-tuple-element.395, s32[]{:T(128)S(6)} %copy.92, bf16[512,128]{1,0:T(8,128)(2,1)} %get-tuple-element.406, f32[1024,512]{1,0:T(8,128)S(1)} %fusion.150, bf16[128,512]{1,0:T(8,128)(2,1)S(1)} %get-tuple-element.404, f32[1024]{0:T(1024)S(1)} %add_rsqrt_fusion.4, ...), kind=kOutput, calls=%fused_computation.18.clone.1 | convolution fusion | flops 272498688 | bytes 3154944 | tf_op jit(solution)/shard_map/while/body/eval_jaxpr/dot_general | solution.py:32
  199.9 14.7 %while.32 = (s32[]{:T(128)}, bf16[4,1024,128]{2,1,0:T(8,128)(2,1)}, bf16[4,1024,128]{2,1,0:T(8,128)(2,1)S(1)}, bf16[128,512]{1,0:T(8,128)(2,1)S(1)}, bf16[128,51...) while((s32[]{:T(128)}, bf16[4,1024,128]{2,1,0:T(8,128)(2,1)}, ...), condition=%wide.region_9.10_spmd, body=%wide.region_6.9_spmd.sunk | while | flops 408028160 | bytes 6206561 | solution.py:124
  204.6 2.6 %fusion.159 = bf16[4,1024,128]{2,1,0:T(8,128)(2,1)} fusion(bf16[4,1024,128]{2,1,0:T(8,128)(2,1)} %get-tuple-element.374, s32[]{:T(128)S(6)} %copy.86, bf16[512,128]{1,0:T(8,128)(2,1)} %get-tuple-element.385, f32[1024,512]{1,0:T(8,128)S(1)} %fusion.158, bf16[128,512]{1,0:T(8,128)(2,1)S(1)} %get-tuple-element.383, f32[1024]{0:T(1024)S(1)} %add_rsqrt_fusion.5, ...), kind=kOutput, calls=%fused_computation.44.clone.1 | convolution fusion | flops 272498688 | bytes 3154944 | tf_op jit(solution)/shard_map/while/body/eval_jaxpr/dot_general | solution.py:32
  208.3 2.6 %fusion.159 = bf16[4,1024,128]{2,1,0:T(8,128)(2,1)} fusion(bf16[4,1024,128]{2,1,0:T(8,128)(2,1)} %get-tuple-element.374, s32[]{:T(128)S(6)} %copy.86, bf16[512,128]{1,0:T(8,128)(2,1)} %get-tuple-element.385, f32[1024,512]{1,0:T(8,128)S(1)} %fusion.158, bf16[128,512]{1,0:T(8,128)(2,1)S(1)} %get-tuple-element.383, f32[1024]{0:T(1024)S(1)} %add_rsqrt_fusion.5, ...), kind=kOutput, calls=%fused_computation.44.clone.1 | convolution fusion | flops 272498688 | bytes 3154944 | tf_op jit(solution)/shard_map/while/body/eval_jaxpr/dot_general | solution.py:32
  218.6 4.1 %collective-permute-start = (bf16[1,64,128]{2,1,0:T(8,128)(2,1)S(1)}, bf16[1,64,128]{2,1,0:T(8,128)(2,1)S(1)}, u32[]{:S(2)}, u32[]{:S(2)}) collective-permute-start(bf16[1,64,128]{2,1,0:T(8,128)(2,1)S(1)} %get-tuple-element.201), channel_id=1, source_target_pairs={{0,4},{4,8},{8,12},{1,5},{5,9},{9,13},{2,6},{6,10},{10,14},{3,7},{... | collective-permute-start | bytes 49160 | tf_op jit(solution)/shard_map/ppermute | solution.py:18
  223.7 4.7 %collective-permute-start.2 = (bf16[66,1,128]{2,1,0:T(2,128)(2,1)S(1)}, bf16[66,1,128]{2,1,0:T(2,128)(2,1)S(1)}, u32[]{:S(2)}, u32[]{:S(2)}) collective-permute-start(bf16[66,1,128]{2,1,0:T(2,128)(2,1)S(1)} %get-tuple-element.197), channel_id=1, source_target_pairs={{0,1},{1,2},{2,3},{4,5},{5,6},{6,7},{8,9},{9,10},{10,11},{12,13},{... | collective-permute-start | bytes 50696 | tf_op jit(solution)/shard_map/ppermute | solution.py:18
  (136 shorter events, 71.1 us)
Async XLA Ops:
  0.0 12.9 %copy-start = (bf16[32,64,64]{2,1,0:T(8,128)(2,1)S(1)}, bf16[32,64,64]{2,1,0:T(8,128)(2,1)}, u32[]{:S(2)}) copy-start(bf16[32,64,64]{2,1,0:T(8,128)(2,1)} %param.18) | copy-start | bytes 786436
  7.8 26.2 %all-to-all-start.1 = ((bf16[4,2,1024]{2,1,0:T(2,128)(2,1)}), bf16[4,2,1024]{2,1,0:T(2,128)(2,1)S(1)}, u32[]{:S(2)}, u32[]{:S(2)}) async-start(bf16[4,2,1024]{2,1,0:T(2,128)(2,1)} %reshape.147), calls=%async_computation.1 | async-start | bytes 32768 | tf_op jit(solution)/shard_map/all_to_all | solution.py:81
  31.0 7.7 %copy-start.4 = (bf16[64,32]{0,1:T(8,128)(2,1)S(1)}, bf16[64,32]{0,1:T(8,128)(2,1)}, u32[]{:S(2)}) copy-start(bf16[64,32]{0,1:T(8,128)(2,1)} %param.22) | copy-start | bytes 12292
  34.0 45.9 %all-to-all-start = ((bf16[4,2,32768]{2,1,0:T(2,128)(2,1)}), bf16[4,2,32768]{2,1,0:T(2,128)(2,1)S(1)}, u32[]{:S(2)}, u32[]{:S(2)}) async-start(bf16[4,2,32768]{2,1,0:T(2,128)(2,1)} %reshape.145), calls=%async_computation | async-start | bytes 1048576 | tf_op jit(solution)/shard_map/all_to_all | solution.py:80
  85.8 4.0 %copy-start.6 = (bf16[1024,128]{1,0:T(8,128)(2,1)S(1)}, bf16[1024,128]{1,0:T(8,128)(2,1)}, u32[]{:S(2)}) copy-start(bf16[1024,128]{1,0:T(8,128)(2,1)} %param.23) | copy-start | bytes 786436
  143.6 5.2 %copy-start.5 = (s32[256]{0:T(256)S(1)}, s32[256]{0:T(256)}, u32[]{:S(2)}) copy-start(s32[256]{0:T(256)} %param.20) | copy-start | bytes 3076
  145.3 28.7 %all-to-all-start.3 = ((bf16[16,256,128]{2,0,1:T(8,128)(2,1)}), bf16[16,256,128]{2,0,1:T(8,128)(2,1)S(1)}, u32[]{:S(2)}, u32[]{:S(2)}) async-start(bf16[16,256,128]{2,0,1:T(8,128)(2,1)} %copy.57), calls=%async_computation.3 | async-start | bytes 2097152 | tf_op jit(solution)/shard_map/all_to_all | solution.py:127
  175.2 6.9 %copy-start.2 = (bf16[128,512]{1,0:T(8,128)(2,1)S(1)}, bf16[128,512]{1,0:T(8,128)(2,1)}, u32[]{:S(2)}) copy-start(bf16[128,512]{1,0:T(8,128)(2,1)} %param.25) | copy-start | bytes 393220
  175.3 6.9 %copy-start.7 = (bf16[128,512]{1,0:T(8,128)(2,1)S(1)}, bf16[128,512]{1,0:T(8,128)(2,1)}, u32[]{:S(2)}) copy-start(bf16[128,512]{1,0:T(8,128)(2,1)} %param.24) | copy-start | bytes 393220
  175.3 21.6 %all-to-all-start.4 = ((bf16[64,64,128]{2,0,1:T(8,128)(2,1)}), bf16[64,64,128]{2,0,1:T(8,128)(2,1)}, u32[]{:S(2)}, u32[]{:S(2)}) async-start(bf16[64,64,128]{2,0,1:T(8,128)(2,1)} %bitcast.36), calls=%async_computation.4 | async-start | bytes 2097152 | tf_op jit(solution)/shard_map/all_to_all | solution.py:135
  217.3 5.4 %collective-permute-start.1 = (bf16[1,64,128]{2,1,0:T(8,128)(2,1)S(1)}, bf16[1,64,128]{2,1,0:T(8,128)(2,1)S(1)}, u32[]{:S(2)}, u32[]{:S(2)}) collective-permute-start(bf16[1,64,128]{2,1,0:T(8,128)(2,1)S(1)} %get-tuple-element.202), channel_id=1, source_target_pairs={{4,0},{8,4},{12,8},{5,1},{9,5},{13,9},{6,2},{10,6},{14,10},{7,3},{... | collective-permute-start | bytes 49160 | tf_op jit(solution)/shard_map/ppermute | solution.py:19
  218.6 12.0 %copy-start.3 = (bf16[3,3,128,128]{3,2,1,0:T(8,128)(2,1)S(1)}, bf16[3,3,128,128]{3,2,1,0:T(8,128)(2,1)}, u32[]{:S(2)}) copy-start(bf16[3,3,128,128]{3,2,1,0:T(8,128)(2,1)} %param.27) | copy-start | bytes 884740
  218.6 5.0 %collective-permute-start = (bf16[1,64,128]{2,1,0:T(8,128)(2,1)S(1)}, bf16[1,64,128]{2,1,0:T(8,128)(2,1)S(1)}, u32[]{:S(2)}, u32[]{:S(2)}) collective-permute-start(bf16[1,64,128]{2,1,0:T(8,128)(2,1)S(1)} %get-tuple-element.201), channel_id=1, source_target_pairs={{0,4},{4,8},{8,12},{1,5},{5,9},{9,13},{2,6},{6,10},{10,14},{3,7},{... | collective-permute-start | bytes 49160 | tf_op jit(solution)/shard_map/ppermute | solution.py:18
  223.7 7.4 %collective-permute-start.2 = (bf16[66,1,128]{2,1,0:T(2,128)(2,1)S(1)}, bf16[66,1,128]{2,1,0:T(2,128)(2,1)S(1)}, u32[]{:S(2)}, u32[]{:S(2)}) collective-permute-start(bf16[66,1,128]{2,1,0:T(2,128)(2,1)S(1)} %get-tuple-element.197), channel_id=1, source_target_pairs={{0,1},{1,2},{2,3},{4,5},{5,6},{6,7},{8,9},{9,10},{10,11},{12,13},{... | collective-permute-start | bytes 50696 | tf_op jit(solution)/shard_map/ppermute | solution.py:18
  228.4 5.2 %collective-permute-start.3 = (bf16[66,1,128]{2,1,0:T(2,128)(2,1)S(1)}, bf16[66,1,128]{2,1,0:T(2,128)(2,1)S(1)}, u32[]{:S(2)}, u32[]{:S(2)}) collective-permute-start(bf16[66,1,128]{2,1,0:T(2,128)(2,1)S(1)} %get-tuple-element.198), channel_id=1, source_target_pairs={{1,0},{2,1},{3,2},{5,4},{6,5},{7,6},{9,8},{10,9},{11,10},{13,12},{... | collective-permute-start | bytes 50696 | tf_op jit(solution)/shard_map/ppermute | solution.py:19
  238.6 1.4 copy-start.1
where the time goes:
time: 241 us; the launch traced here: 240 us
  blocking collectives  82.6 us (34%)
  matrix products  45.7 us (19%)
  local copies, waits for them, and re-layouts  35 us (15%)
  starting transfers between devices  31.4 us (13%)
  waiting for transfers between devices  28.1 us (12%)
  other arithmetic  8.75 us (4%)
  loops' own time  8.13 us (3%)
    all_gather x1, blocking collectives, on_device(): lax.all_gather(right_local, 'row', axis=0, tiled=True)  28.4 us
    all_to_all x1, waiting for transfers between devices, on_device(): lax.all_to_all(lax.all_to_all(pair_one, ('col', 'chan'), split_axis=0, co...  24.7 us
    all_to_all x1, blocking collectives, on_device(): lax.all_to_all(pair_one, ('col', 'chan'), split_axis=0, concat_axis=1, ti...  21.9 us
    dot_general x8, matrix products, transition(): jnp.dot(hidden, down_weight, preferred_element_type=jnp.float32)  21.2 us
    all_gather x1, blocking collectives, on_device(): lax.all_gather(left_local, ('col', 'chan'), axis=1, tiled=True)  16 us
    all_gather x1, blocking collectives, on_device(): lax.all_gather(halved_mask, 'row', axis=0, tiled=True)  10.2 us
    dot_general x4, matrix products, outer_rows(): jnp.dot(products, output_weight, preferred_element_type=jnp.float32)  9.26 us
    ppermute x2, starting transfers between devices, with_halo(): before = lax.ppermute(last, axis, up)  8.79 us
  transfers between devices with their start and end apart: 8, of which 3 were waited for; matrix products, arithmetic and copies ran while one was open for 10% of the time, Pallas kernels for 0%

commit v1 on v0

v1 whole, which is shorter than its diff:
```python
import functools
import math

import jax
import jax.numpy as jnp
from jax import lax
from jax.experimental import pallas as pl
from jax.experimental.pallas import tpu as pltpu
from jax.sharding import PartitionSpec as P

epsilon = 1e-05
lanes = 128
turns = 4
plane = ("col", "chan")
whole = ("row", "col", "chan")


def kernel_params(mib):
    return pltpu.CompilerParams(vmem_limit_bytes=mib * 1024 * 1024)


def outer_kernel(
    places, *refs, row_blocks, col_blocks, width, tokens_i, tokens_j, lane_at, row_at, mask_at, add
):
    row_refs, refs = refs[:row_blocks], refs[row_blocks:]
    col_refs, refs = refs[:col_blocks], refs[col_blocks:]
    weight, refs = refs[0], refs[1:]
    if add:
        base, refs = refs[0], refs[1:]
    out, lane_side, gathered, turned, row_side, scale, products, stacked = refs
    step = pl.program_id(0)
    strip = out.shape[0]
    groups = strip // turns
    high = width // turns
    depth = lane_side.shape[1]
    chunk = strip * width

    @pl.when(step == 0)
    def _():
        for n, block in enumerate(col_refs):
            count = block.shape[0]
            at = pl.ds(pl.multiple_of(places[row_blocks + n], 16), count)
            gathered[at, :] = block[:, row_at : row_at + tokens_j * width]
        for n in range(tokens_j * width // lanes):
            piece = gathered[:, n * lanes : (n + 1) * lanes].astype(jnp.float32)
            turned[n * lanes : (n + 1) * lanes, :] = piece.T
        for channel in range(width):
            spot = ((channel % turns) * high + channel // turns) * tokens_j
            rows = turned[pl.ds(channel, tokens_j, stride=width), :]
            row_side[spot : spot + tokens_j, :] = rows.astype(jnp.bfloat16)
        for n, block in enumerate(col_refs):
            count = block.shape[0]
            at = pl.ds(pl.multiple_of(places[row_blocks + n], 16), count)
            gathered[at, :lanes] = block[:, mask_at : mask_at + lanes]
        col_mask = gathered[:, :lanes]
        for n, block in enumerate(row_refs):
            count = block.shape[0]
            at = pl.ds(pl.multiple_of(places[n], 16), count)
            gathered[at, :lanes] = block[:, mask_at : mask_at + lanes]
        counts = lax.dot_general(
            col_mask,
            gathered[:, :lanes],
            (((0,), (0,)), ((), ())),
            preferred_element_type=jnp.float32,
        )[:tokens_j]
        inverse = 1.0 / jnp.maximum(counts, 1.0)
        for n in range(tokens_i // strip):
            scale[n, :, :strip] = inverse[:, n * strip : (n + 1) * strip]
        for n, block in enumerate(row_refs):
            count = block.shape[0]
            at = pl.ds(pl.multiple_of(places[n], 16), count)
            for g in range(tokens_i * width // lanes):
                piece = block[:, lane_at + g * lanes : lane_at + (g + 1) * lanes]
                lane_side[0, at, g * lanes : (g + 1) * lanes] = piece
                piece = piece.astype(jnp.float32)
                for turn in range(1, turns):
                    lane_side[turn, at, g * lanes : (g + 1) * lanes] = pltpu.roll(
                        piece, turn * width, 1
                    ).astype(jnp.bfloat16)

    span = high * tokens_j
    for turn in range(turns):
        products[turn] = jnp.dot(
            row_side[turn * span : (turn + 1) * span, :],
            lane_side[turn, :, pl.ds(pl.multiple_of(step * chunk, lanes), chunk)],
            preferred_element_type=jnp.float32,
        ).astype(jnp.bfloat16)
    position = lax.broadcasted_iota(jnp.int32, (tokens_j, lanes), 1) // width
    strip_scale = scale[step]
    for u in range(turns):
        for g in range(groups):
            for h in range(high):
                parts = [
                    products[
                        (t - u) % turns,
                        h * tokens_j : (h + 1) * tokens_j,
                        g * lanes : (g + 1) * lanes,
                    ]
                    for t in range(turns)
                ]
                mixed = parts[-1]
                for t in range(turns - 1):
                    mixed = jnp.where(position == t, parts[t], mixed)
                stacked[g * tokens_j : (g + 1) * tokens_j, h * lanes : (h + 1) * lanes] = mixed
        update = jnp.dot(stacked[...], weight[u], preferred_element_type=jnp.float32)
        for g in range(groups):
            i = turns * g + u
            value = update[g * tokens_j : (g + 1) * tokens_j] * strip_scale[:, i : i + 1]
            if add:
                value = value + base[i].astype(jnp.float32)
            out[i] = value.astype(out.dtype)


def outer_update(places, row_side, col_side, weight, base, sizes, swapped):
    tokens_i, tokens_j, width, channels = sizes
    strip = math.gcd(16, tokens_i)
    depth = sum(block.shape[0] for block in row_side)
    lane_at = tokens_i * width if swapped else 0
    row_at = 0 if swapped else tokens_j * width
    body = functools.partial(
        outer_kernel,
        row_blocks=len(row_side),
        col_blocks=len(col_side),
        width=width,
        tokens_i=tokens_i,
        tokens_j=tokens_j,
        lane_at=lane_at,
        row_at=row_at,
        mask_at=2 * tokens_i * width,
        add=base is not None,
    )
    if tokens_i != tokens_j:
        body = functools.partial(body, mask_at=0, lane_at=lane_at + lanes, row_at=row_at + lanes)
    whole_array = lambda a: pl.BlockSpec(a.shape, lambda n, rank=a.ndim: (0,) * rank)
    tile = pl.BlockSpec((strip, tokens_j, channels), lambda n: (n, 0, 0))
    operands = [*row_side, *col_side, weight]
    specs = [whole_array(a) for a in operands]
    if base is not None:
        operands.append(base)
        specs.append(tile)
    flops = 2 * tokens_i * tokens_j * width * width * (depth + channels)
    return pl.pallas_call(
        body,
        grid=(tokens_i // strip,),
        in_specs=[pl.BlockSpec(memory_space=pltpu.SMEM), *specs],
        out_specs=tile,
        out_shape=jax.ShapeDtypeStruct((tokens_i, tokens_j, channels), jnp.bfloat16),
        scratch_shapes=[
            pltpu.VMEM((turns, depth, tokens_i * width), jnp.bfloat16),
            pltpu.VMEM((depth, tokens_j * width), jnp.bfloat16),
            pltpu.VMEM((tokens_j * width, depth), jnp.float32),
            pltpu.VMEM((tokens_j * width, depth), jnp.bfloat16),
            pltpu.VMEM((tokens_i // strip, tokens_j, lanes), jnp.float32),
            pltpu.VMEM((turns, tokens_j * width // turns, strip * width), jnp.bfloat16),
            pltpu.VMEM((strip // turns * tokens_j, width * width), jnp.bfloat16),
        ],
        compiler_params=kernel_params(40),
        cost_estimate=pl.CostEstimate(flops=flops, bytes_accessed=4 << 20, transcendentals=0),
    )(places, *operands)


def transition_rows(values, gate_up, down):
    centre = jnp.mean(values, axis=-1, keepdims=True)
    offset = values - centre
    spread = jnp.mean(offset * offset, axis=-1, keepdims=True)
    normed = (offset * lax.rsqrt(spread + epsilon)).astype(jnp.bfloat16)
    both = jnp.dot(normed, gate_up, preferred_element_type=jnp.float32)
    hidden_width = gate_up.shape[1] // 2
    half, up = both[:, :hidden_width], both[:, hidden_width:]
    hidden = ((half + half * jnp.tanh(half)) * up).astype(jnp.bfloat16)
    return values + jnp.dot(hidden, down, preferred_element_type=jnp.float32)


def own_kernel(pair_one, gate_up, down, out):
    rows, columns, channels = out.shape
    values = pair_one[...].astype(jnp.float32).reshape(rows * columns, channels)
    result = transition_rows(values, gate_up[...], down[...])
    out[...] = result.astype(out.dtype).reshape(out.shape)


def mirror_kernel(base, update, pair_two, gate_up, down, out):
    rows, columns, channels = out.shape
    values = base[...].astype(jnp.float32) + update[...].astype(jnp.float32)
    values = values.astype(jnp.bfloat16).astype(jnp.float32).reshape(rows * columns, channels)
    result = transition_rows(values, gate_up[...], down[...]).astype(jnp.bfloat16)
    mirrored = result.astype(jnp.float32).reshape(out.shape)
    out[...] = ((pair_two[...].astype(jnp.float32) + mirrored) * 0.5).astype(out.dtype)


def run_transition(body, tiles, gate_up, down):
    rows, columns, channels = tiles[0].shape
    strip = max(1, math.gcd(rows, 512 // columns))
    tile = pl.BlockSpec((strip, columns, channels), lambda n: (n, 0, 0))
    fixed = lambda a: pl.BlockSpec(a.shape, lambda n: (0, 0))
    flops = 6 * rows * columns * channels * down.shape[0]
    return pl.pallas_call(
        body,
        grid=(rows // strip,),
        in_specs=[tile] * len(tiles) + [fixed(gate_up), fixed(down)],
        out_specs=tile,
        out_shape=jax.ShapeDtypeStruct((rows, columns, channels), jnp.bfloat16),
        compiler_params=kernel_params(40),
        cost_estimate=pl.CostEstimate(
            flops=flops, bytes_accessed=4 << 20, transcendentals=rows * columns * down.shape[0]
        ),
    )(*tiles, gate_up, down)


def conv_kernel(valid_i, symmetric, valid_j, top, bottom, left, right, weight, out, padded):
    step = pl.program_id(0)
    rows, columns, channels = symmetric.shape
    strip = out.shape[0]

    @pl.when(step == 0)
    def _():
        padded[0, 8 : 8 + columns, :] = top[...].astype(jnp.float32)
        padded[rows + 1, 8 : 8 + columns, :] = bottom[...].astype(jnp.float32)
        for i in range(rows):
            keep = valid_j[...] * valid_i[i].astype(jnp.float32)
            padded[i + 1, 8 : 8 + columns, :] = symmetric[i].astype(jnp.float32) * keep
        for i in range(rows + 2):
            padded[i, 7:8, :] = left[i : i + 1, :].astype(jnp.float32)
            padded[i, 8 + columns : 9 + columns, :] = right[i : i + 1, :].astype(jnp.float32)

    window = padded.at[pl.ds(step * strip, strip + 2)]
    shifted = [
        window[:, 7 + b : 7 + b + columns, :]
        .astype(jnp.bfloat16)
        .reshape((strip + 2) * columns, channels)
        for b in range(3)
    ]
    taps = jnp.dot(
        jnp.concatenate(shifted, axis=1), weight[...], preferred_element_type=jnp.float32
    ).reshape(strip + 2, columns, 3 * channels)
    total = symmetric[pl.ds(step * strip, strip)].astype(jnp.float32)
    for a in range(3):
        total = total + taps[a : a + strip, :, a * channels : (a + 1) * channels]
    out[...] = total.astype(out.dtype)


def convolve(symmetric, valid_i, valid_j, halos, kernel_weight):
    rows, columns, channels = symmetric.shape
    strip = math.gcd(16, rows)
    weight = kernel_weight.transpose(1, 2, 0, 3).reshape(3 * channels, 3 * channels)
    operands = [symmetric, valid_j, *halos, weight]
    fixed = lambda a: pl.BlockSpec(a.shape, lambda n, rank=a.ndim: (0,) * rank)
    return pl.pallas_call(
        conv_kernel,
        grid=(rows // strip,),
        in_specs=[pl.BlockSpec(memory_space=pltpu.SMEM)] + [fixed(a) for a in operands],
        out_specs=pl.BlockSpec((strip, columns, channels), lambda n: (n, 0, 0)),
        out_shape=jax.ShapeDtypeStruct(symmetric.shape, jnp.bfloat16),
        scratch_shapes=[pltpu.VMEM((rows + 2, columns + 16, channels), jnp.float32)],
        compiler_params=kernel_params(40),
        cost_estimate=pl.CostEstimate(
            flops=18 * rows * columns * channels * channels,
            bytes_accessed=3 << 20,
            transcendentals=0,
        ),
    )(valid_i, *operands)


def shifts(axis, size, step):
    return [(n, (n + step) % size) for n in range(size)]


def on_device(
    pair_input,
    alignment_features,
    alignment_mask,
    token_valid,
    left_weight,
    right_weight,
    output_weight,
    gate_weight,
    up_weight,
    down_weight,
    kernel_weight,
):
    rows_dev, cols_dev, channels = pair_input.shape
    local_rows, local_tokens, align_width = alignment_features.shape
    width = left_weight.shape[1]
    row_count, col_count = lax.axis_size("row"), lax.axis_size(plane)
    x_count, core_count = lax.axis_size("col"), lax.axis_size("chan")
    row_index, col_index = lax.axis_index("row"), lax.axis_index(plane)
    x_index, core_index = lax.axis_index("col"), lax.axis_index("chan")
    square = row_count == col_count
    mirror_pairs = [
        (r * col_count + c, c * col_count + r) for r in range(row_count) for c in range(col_count)
    ]

    flat = alignment_features.reshape(local_rows * local_tokens, align_width)
    mask_rows = alignment_mask.astype(jnp.float32)
    projected = []
    for weight in (left_weight, right_weight):
        value = jnp.dot(flat, weight, preferred_element_type=jnp.float32)
        value = value.reshape(local_rows, local_tokens, width) * mask_rows[:, :, None]
        projected.append(value.astype(jnp.bfloat16))
    mask_block = jnp.pad(
        alignment_mask.astype(jnp.bfloat16), ((0, 0), (0, lanes - local_tokens % lanes))
    )

    if square:
        block = jnp.concatenate(
            [p.reshape(local_rows, local_tokens * width) for p in projected] + [mask_block], axis=1
        )
        col_side, col_places = [block], [row_index]
        for step in range(1, row_count):
            col_side.append(lax.ppermute(block, "row", shifts("row", row_count, -step)))
            col_places.append((row_index + step) % row_count)
        first = lax.ppermute(block, whole, mirror_pairs)
        row_side, row_places = [first], [col_index]
        for step in range(1, x_count):
            row_side.append(lax.ppermute(first, "col", shifts("col", x_count, -step)))
            row_places.append(((x_index + step) % x_count) * core_count + core_index)
        for step in range(1, core_count):
            for n in range(x_count):
                row_side.append(
                    lax.ppermute(row_side[n], "chan", shifts("chan", core_count, -step))
                )
                row_places.append(
                    ((x_index + n) % x_count) * core_count + (core_index + step) % core_count
                )
        places = jnp.stack(row_places + col_places).astype(jnp.int32) * local_rows
        mirrored_input = lax.ppermute(jnp.swapaxes(pair_input, 0, 1), whole, mirror_pairs)
    else:
        block = jnp.stack(projected, axis=2)
        col_full = lax.all_gather(block, "row", axis=0, tiled=True)
        col_mask = lax.all_gather(mask_block, "row", axis=0, tiled=True)
        wide = lax.all_gather(block, plane, axis=1, tiled=True)
        row_full = lax.all_to_all(wide, "row", split_axis=1, concat_axis=0, tiled=True)
        wide_mask = lax.all_gather(mask_block[:, :local_tokens], plane, axis=1, tiled=True)
        row_mask = lax.all_to_all(wide_mask, "row", split_axis=1, concat_axis=0, tiled=True)
        row_mask = jnp.pad(row_mask, ((0, 0), (0, lanes - rows_dev % lanes)))
        depth = row_full.shape[0]

        def laid_out(mask, full):
            sides = [full[:, :, n].reshape(depth, full.shape[1] * width) for n in range(2)]
            return [jnp.concatenate([mask] + sides, axis=1)]

        row_side, col_side = laid_out(row_mask, row_full), laid_out(col_mask, col_full)
        places = jnp.zeros((2,), jnp.int32)
        share = rows_dev // col_count
        fold = row_count // col_count
        second = lax.all_to_all(
            lax.all_to_all(pair_input, plane, split_axis=0, concat_axis=1, tiled=True),
            "row",
            split_axis=1,
            concat_axis=0,
            tiled=True,
        )
        third = lax.all_to_all(
            jnp.swapaxes(second, 0, 1), plane, split_axis=1, concat_axis=1, tiled=True
        )
        mirrored_input = (
            third.reshape(rows_dev, col_count, fold, share, channels)
            .transpose(0, 2, 1, 3, 4)
            .reshape(rows_dev, cols_dev, channels)
        )

    def ordered(weight):
        split = weight.reshape(width // turns, turns, width, channels)
        return jnp.stack(
            [jnp.roll(split, u, axis=1).reshape(width * width, channels) for u in range(turns)]
        )

    by_pair = output_weight.reshape(width, width, channels)
    own_weight = ordered(jnp.swapaxes(by_pair, 0, 1))
    mirror_weight = ordered(by_pair)
    gate_up = jnp.concatenate([gate_weight * 0.5, up_weight], axis=1).astype(jnp.bfloat16)

    sizes = (rows_dev, cols_dev, width, channels)
    pair_one = outer_update(places, row_side, col_side, own_weight, pair_input, sizes, False)
    mirror_update = outer_update(places, row_side, col_side, mirror_weight, None, sizes, True)
    pair_two = run_transition(own_kernel, [pair_one], gate_up, down_weight)
    symmetric = run_transition(
        mirror_kernel, [mirrored_input, mirror_update, pair_two], gate_up, down_weight
    )

    valid_i = lax.dynamic_slice_in_dim(token_valid, row_index * rows_dev, rows_dev)
    valid_j = lax.dynamic_slice_in_dim(token_valid, col_index * cols_dev, cols_dev)
    keep_i = valid_i.astype(jnp.bfloat16)[:, None]
    keep_j = valid_j.astype(jnp.bfloat16)[:, None]
    edge = lambda j: symmetric[:, j] * keep_i * keep_j[j]
    ahead = lambda size: [(n, n + 1) for n in range(size - 1)]
    back = lambda size: [(n + 1, n) for n in range(size - 1)]
    left = lax.ppermute(edge(cols_dev - 1), plane, ahead(col_count))
    right = lax.ppermute(edge(0), plane, back(col_count))

    def border(i):
        line = symmetric[i] * keep_j * keep_i[i]
        return jnp.concatenate([left[i : i + 1], line, right[i : i + 1]], axis=0)

    top = lax.ppermute(border(rows_dev - 1), "row", ahead(row_count))
    bottom = lax.ppermute(border(0), "row", back(row_count))
    left = jnp.concatenate([top[:1], left, bottom[:1]], axis=0)
    right = jnp.concatenate([top[-1:], right, bottom[-1:]], axis=0)
    wide_valid = jnp.broadcast_to(valid_j.astype(jnp.float32)[:, None], (cols_dev, channels))
    return convolve(
        symmetric, valid_i, wide_valid, [top[1:-1], bottom[1:-1], left, right], kernel_weight
    )


def solution(mesh):
    placed = (
        P(("groups", "row"), plane, None),
        P("row", ("groups", "col", "chan"), None),
        P("row", ("groups", "col", "chan")),
        P("groups"),
        P(),
        P(),
        P(),
        P(),
        P(),
        P(),
        P(),
    )
    return jax.shard_map(
        on_device,
        mesh=mesh,
        in_specs=placed,
        out_specs=P(("groups", "row"), plane, None),
        check_vma=False,
    )
```

time: 241 us -> 128 us (0.53)
  blocking collectives: 82.6 us -> 0 us
  matrix products: 45.7 us -> 1.16 us
  Pallas kernels: 0 us -> 42.3 us
  local copies, waits for them, and re-layouts: 35 us -> 11.3 us
  loops' own time: 8.13 us -> 0 us
  waiting for transfers between devices: 28.1 us -> 31.2 us
    all_gather x4 -> x0, blocking collectives: 60.7 us -> none  [the longest x1 28.4 us: on_device(): lax.all_gather(right_local, 'row', axis=0, tiled=True)]
    dot_general x36 -> x2, matrix products: 45.7 us -> 1.16 us  [on_device(): value = jnp.dot(flat, weight, preferred_element_type=jnp.float32)]
    pallas_call x0 -> x5, Pallas kernels: none -> 42.3 us  [the longest x2 22.8 us: outer_update(): pl.pallas_call(body, grid=(tokens_i // strip,), in_specs=[pl.BlockSpec(me...]
    ppermute x4 -> x12, waiting for transfers between devices: 3.36 us -> 31.2 us  [the longest x3 29.1 us: on_device(): col_side.append(lax.ppermute(block, 'row', shifts('row', row_count, -step)))]
    all_to_all x4 -> x0, waiting for transfers between devices: 24.8 us -> none  [the longest x1 24.7 us: on_device(): lax.all_to_all(lax.all_to_all(pair_one, ('col', 'chan'), split_axis=0, co...]
    all_to_all x1 -> x0, blocking collectives: 21.9 us -> none  [on_device(): lax.all_to_all(pair_one, ('col', 'chan'), split_axis=0, concat_axis=1, ti...]
    ppermute x4 -> x12, starting transfers between devices: 12.2 us -> 33.5 us  [the longest x2 9.33 us: on_device(): lax.ppermute(row_side[n], 'chan', shifts('chan', core_count, -step))]
    all_to_all x4 -> x0, starting transfers between devices: 19.2 us -> none  [the longest x1 5.79 us: on_device(): lax.all_to_all(flipped, ('col', 'chan'), split_axis=1, concat_axis=1, til...]
  transfers between devices with their start and end apart: 8 -> 12, of which waited for: 3 -> 3; matrix products, arithmetic and copies ran while one was open for 10% -> 8% of each run, Pallas kernels for 0% -> 23%
where the time goes in v1:
time: 128 us; the launch traced here: 127 us
  Pallas kernels  42.3 us (33%)
  starting transfers between devices  33.5 us (26%)
  waiting for transfers between devices  31.2 us (24%)
  local copies, waits for them, and re-layouts  11.3 us (9%)
  other arithmetic  7.28 us (6%)
    ppermute x3, waiting for transfers between devices, on_device(): col_side.append(lax.ppermute(block, 'row', shifts('row', row_count, -step)))  29.1 us
    pallas_call x2, Pallas kernels, outer_update(): pl.pallas_call(body, grid=(tokens_i // strip,), in_specs=[pl.BlockSpec(me...  22.8 us
    pallas_call x2, Pallas kernels, run_transition(): pl.pallas_call(body, grid=(rows // strip,), in_specs=[tile] * len(tiles)...  15.1 us
    ppermute x2, starting transfers between devices, on_device(): lax.ppermute(row_side[n], 'chan', shifts('chan', core_count, -step))  9.33 us
    unnamed x44, local copies, waits for them, and re-layouts  6.07 us
    ppermute x1, starting transfers between devices, on_device(): first = lax.ppermute(block, whole, mirror_pairs)  4.73 us
    ppermute x1, starting transfers between devices, on_device(): lax.ppermute(jnp.swapaxes(pair_input, 0, 1), whole, mirror_pairs)  4.6 us
    pallas_call x1, Pallas kernels, convolve(): pl.pallas_call(conv_kernel, grid=(rows // strip,), in_specs=[pl.BlockSpec...  4.35 us
  transfers between devices with their start and end apart: 12, of which 3 were waited for; matrix products, arithmetic and copies ran while one was open for 8% of the time, Pallas kernels for 23%

profile of v1, /device:TPU:1, one launch (start us, length us, event | category | flops | bytes accessed | tf_op | source)
XLA Modules:
  0.0 127.2 jit_solution(17391110041336929948)
XLA Ops:
  4.1 4.7 %collective-permute-start.1 = (bf16[32,4224]{1,0:T(8,128)(2,1)S(1)}, bf16[32,4224]{1,0:T(8,128)(2,1)}, u32[]{:S(2)}, u32[]{:S(2)}) collective-permute-start(bf16[32,4224]{1,0:T(8,128)(2,1)S(1)} %fusion.3.refs_4_), channel_id=1, source_target_pairs={{0,0},{1,4},{2,8},{3,12},{4,1},{5,5},{6,9},{7,13},{8,2},{9,6},{10,... | collective-permute-start | bytes 811016 | tf_op jit(solution)/shard_map/ppermute | solution.py:311
  8.9 2.5 %collective-permute-start.5 = (bf16[32,4224]{1,0:T(8,128)(2,1)S(1)}, bf16[32,4224]{1,0:T(8,128)(2,1)S(1)}, u32[]{:S(2)}, u32[]{:S(2)}) collective-permute-start(bf16[32,4224]{1,0:T(8,128)(2,1)S(1)} %fusion.3.refs_4_), channel_id=1, source_target_pairs={{0,12},{4,0},{8,4},{12,8},{1,13},{5,1},{9,5},{13,9},{2,14},{6,2},{... | collective-permute-start | bytes 811016 | tf_op jit(solution)/shard_map/ppermute | solution.py:309
  11.4 1.1 collective-permute-start.7
  12.5 1.6 %copy.41 = bf16[64,64,128]{2,0,1:T(8,128)(2,1)} copy(bf16[64,64,128]{2,1,0:T(8,128)(2,1)S(1)} %copy-done.1) | data formatting | bytes 2097152 | tf_op args[0]
  14.2 4.6 %collective-permute-start = (bf16[64,64,128]{2,1,0:T(8,128)(2,1)}, bf16[64,64,128]{2,1,0:T(8,128)(2,1)}, u32[]{:S(2)}, u32[]{:S(2)}) collective-permute-start(bf16[64,64,128]{2,1,0:T(8,128)(2,1)} %bitcast.65), channel_id=1, source_target_pairs={{0,0},{1,4},{2,8},{3,12},{4,1},{5,5},{6,9},{7,13},{8,2},{9,6},{10,... | collective-permute-start | bytes 3145736 | tf_op jit(solution)/shard_map/ppermute | solution.py:325
  25.2 1.6 %collective-permute-start.2 = (bf16[32,4224]{1,0:T(8,128)(2,1)}, bf16[32,4224]{1,0:T(8,128)(2,1)}, u32[]{:S(2)}, u32[]{:S(2)}) collective-permute-start(bf16[32,4224]{1,0:T(8,128)(2,1)} %collective-permute-done.1.refs_0_), channel_id=1, source_target_pairs={{0,2},{2,0},{1,3},{3,1},{4,6},{6,4},{5,7},{7,5},{8,10},{10,8},{9,1... | collective-permute-start | bytes 811016 | tf_op jit(solution)/shard_map/ppermute | solution.py:314
  27.6 1.1 pad_maximum_fusion.refs_8_
  28.7 4.9 %collective-permute-start.3 = (bf16[32,4224]{1,0:T(8,128)(2,1)}, bf16[32,4224]{1,0:T(8,128)(2,1)}, u32[]{:S(2)}, u32[]{:S(2)}) collective-permute-start(bf16[32,4224]{1,0:T(8,128)(2,1)} %collective-permute-done.1.refs_0_), channel_id=1, source_target_pairs={{0,1},{1,0},{2,3},{3,2},{4,5},{5,4},{6,7},{7,6},{8,9},{9,8},{10,11... | collective-permute-start | bytes 811016 | tf_op jit(solution)/shard_map/ppermute | solution.py:319
  33.6 4.5 %collective-permute-start.4 = (bf16[32,4224]{1,0:T(8,128)(2,1)}, bf16[32,4224]{1,0:T(8,128)(2,1)}, u32[]{:S(2)}, u32[]{:S(2)}) collective-permute-start(bf16[32,4224]{1,0:T(8,128)(2,1)} %collective-permute-done.2.refs_1_), channel_id=1, source_target_pairs={{0,1},{1,0},{2,3},{3,2},{4,5},{5,4},{6,7},{7,6},{8,9},{9,8},{10,11... | collective-permute-start | bytes 811016 | tf_op jit(solution)/shard_map/ppermute | solution.py:319
  38.6 1.2 copy.25
  40.0 29.1 %collective-permute-done.6.refs_6_ = bf16[32,4224]{1,0:T(8,128)(2,1)} collective-permute-done((bf16[32,4224]{1,0:T(8,128)(2,1)S(1)}, bf16[32,4224]{1,0:T(8,128)(2,1)}, u32[]{:S(2)}, u32[]{:S(2)}) %collective-permute-start.6) | collective-permute-done | bytes 270368 | tf_op jit(solution)/shard_map/ppermute | solution.py:309
  69.2 0.9 copy-done.4
  70.1 11.4 %shard_map.110.pair_one = bf16[64,64,128]{2,1,0:T(8,128)(2,1)S(1)} custom-call(s32[8]{0:T(128)S(1)} %broadcast_multiply_fusion.1.places, bf16[32,4224]{1,0:T(8,128)(2,1)} %collective-permute-done.1.refs_0_, bf16[32,4224]{1,0:T(8,128)(2,1)} %collective-permute-done.2.refs_1_, bf16[32,4224]{1,0:T(8,128)(2,1)} %collective-permute-done.3.refs_2_, ...), custom_call_target="tpu_custom_call" | custom-call | flops 2147483648 | bytes 4194304 | tf_op jit(solution)/shard_map/pallas_call | solution.py:142
  81.5 7.0 %shard_map.111.pair_two = bf16[64,64,128]{2,1,0:T(8,128)(2,1)S(1)} custom-call(bf16[64,64,128]{2,1,0:T(8,128)(2,1)S(1)} %shard_map.110.pair_one, bf16[128,1024]{1,0:T(8,128)(2,1)S(1)} %pad_maximum_fusion.8.gate_up, bf16[512,128]{1,0:T(8,128)(2,1)S(1)} %copy-done.6), custom_call_target="tpu_custom_call" | custom-call | flops 1610612736 | bytes 4194304 | tf_op jit(solution)/shard_map/pallas_call | solution.py:196
  88.6 11.4 %shard_map.109.update = bf16[64,64,128]{2,1,0:T(8,128)(2,1)S(1)} custom-call(s32[8]{0:T(128)S(1)} %broadcast_multiply_fusion.1.places, bf16[32,4224]{1,0:T(8,128)(2,1)} %collective-permute-done.1.refs_0_, bf16[32,4224]{1,0:T(8,128)(2,1)} %collective-permute-done.2.refs_1_, bf16[32,4224]{1,0:T(8,128)(2,1)} %collective-permute-done.3.refs_2_, ...), custom_call_target="tpu_custom_call" | custom-call | flops 2147483648 | bytes 4194304 | tf_op jit(solution)/shard_map/pallas_call | solution.py:142
  100.1 8.1 %shard_map.112.symmetric = bf16[64,64,128]{2,1,0:T(8,128)(2,1)S(1)} custom-call(bf16[64,64,128]{2,1,0:T(8,128)(2,1)} %collective-permute-done.base, bf16[64,64,128]{2,1,0:T(8,128)(2,1)S(1)} %shard_map.109.update, bf16[64,64,128]{2,1,0:T(8,128)(2,1)S(1)} %shard_map.111.pair_two, bf16[128,1024]{1,0:T(8,128)(2,1)S(1)} %pad_maximum_fusion.8.gate_up, ...), custom_call_target="tpu_custom_call" | custom-call | flops 1610612736 | bytes 4194304 | tf_op jit(solution)/shard_map/pallas_call | solution.py:196
  108.2 1.3 %fusion.11 = (bf16[64,128]{1,0:T(8,128)(2,1)S(1)}, bf16[64,128]{1,0:T(8,128)(2,1)S(1)}) fusion(bf16[64,1,128]{2,1,0:T(2,128)(2,1)S(1)} %get-tuple-element.9, bf16[]{:T(256)} %bitcast.25, bf16[64]{0:T(256)(128)(2,1)S(1)} %get-tuple-element.35, bf16[]{:T(256)} %bitcast.29, bf16[64,1,128]{2,1,0:T(2,128)(2,1)S(1)} %get-tuple-element.10), kind=kLoop, calls=%fused_computation.34 | loop fusion | flops 32768 | bytes 65668 | tf_op jit(solution)/shard_map/mul | solution.py:384
  109.5 1.9 %collective-permute-start.8 = (bf16[64,128]{1,0:T(8,128)(2,1)S(1)}, bf16[64,128]{1,0:T(8,128)(2,1)S(1)}, u32[]{:S(2)}, u32[]{:S(2)}) collective-permute-start(bf16[64,128]{1,0:T(8,128)(2,1)S(1)} %get-tuple-element.39), channel_id=1, source_target_pairs={{0,1},{1,2},{2,3},{4,5},{5,6},{6,7},{8,9},{9,10},{10,11},{12,13},{... | collective-permute-start | bytes 49160 | tf_op jit(solution)/shard_map/ppermute | solution.py:387
  111.4 2.4 %collective-permute-start.9 = (bf16[64,128]{1,0:T(8,128)(2,1)S(1)}, bf16[64,128]{1,0:T(8,128)(2,1)S(1)}, u32[]{:S(2)}, u32[]{:S(2)}) collective-permute-start(bf16[64,128]{1,0:T(8,128)(2,1)S(1)} %get-tuple-element.40), channel_id=1, source_target_pairs={{1,0},{2,1},{3,2},{5,4},{6,5},{7,6},{9,8},{10,9},{11,10},{13,12},{... | collective-permute-start | bytes 49160 | tf_op jit(solution)/shard_map/ppermute | solution.py:388
  113.8 1.4 %fusion.5 = (bf16[64,128]{1,0:T(8,128)(2,1)S(1)}, bf16[64,128]{1,0:T(8,128)(2,1)S(1)}) fusion(bf16[64,64,128]{2,1,0:T(8,128)(2,1)S(1)} %shard_map.112.symmetric, bf16[]{:T(256)} %bitcast.31, bf16[64]{0:T(256)(128)(2,1)S(1)} %get-tuple-element.33, bf16[]{:T(256)} %bitcast.27), kind=kLoop, calls=%fused_computation.25 | loop fusion | flops 32768 | bytes 65668 | tf_op jit(solution)/shard_map/mul | solution.py:391
  115.3 1.2 collective-permute-done.9
  116.5 1.3 %collective-permute-start.11 = (bf16[66,128]{1,0:T(8,128)(2,1)S(1)}, bf16[66,128]{1,0:T(8,128)(2,1)S(1)}, u32[]{:S(2)}, u32[]{:S(2)}) collective-permute-start(bf16[66,128]{1,0:T(8,128)(2,1)S(1)} %pad_maximum_fusion.10), channel_id=1, source_target_pairs={{4,0},{8,4},{12,8},{5,1},{9,5},{13,9},{6,2},{10,6},{14,10},{7,3},{... | collective-permute-start | bytes 50696 | tf_op jit(solution)/shard_map/ppermute | solution.py:395
  117.8 4.0 %collective-permute-start.10 = (bf16[66,128]{1,0:T(8,128)(2,1)S(1)}, bf16[66,128]{1,0:T(8,128)(2,1)S(1)}, u32[]{:S(2)}, u32[]{:S(2)}) collective-permute-start(bf16[66,128]{1,0:T(8,128)(2,1)S(1)} %pad_maximum_fusion.9), channel_id=1, source_target_pairs={{0,4},{4,8},{8,12},{1,5},{5,9},{9,13},{2,6},{6,10},{10,14},{3,7},{... | collective-permute-start | bytes 50696 | tf_op jit(solution)/shard_map/ppermute | solution.py:394
  122.8 4.4 %shard_map.113 = bf16[64,64,128]{2,1,0:T(8,128)(2,1)} custom-call(s32[64]{0:T(128)S(1)} %get-tuple-element.36.valid_i, bf16[64,64,128]{2,1,0:T(8,128)(2,1)S(1)} %shard_map.112.symmetric, f32[64,128]{1,0:T(8,128)S(1)} %broadcast_in_dim.2.valid_j, bf16[64,128]{1,0:T(8,128)(2,1)S(1)} %slice.147.top, bf16[64,128]{1,0:T(8,128)(2,1)S(1)} %slice.151.bottom, ...), custom_call_target="tpu_custom_call" | custom-call | flops 1207959552 | bytes 3145728 | tf_op jit(solution)/shard_map/pallas_call | solution.py:247
  (92 shorter events, 13.0 us)
Async XLA Ops:
  0.0 1.1 copy-start
  3.2 9.3 %copy-start.1 = (bf16[64,64,128]{2,1,0:T(8,128)(2,1)S(1)}, bf16[64,64,128]{2,1,0:T(8,128)(2,1)}, u32[]{:S(2)}) copy-start(bf16[64,64,128]{2,1,0:T(8,128)(2,1)} %refs_9_.1) | copy-start | bytes 3145732
  4.1 14.6 %copy-start.7 = (bf16[1024,128]{1,0:T(8,128)(2,1)S(1)}, bf16[1024,128]{1,0:T(8,128)(2,1)}, u32[]{:S(2)}) copy-start(bf16[1024,128]{1,0:T(8,128)(2,1)} %param.17) | copy-start | bytes 786436
  4.1 21.1 %collective-permute-start.1 = (bf16[32,4224]{1,0:T(8,128)(2,1)S(1)}, bf16[32,4224]{1,0:T(8,128)(2,1)}, u32[]{:S(2)}, u32[]{:S(2)}) collective-permute-start(bf16[32,4224]{1,0:T(8,128)(2,1)S(1)} %fusion.3.refs_4_), channel_id=1, source_target_pairs={{0,0},{1,4},{2,8},{3,12},{4,1},{5,5},{6,9},{7,13},{8,2},{9,6},{10,... | collective-permute-start | bytes 811016 | tf_op jit(solution)/shard_map/ppermute | solution.py:311
  8.9 19.8 %collective-permute-start.5 = (bf16[32,4224]{1,0:T(8,128)(2,1)S(1)}, bf16[32,4224]{1,0:T(8,128)(2,1)S(1)}, u32[]{:S(2)}, u32[]{:S(2)}) collective-permute-start(bf16[32,4224]{1,0:T(8,128)(2,1)S(1)} %fusion.3.refs_4_), channel_id=1, source_target_pairs={{0,12},{4,0},{8,4},{12,8},{1,13},{5,1},{9,5},{13,9},{2,14},{6,2},{... | collective-permute-start | bytes 811016 | tf_op jit(solution)/shard_map/ppermute | solution.py:309
  11.4 57.8 %collective-permute-start.6 = (bf16[32,4224]{1,0:T(8,128)(2,1)S(1)}, bf16[32,4224]{1,0:T(8,128)(2,1)}, u32[]{:S(2)}, u32[]{:S(2)}) collective-permute-start(bf16[32,4224]{1,0:T(8,128)(2,1)S(1)} %fusion.3.refs_4_), channel_id=1, source_target_pairs={{0,8},{4,12},{8,0},{12,4},{1,9},{5,13},{9,1},{13,5},{2,10},{6,14},... | collective-permute-start | bytes 811016 | tf_op jit(solution)/shard_map/ppermute | solution.py:309
  11.4 57.8 %collective-permute-start.7 = (bf16[32,4224]{1,0:T(8,128)(2,1)S(1)}, bf16[32,4224]{1,0:T(8,128)(2,1)}, u32[]{:S(2)}, u32[]{:S(2)}) collective-permute-start(bf16[32,4224]{1,0:T(8,128)(2,1)S(1)} %fusion.3.refs_4_), channel_id=1, source_target_pairs={{0,4},{4,8},{8,12},{12,0},{1,5},{5,9},{9,13},{13,1},{2,6},{6,10},{... | collective-permute-start | bytes 811016 | tf_op jit(solution)/shard_map/ppermute | solution.py:309
  14.2 85.9 %collective-permute-start = (bf16[64,64,128]{2,1,0:T(8,128)(2,1)}, bf16[64,64,128]{2,1,0:T(8,128)(2,1)}, u32[]{:S(2)}, u32[]{:S(2)}) collective-permute-start(bf16[64,64,128]{2,1,0:T(8,128)(2,1)} %bitcast.65), channel_id=1, source_target_pairs={{0,0},{1,4},{2,8},{3,12},{4,1},{5,5},{6,9},{7,13},{8,2},{9,6},{10,... | collective-permute-start | bytes 3145736 | tf_op jit(solution)/shard_map/ppermute | solution.py:325
  23.9 1.1 copy-start.13
  23.9 1.2 copy-start.14
  25.1 1.7 %copy-start.20 = (s32[256]{0:T(256)S(1)}, s32[256]{0:T(256)}, u32[]{:S(2)}) copy-start(s32[256]{0:T(256)} %param.14) | copy-start | bytes 3076
  25.1 2.5 %copy-start.8 = (bf16[1024,128]{1,0:T(8,128)(2,1)S(1)}, bf16[1024,128]{1,0:T(8,128)(2,1)}, u32[]{:S(2)}) copy-start(bf16[1024,128]{1,0:T(8,128)(2,1)} %param.17) | copy-start | bytes 786436
  25.1 2.5 %copy-start.11 = (bf16[8,4,32,128]{3,2,1,0:T(8,128)(2,1)S(1)}, bf16[8,4,32,128]{3,2,1,0:T(8,128)(2,1)}, u32[]{:S(2)}) copy-start(bf16[8,4,32,128]{3,2,1,0:T(8,128)(2,1)} %pad_maximum_fusion.3) | copy-start | bytes 786436
  25.2 8.3 %collective-permute-start.2 = (bf16[32,4224]{1,0:T(8,128)(2,1)}, bf16[32,4224]{1,0:T(8,128)(2,1)}, u32[]{:S(2)}, u32[]{:S(2)}) collective-permute-start(bf16[32,4224]{1,0:T(8,128)(2,1)} %collective-permute-done.1.refs_0_), channel_id=1, source_target_pairs={{0,2},{2,0},{1,3},{3,1},{4,6},{6,4},{5,7},{7,5},{8,10},{10,8},{9,1... | collective-permute-start | bytes 811016 | tf_op jit(solution)/shard_map/ppermute | solution.py:314
  28.7 11.2 %copy-start.3 = (bf16[32,4224]{1,0:T(8,128)(2,1)}, bf16[32,4224]{1,0:T(8,128)(2,1)S(1)}, u32[]{:S(2)}) copy-start(bf16[32,4224]{1,0:T(8,128)(2,1)S(1)} %collective-permute-done.5.refs_5_) | copy-start | bytes 811012
  28.7 40.5 %collective-permute-start.3 = (bf16[32,4224]{1,0:T(8,128)(2,1)}, bf16[32,4224]{1,0:T(8,128)(2,1)}, u32[]{:S(2)}, u32[]{:S(2)}) collective-permute-start(bf16[32,4224]{1,0:T(8,128)(2,1)} %collective-permute-done.1.refs_0_), channel_id=1, source_target_pairs={{0,1},{1,0},{2,3},{3,2},{4,5},{5,4},{6,7},{7,6},{8,9},{9,8},{10,11... | collective-permute-start | bytes 811016 | tf_op jit(solution)/shard_map/ppermute | solution.py:319
  33.6 35.6 %collective-permute-start.4 = (bf16[32,4224]{1,0:T(8,128)(2,1)}, bf16[32,4224]{1,0:T(8,128)(2,1)}, u32[]{:S(2)}, u32[]{:S(2)}) collective-permute-start(bf16[32,4224]{1,0:T(8,128)(2,1)} %collective-permute-done.2.refs_1_), channel_id=1, source_target_pairs={{0,1},{1,0},{2,3},{3,2},{4,5},{5,4},{6,7},{7,6},{8,9},{9,8},{10,11... | collective-permute-start | bytes 811016 | tf_op jit(solution)/shard_map/ppermute | solution.py:319
  70.1 11.4 %copy-start.6 = (bf16[512,128]{1,0:T(8,128)(2,1)S(1)}, bf16[512,128]{1,0:T(8,128)(2,1)}, u32[]{:S(2)}) copy-start(bf16[512,128]{1,0:T(8,128)(2,1)} %down.3) | copy-start | bytes 393220
  81.5 7.1 %copy-start.2 = (bf16[4,1024,128]{2,1,0:T(8,128)(2,1)S(1)}, bf16[4,1024,128]{2,1,0:T(8,128)(2,1)}, u32[]{:S(2)}) copy-start(bf16[4,1024,128]{2,1,0:T(8,128)(2,1)} %pad_maximum_fusion.refs_8_) | copy-start | bytes 3145732
  81.5 7.1 %copy-start.5 = (bf16[32,4224]{1,0:T(8,128)(2,1)S(1)}, bf16[32,4224]{1,0:T(8,128)(2,1)}, u32[]{:S(2)}) copy-start(bf16[32,4224]{1,0:T(8,128)(2,1)} %copy-done.3) | copy-start | bytes 811012
  109.5 5.7 %collective-permute-start.8 = (bf16[64,128]{1,0:T(8,128)(2,1)S(1)}, bf16[64,128]{1,0:T(8,128)(2,1)S(1)}, u32[]{:S(2)}, u32[]{:S(2)}) collective-permute-start(bf16[64,128]{1,0:T(8,128)(2,1)S(1)} %get-tuple-element.39), channel_id=1, source_target_pairs={{0,1},{1,2},{2,3},{4,5},{5,6},{6,7},{8,9},{9,10},{10,11},{12,13},{... | collective-permute-start | bytes 49160 | tf_op jit(solution)/shard_map/ppermute | solution.py:387
  111.4 5.1 %collective-permute-start.9 = (bf16[64,128]{1,0:T(8,128)(2,1)S(1)}, bf16[64,128]{1,0:T(8,128)(2,1)S(1)}, u32[]{:S(2)}, u32[]{:S(2)}) collective-permute-start(bf16[64,128]{1,0:T(8,128)(2,1)S(1)} %get-tuple-element.40), channel_id=1, source_target_pairs={{1,0},{2,1},{3,2},{5,4},{6,5},{7,6},{9,8},{10,9},{11,10},{13,12},{... | collective-permute-start | bytes 49160 | tf_op jit(solution)/shard_map/ppermute | solution.py:388
  116.5 5.3 %collective-permute-start.11 = (bf16[66,128]{1,0:T(8,128)(2,1)S(1)}, bf16[66,128]{1,0:T(8,128)(2,1)S(1)}, u32[]{:S(2)}, u32[]{:S(2)}) collective-permute-start(bf16[66,128]{1,0:T(8,128)(2,1)S(1)} %pad_maximum_fusion.10), channel_id=1, source_target_pairs={{4,0},{8,4},{12,8},{5,1},{9,5},{13,9},{6,2},{10,6},{14,10},{7,3},{... | collective-permute-start | bytes 50696 | tf_op jit(solution)/shard_map/ppermute | solution.py:395
  117.8 4.9 %collective-permute-start.10 = (bf16[66,128]{1,0:T(8,128)(2,1)S(1)}, bf16[66,128]{1,0:T(8,128)(2,1)S(1)}, u32[]{:S(2)}, u32[]{:S(2)}) collective-permute-start(bf16[66,128]{1,0:T(8,128)(2,1)S(1)} %pad_maximum_fusion.9), channel_id=1, source_target_pairs={{0,4},{4,8},{8,12},{1,5},{5,9},{9,13},{2,6},{6,10},{10,14},{3,7},{... | collective-permute-start | bytes 50696 | tf_op jit(solution)/shard_map/ppermute | solution.py:394
  (9 other events, 8.1 us)

commit v2 on v1

v2 whole, which is shorter than its diff:
```python
import functools
import math

import jax
import jax.numpy as jnp
from jax import lax
from jax.experimental import pallas as pl
from jax.experimental.pallas import tpu as pltpu
from jax.sharding import PartitionSpec as P

epsilon = 1e-05
lanes = 128
turns = 4
plane = ("col", "chan")
whole = ("row", "col", "chan")
unit = 16


def kernel_params(mib):
    return pltpu.CompilerParams(vmem_limit_bytes=mib * 1024 * 1024)


def arrange_kernel(
    places, *refs, row_blocks, col_blocks, width, tokens_row, tokens_col
):
    row_refs, refs = refs[:row_blocks], refs[row_blocks:]
    col_refs, refs = refs[:col_blocks], refs[col_blocks:]
    row_side, lane_side, scale, gathered, turned, row_mask, col_mask = refs
    high = width // turns
    row_span, col_span = tokens_row * width, tokens_col * width
    for n, block in enumerate(row_refs):
        at = pl.ds(pl.multiple_of(places[n], 16), block.shape[0])
        gathered[at, :] = block[:, :row_span]
        row_mask[at, :] = block[:, row_span:]
    for n, block in enumerate(col_refs):
        at = pl.ds(pl.multiple_of(places[row_blocks + n], 16), block.shape[0])
        col_mask[at, :] = block[:, col_span:]
        for g in range(col_span // lanes):
            spot = slice(g * lanes, (g + 1) * lanes)
            piece = block[:, spot]
            lane_side[0, at, spot] = piece
            piece = piece.astype(jnp.float32)
            for turn in range(1, turns):
                lane_side[turn, at, spot] = pltpu.roll(piece, turn * width, 1).astype(jnp.bfloat16)
    for n in range(row_span // lanes):
        spot = slice(n * lanes, (n + 1) * lanes)
        turned[spot, :] = gathered[:, spot].astype(jnp.float32).T
    for channel in range(width):
        spot = ((channel % turns) * high + channel // turns) * tokens_row
        rows = turned[pl.ds(channel, tokens_row, stride=width), :]
        row_side[spot : spot + tokens_row, :] = rows.astype(jnp.bfloat16)
    counts = lax.dot_general(
        row_mask[...],
        col_mask[...],
        (((0,), (0,)), ((), ())),
        preferred_element_type=jnp.float32,
    )[:tokens_row]
    inverse = 1.0 / jnp.maximum(counts, 1.0)
    strip = scale.shape[0]
    for n in range(strip):
        count = tokens_col // strip
        scale[n, :, :count] = inverse[:, n * count : (n + 1) * count]


def arrange(places, row_side, col_side, width, tokens_row, tokens_col):
    depth = sum(block.shape[0] for block in row_side)
    body = functools.partial(
        arrange_kernel,
        row_blocks=len(row_side),
        col_blocks=len(col_side),
        width=width,
        tokens_row=tokens_row,
        tokens_col=tokens_col,
    )
    in_vmem = pl.BlockSpec(memory_space=pltpu.VMEM)
    return pl.pallas_call(
        body,
        in_specs=[pl.BlockSpec(memory_space=pltpu.SMEM)]
        + [in_vmem] * (len(row_side) + len(col_side)),
        out_specs=[in_vmem] * 3,
        out_shape=[
            jax.ShapeDtypeStruct((tokens_row * width, depth), jnp.bfloat16),
            jax.ShapeDtypeStruct((turns, depth, tokens_col * width), jnp.bfloat16),
            jax.ShapeDtypeStruct((tokens_col // unit, tokens_row, lanes), jnp.float32),
        ],
        scratch_shapes=[
            pltpu.VMEM((depth, tokens_row * width), jnp.bfloat16),
            pltpu.VMEM((tokens_row * width, depth), jnp.float32),
            pltpu.VMEM((depth, lanes), jnp.bfloat16),
            pltpu.VMEM((depth, lanes), jnp.bfloat16),
        ],
        compiler_params=kernel_params(12),
        cost_estimate=pl.CostEstimate(flops=1 << 24, bytes_accessed=4 << 20, transcendentals=0),
    )(places, *row_side, *col_side)


def transition_rows(values, gate_up, down):
    channels = values.shape[1]
    mean_of = jnp.full((channels, channels), 1.0 / channels, jnp.bfloat16)
    centre = jnp.dot(values.astype(jnp.bfloat16), mean_of, preferred_element_type=jnp.float32)
    offset = values - centre
    squares = (offset * offset).astype(jnp.bfloat16)
    spread = jnp.dot(squares, mean_of, preferred_element_type=jnp.float32)
    normed = (offset * lax.rsqrt(spread + epsilon)).astype(jnp.bfloat16)
    both = jnp.dot(normed, gate_up, preferred_element_type=jnp.float32)
    hidden_width = gate_up.shape[1] // 2
    half, up = both[:, :hidden_width], both[:, hidden_width:]
    hidden = ((half + half * jnp.tanh(half)) * up).astype(jnp.bfloat16)
    return values + jnp.dot(hidden, down, preferred_element_type=jnp.float32)


def tile_kernel(
    row_side, lane_side, scale, base, weight, gate_up, down, out, products, stacked, held
):
    strip, tokens_row, channels = out.shape
    width = lane_side.shape[2] // strip
    high = width // turns
    groups = strip // turns
    span = high * tokens_row
    for turn in range(turns):
        products[turn] = jnp.dot(
            row_side[turn * span : (turn + 1) * span, :],
            lane_side[turn],
            preferred_element_type=jnp.float32,
        ).astype(jnp.bfloat16)
    position = lax.broadcasted_iota(jnp.int32, (tokens_row, lanes), 1) // width
    for g in range(groups):
        for h in range(high):
            parts = [
                products[t, h * tokens_row : (h + 1) * tokens_row, g * lanes : (g + 1) * lanes]
                for t in range(turns)
            ]
            for u in range(turns):
                mixed = parts[(turns - 1 - u) % turns]
                for t in range(turns - 1):
                    mixed = jnp.where(position == t, parts[(t - u) % turns], mixed)
                stacked[
                    u, g * tokens_row : (g + 1) * tokens_row, h * lanes : (h + 1) * lanes
                ] = mixed
    for u in range(turns):
        update = jnp.dot(stacked[u], weight[u], preferred_element_type=jnp.float32)
        for g in range(groups):
            n = turns * g + u
            factor = scale[n // unit][:, n % unit : n % unit + 1]
            value = update[g * tokens_row : (g + 1) * tokens_row] * factor
            value = base[n].astype(jnp.float32) + value
            held[n * tokens_row : (n + 1) * tokens_row, :] = value.astype(jnp.bfloat16)
    piece = min(16, strip)
    for first in range(0, strip, piece):
        at = slice(first * tokens_row, (first + piece) * tokens_row)
        result = transition_rows(held[at, :].astype(jnp.float32), gate_up[...], down[...])
        out[first : first + piece] = result.astype(out.dtype).reshape(piece, tokens_row, channels)


def tile_strips(first, count, strip, row_side, lane_side, scale, base, weight, gate_up, down):
    tokens_row, channels = base.shape[1:]
    turn_count, depth, span = lane_side.shape
    width = span // base.shape[0]
    start = first // strip
    fixed = lambda a: pl.BlockSpec(a.shape, lambda n, rank=a.ndim: (0,) * rank)
    flops = 2 * count * tokens_row * (width * width * (depth + channels) + 3 * channels * 512)
    return pl.pallas_call(
        tile_kernel,
        grid=(count // strip,),
        in_specs=[
            fixed(row_side),
            pl.BlockSpec((turn_count, depth, strip * width), lambda n: (0, 0, n + start)),
            pl.BlockSpec((strip // unit, tokens_row, lanes), lambda n: (n + start, 0, 0)),
            pl.BlockSpec((strip, tokens_row, channels), lambda n: (n + start, 0, 0)),
            fixed(weight),
            fixed(gate_up),
            fixed(down),
        ],
        out_specs=pl.BlockSpec((strip, tokens_row, channels), lambda n: (n, 0, 0)),
        out_shape=jax.ShapeDtypeStruct((count, tokens_row, channels), jnp.bfloat16),
        scratch_shapes=[
            pltpu.VMEM((turns, tokens_row * width // turns, strip * width), jnp.bfloat16),
            pltpu.VMEM((turns, strip // turns * tokens_row, width * width), jnp.bfloat16),
            pltpu.VMEM((strip * tokens_row, channels), jnp.bfloat16),
        ],
        compiler_params=kernel_params(40),
        cost_estimate=pl.CostEstimate(flops=flops, bytes_accessed=4 << 20, transcendentals=0),
    )(row_side, lane_side, scale, base, weight, gate_up, down)


def conv_kernel(
    valid_i, pair_two, *refs, parts
):
    counts = [len(p) for p in parts]
    total_parts = sum(counts)
    mirrored, refs = refs[:total_parts], refs[total_parts:]
    valid_j, top, bottom, left, right, weight, out, padded, centre = refs
    step = pl.program_id(0)
    rows, columns, channels = pair_two.shape
    strip = out.shape[0]

    @pl.when(step == 0)
    def _():
        padded[0, 8 : 8 + columns, :] = top[...].astype(jnp.float32)
        padded[rows + 1, 8 : 8 + columns, :] = bottom[...].astype(jnp.float32)
        i = 0
        used = 0
        for count in counts:
            group = mirrored[used : used + count]
            used += count
            for n in range(group[0].shape[0]):
                other = group[0][n].astype(jnp.float32)
                for more in group[1:]:
                    other = other + more[n].astype(jnp.float32)
                symmetric = (pair_two[i].astype(jnp.float32) + other) * 0.5
                centre[i] = symmetric
                keep = valid_j[...] * valid_i[i].astype(jnp.float32)
                padded[i + 1, 8 : 8 + columns, :] = symmetric * keep
                i += 1
        for i in range(rows + 2):
            padded[i, 7:8, :] = left[i : i + 1, :].astype(jnp.float32)
            padded[i, 8 + columns : 9 + columns, :] = right[i : i + 1, :].astype(jnp.float32)

    window = padded.at[pl.ds(step * strip, strip + 2)]
    shifted = [
        window[:, 7 + b : 7 + b + columns, :]
        .astype(jnp.bfloat16)
        .reshape((strip + 2) * columns, channels)
        for b in range(3)
    ]
    taps = jnp.dot(
        jnp.concatenate(shifted, axis=1), weight[...], preferred_element_type=jnp.float32
    ).reshape(strip + 2, columns, 3 * channels)
    total = centre[pl.ds(step * strip, strip)]
    for a in range(3):
        total = total + taps[a : a + strip, :, a * channels : (a + 1) * channels]
    out[...] = total.astype(out.dtype)


def convolve(pair_two, mirrored, valid_i, valid_j, halos, weight):
    rows, columns, channels = pair_two.shape
    strip = math.gcd(32, rows)
    operands = [pair_two, *[a for part in mirrored for a in part], valid_j, *halos, weight]
    fixed = lambda a: pl.BlockSpec(a.shape, lambda n, rank=a.ndim: (0,) * rank)
    return pl.pallas_call(
        functools.partial(conv_kernel, parts=[tuple(range(len(part))) for part in mirrored]),
        grid=(rows // strip,),
        in_specs=[pl.BlockSpec(memory_space=pltpu.SMEM)] + [fixed(a) for a in operands],
        out_specs=pl.BlockSpec((strip, columns, channels), lambda n: (n, 0, 0)),
        out_shape=jax.ShapeDtypeStruct(pair_two.shape, jnp.bfloat16),
        scratch_shapes=[
            pltpu.VMEM((rows + 2, columns + 16, channels), jnp.float32),
            pltpu.VMEM((rows, columns, channels), jnp.float32),
        ],
        compiler_params=kernel_params(40),
        cost_estimate=pl.CostEstimate(
            flops=18 * rows * columns * channels * channels,
            bytes_accessed=3 << 20,
            transcendentals=0,
        ),
    )(valid_i, *operands)


def shifts(size, step):
    return [(n, (n + step) % size) for n in range(size)]


def on_device(
    pair_input,
    alignment_features,
    alignment_mask,
    token_valid,
    left_weight,
    right_weight,
    output_weight,
    gate_weight,
    up_weight,
    down_weight,
    kernel_weight,
):
    rows_dev, cols_dev, channels = pair_input.shape
    local_rows, local_tokens, align_width = alignment_features.shape
    width = left_weight.shape[1]
    row_count, col_count = lax.axis_size("row"), lax.axis_size(plane)
    x_count, core_count = lax.axis_size("col"), lax.axis_size("chan")
    row_index, col_index = lax.axis_index("row"), lax.axis_index(plane)
    x_index, core_index = lax.axis_index("col"), lax.axis_index("chan")
    square = row_count == col_count
    tiles = [(r, c) for r in range(row_count) for c in range(col_count)]
    place_of = lambda r, c: r * col_count + c

    flat = alignment_features.reshape(local_rows * local_tokens, align_width)
    mask_rows = alignment_mask.astype(jnp.float32)
    projected = []
    for weight in (left_weight, right_weight):
        value = jnp.dot(flat, weight, preferred_element_type=jnp.float32)
        value = value.reshape(local_rows, local_tokens, width) * mask_rows[:, :, None]
        projected.append(value.astype(jnp.bfloat16))
    narrow_mask = alignment_mask.astype(jnp.bfloat16)

    def beside(side, mask):
        depth, tokens = mask.shape
        room = jnp.pad(mask, ((0, 0), (0, lanes - tokens % lanes)))
        return jnp.concatenate([side.reshape(depth, tokens * width), room], axis=1)

    if square:
        left_block, right_block = (beside(side, narrow_mask) for side in projected)
        mirror_pairs = [(place_of(r, c), place_of(c, r)) for r, c in tiles]
        first = lax.ppermute(left_block, whole, mirror_pairs)
        col_side, col_places = [right_block], [row_index]
        for step in range(1, row_count):
            col_side.append(lax.ppermute(right_block, "row", shifts(row_count, -step)))
            col_places.append((row_index + step) % row_count)
        row_side, row_places = [first], [col_index]
        for step in range(1, x_count):
            row_side.append(lax.ppermute(first, "col", shifts(x_count, -step)))
            row_places.append(((x_index + step) % x_count) * core_count + core_index)
        for step in range(1, core_count):
            for n in range(x_count):
                row_side.append(lax.ppermute(row_side[n], "chan", shifts(core_count, -step)))
                row_places.append(
                    ((x_index + n) % x_count) * core_count + (core_index + step) % core_count
                )
        places = jnp.stack(row_places + col_places).astype(jnp.int32) * local_rows
    else:
        left_wide = lax.all_gather(projected[0], plane, axis=1, tiled=True)
        mask_wide = lax.all_gather(narrow_mask, plane, axis=1, tiled=True)
        turn = lambda a: lax.all_to_all(a, "row", split_axis=1, concat_axis=0, tiled=True)
        gather = lambda a: lax.all_gather(a, "row", axis=0, tiled=True)
        row_side = [beside(turn(left_wide), turn(mask_wide))]
        col_side = [beside(gather(projected[1]), gather(narrow_mask))]
        places = jnp.zeros((2,), jnp.int32)

    split = output_weight.reshape(width // turns, turns, width, channels)
    weight = jnp.stack(
        [jnp.roll(split, u, axis=1).reshape(width * width, channels) for u in range(turns)]
    )
    gate_up = jnp.concatenate([gate_weight * 0.5, up_weight], axis=1).astype(jnp.bfloat16)
    conv_weight = kernel_weight.transpose(1, 2, 0, 3).reshape(3 * channels, 3 * channels)
    base = jnp.swapaxes(pair_input, 0, 1)

    sides = arrange(places, row_side, col_side, width, rows_dev, cols_dev)
    run = lambda first, count, strip: tile_strips(
        first, count, strip, *sides, base, weight, gate_up, down_weight
    )
    ahead = lambda size: [(n, n + 1) for n in range(size - 1)]
    back = lambda size: [(n + 1, n) for n in range(size - 1)]

    if square and cols_dev % (4 * unit) == 0 and x_count > 1:
        part = cols_dev // 4
        host = lambda r, c: place_of(r, (r // core_count) * core_count + c % core_count)
        away = [(r, c) for r, c in tiles if r // core_count != c // core_count]
        near = [(r, c) for r, c in tiles if r // core_count == c // core_count]
        to_host = [(place_of(r, c), host(r, c)) for r, c in away]
        from_host = [(host(r, c), place_of(c, r)) for r, c in away]
        beside_pairs = [(place_of(r, c), place_of(c, r)) for r, c in near]
        send = lambda value, pairs: lax.ppermute(value, whole, pairs)
        sent, mirrored = [], []
        for n in range(2):
            strip = run(n * part, part, part)
            sent.append(strip)
            mirrored.append(
                [send(send(strip, to_host), from_host), send(strip, beside_pairs)]
            )
        strip = run(2 * part, 2 * part, 2 * part)
        sent.append(strip)
        turned = jnp.concatenate(sent, axis=0)
        edges = jnp.stack([turned[0], turned[-1], turned[:, 0], turned[:, -1]])
        edges = send(edges, mirror_pairs)
        mirrored.append([send(strip, mirror_pairs)])
    else:
        turned = run(0, cols_dev, math.gcd(unit, cols_dev))
        share = rows_dev // col_count
        fold = row_count // col_count
        second = lax.all_to_all(
            lax.all_to_all(
                jnp.swapaxes(turned, 0, 1), plane, split_axis=0, concat_axis=1, tiled=True
            ),
            "row",
            split_axis=1,
            concat_axis=0,
            tiled=True,
        )
        third = lax.all_to_all(
            jnp.swapaxes(second, 0, 1), plane, split_axis=1, concat_axis=1, tiled=True
        )
        full = (
            third.reshape(rows_dev, col_count, fold, share, channels)
            .transpose(0, 2, 1, 3, 4)
            .reshape(rows_dev, cols_dev, channels)
        )
        mirrored = [[full]]
        edges = (full[0], full[-1], full[:, 0], full[:, -1])

    pair_two = jnp.swapaxes(turned, 0, 1)
    valid_i = lax.dynamic_slice_in_dim(token_valid, row_index * rows_dev, rows_dev)
    valid_j = lax.dynamic_slice_in_dim(token_valid, col_index * cols_dev, cols_dev)
    keep_i = valid_i.astype(jnp.float32)[:, None]
    keep_j = valid_j.astype(jnp.float32)[:, None]
    mean = lambda a, b: (a.astype(jnp.float32) + b.astype(jnp.float32)) * 0.5
    last_i, last_j = rows_dev - 1, cols_dev - 1
    first_line = (mean(turned[:, 0], edges[0]) * keep_j * keep_i[0]).astype(jnp.bfloat16)
    last_line = (mean(turned[:, -1], edges[1]) * keep_j * keep_i[last_i]).astype(jnp.bfloat16)
    first_side = (mean(turned[0], edges[2]) * keep_i * keep_j[0]).astype(jnp.bfloat16)
    last_side = (mean(turned[-1], edges[3]) * keep_i * keep_j[last_j]).astype(jnp.bfloat16)
    left = lax.ppermute(last_side, plane, ahead(col_count))
    right = lax.ppermute(first_side, plane, back(col_count))
    border = lambda i, line: jnp.concatenate([left[i][None], line, right[i][None]], axis=0)
    top = lax.ppermute(border(last_i, last_line), "row", ahead(row_count))
    bottom = lax.ppermute(border(0, first_line), "row", back(row_count))
    left = jnp.concatenate([top[:1], left, bottom[:1]], axis=0)
    right = jnp.concatenate([top[-1:], right, bottom[-1:]], axis=0)
    wide_valid = jnp.broadcast_to(keep_j, (cols_dev, channels))
    return convolve(
        pair_two,
        mirrored,
        valid_i,
        wide_valid,
        [top[1:-1], bottom[1:-1], left, right],
        conv_weight,
    )


def solution(mesh):
    placed = (
        P(("groups", "row"), plane, None),
        P("row", ("groups", "col", "chan"), None),
        P("row", ("groups", "col", "chan")),
        P("groups"),
        P(),
        P(),
        P(),
        P(),
        P(),
        P(),
        P(),
    )
    return jax.shard_map(
        on_device,
        mesh=mesh,
        in_specs=placed,
        out_specs=P(("groups", "row"), plane, None),
        check_vma=False,
    )
```

time: 128 us -> 124 us (0.969)
  the two profiles are of different devices: /device:TPU:1 before, /device:TPU:21 now
where the time goes in v2:
time: 124 us; the launch traced here: 123 us
  waiting for transfers between devices  51.2 us (41%)
  starting transfers between devices  37.4 us (30%)
  Pallas kernels  18.7 us (15%)
  other arithmetic  7.25 us (6%)
  local copies, waits for them, and re-layouts  6.44 us (5%)
  matrix products  1.86 us (2%)
    ppermute x8, waiting for transfers between devices, on_device(): send = lambda value, pairs: lax.ppermute(value, whole, pairs)  28.1 us
    pallas_call x3, Pallas kernels, tile_strips(): pl.pallas_call(tile_kernel, grid=(count // strip,), in_specs=[fixed(row_s...  12.5 us
    ppermute x8, starting transfers between devices, on_device(): send = lambda value, pairs: lax.ppermute(value, whole, pairs)  11.7 us
    ppermute x1, waiting for transfers between devices, on_device(): first = lax.ppermute(left_block, whole, mirror_pairs)  9.77 us
    ppermute x1, starting transfers between devices, on_device(): bottom = lax.ppermute(border(0, first_line), 'row', back(row_count))  7.88 us
    ppermute x1, waiting for transfers between devices, on_device(): bottom = lax.ppermute(border(0, first_line), 'row', back(row_count))  6.29 us
    ppermute x1, starting transfers between devices, on_device(): first = lax.ppermute(left_block, whole, mirror_pairs)  5.87 us
    ppermute x1, starting transfers between devices, on_device(): right = lax.ppermute(first_side, plane, back(col_count))  4.62 us
  transfers between devices with their start and end apart: 19, of which 8 were waited for; matrix products, arithmetic and copies ran while one was open for 5% of the time, Pallas kernels for 0%

profile of v2, /device:TPU:21, one launch (start us, length us, event | category | flops | bytes accessed | tf_op | source)
XLA Modules:
  0.0 123.4 jit_solution(11636116263217420308)
XLA Ops:
  5.5 3.2 %collective-permute-start.5 = (bf16[32,2176]{1,0:T(8,128)(2,1)S(1)}, bf16[32,2176]{1,0:T(8,128)(2,1)S(1)}, u32[]{:S(2)}, u32[]{:S(2)}) collective-permute-start(bf16[32,2176]{1,0:T(8,128)(2,1)S(1)} %get-tuple-element.39.refs_4_), channel_id=1, source_target_pairs={{0,8},{4,12},{8,0},{12,4},{1,9},{5,13},{9,1},{13,5},{2,10},{6,14},... | collective-permute-start | bytes 417800 | tf_op jit(solution)/shard_map/ppermute | solution.py:307
  8.7 5.9 %collective-permute-start = (bf16[32,2176]{1,0:T(8,128)(2,1)}, bf16[32,2176]{1,0:T(8,128)(2,1)S(1)}, u32[]{:S(2)}, u32[]{:S(2)}) collective-permute-start(bf16[32,2176]{1,0:T(8,128)(2,1)} %get-tuple-element.40), channel_id=1, source_target_pairs={{0,0},{1,4},{2,8},{3,12},{4,1},{5,5},{6,9},{7,13},{8,2},{9,6},{10,... | collective-permute-start | bytes 417800 | tf_op jit(solution)/shard_map/ppermute | solution.py:304
  18.1 9.8 %collective-permute-done.refs_0_ = bf16[32,2176]{1,0:T(8,128)(2,1)S(1)} collective-permute-done((bf16[32,2176]{1,0:T(8,128)(2,1)}, bf16[32,2176]{1,0:T(8,128)(2,1)S(1)}, u32[]{:S(2)}, u32[]{:S(2)}) %collective-permute-start) | collective-permute-done | bytes 139296 | tf_op jit(solution)/shard_map/ppermute | solution.py:304
  28.9 2.9 %collective-permute-done.1.refs_1_ = bf16[32,2176]{1,0:T(8,128)(2,1)S(1)} collective-permute-done((bf16[32,2176]{1,0:T(8,128)(2,1)S(1)}, bf16[32,2176]{1,0:T(8,128)(2,1)S(1)}, u32[]{:S(2)}, u32[]{:S(2)}) %collective-permute-start.1) | collective-permute-done | bytes 139296 | tf_op jit(solution)/shard_map/ppermute | solution.py:311
  33.3 2.0 %shard_map.109 = (bf16[2048,128]{1,0:T(8,128)(2,1)S(1)}, bf16[4,128,2048]{2,1,0:T(8,128)(2,1)S(1)}, f32[4,64,128]{2,1,0:T(8,128)S(1)}) custom-call(s32[8]{0:T(128)S(1)} %broadcast_multiply_fusion.3.places, bf16[32,2176]{1,0:T(8,128)(2,1)S(1)} %collective-permute-done.refs_0_, bf16[32,2176]{1,0:T(8,128)(2,1)S(1)} %collective-permute-done.1.refs_1_, ...), custom_call_target="tpu_custom_call" | custom-call | flops 16777216 | bytes 4194304 | tf_op jit(solution)/shard_map/pallas_call | solution.py:76
  35.3 5.9 %shard_map.112 = bf16[32,64,128]{2,1,0:T(8,128)(2,1)S(1)} custom-call(bf16[2048,128]{1,0:T(8,128)(2,1)S(1)} %get-tuple-element.8.row_side, bf16[4,128,2048]{2,1,0:T(8,128)(2,1)S(1)} %get-tuple-element.9.lane_side, f32[4,64,128]{2,1,0:T(8,128)S(1)} %get-tuple-element.10.scale, bf16[64,64,128]{2,1,0:T(8,128)(2,1)S(1)} %bitcast.67, ...), custom_call_target="tpu_custom_call" | custom-call | flops 1879048192 | bytes 4194304 | tf_op jit(solution)/shard_map/pallas_call | solution.py:162
  41.1 3.2 %shard_map.111 = bf16[16,64,128]{2,1,0:T(8,128)(2,1)S(1)} custom-call(bf16[2048,128]{1,0:T(8,128)(2,1)S(1)} %get-tuple-element.8.row_side, bf16[4,128,2048]{2,1,0:T(8,128)(2,1)S(1)} %get-tuple-element.9.lane_side, f32[4,64,128]{2,1,0:T(8,128)S(1)} %get-tuple-element.10.scale, bf16[64,64,128]{2,1,0:T(8,128)(2,1)S(1)} %bitcast.68, ...), custom_call_target="tpu_custom_call" | custom-call | flops 939524096 | bytes 4194304 | tf_op jit(solution)/shard_map/pallas_call | solution.py:162
  44.3 3.4 %shard_map.110 = bf16[16,64,128]{2,1,0:T(8,128)(2,1)S(1)} custom-call(bf16[2048,128]{1,0:T(8,128)(2,1)S(1)} %get-tuple-element.8.row_side, bf16[4,128,2048]{2,1,0:T(8,128)(2,1)S(1)} %get-tuple-element.9.lane_side, f32[4,64,128]{2,1,0:T(8,128)S(1)} %get-tuple-element.10.scale, bf16[64,64,128]{2,1,0:T(8,128)(2,1)S(1)} %bitcast.69, ...), custom_call_target="tpu_custom_call" | custom-call | flops 939524096 | bytes 4194304 | tf_op jit(solution)/shard_map/pallas_call | solution.py:162
  48.6 3.0 %collective-permute-start.14 = (bf16[4,64,128]{2,1,0:T(8,128)(2,1)S(1)}, bf16[4,64,128]{2,1,0:T(8,128)(2,1)S(1)}, u32[]{:S(2)}, u32[]{:S(2)}) collective-permute-start(bf16[4,64,128]{2,1,0:T(8,128)(2,1)S(1)} %pad_maximum_fusion.5), channel_id=1, source_target_pairs={{0,0},{1,4},{2,8},{3,12},{4,1},{5,5},{6,9},{7,13},{8,2},{9,6},{10,... | collective-permute-start | bytes 196616 | tf_op jit(solution)/shard_map/ppermute | solution.py:352
  52.2 4.6 %collective-permute-done.14 = bf16[4,64,128]{2,1,0:T(8,128)(2,1)S(1)} collective-permute-done((bf16[4,64,128]{2,1,0:T(8,128)(2,1)S(1)}, bf16[4,64,128]{2,1,0:T(8,128)(2,1)S(1)}, u32[]{:S(2)}, u32[]{:S(2)}) %collective-permute-start.14) | collective-permute-done | bytes 65568 | tf_op jit(solution)/shard_map/ppermute | solution.py:352
  56.8 2.6 %fusion.7 = (bf16[64,128]{1,0:T(8,128)(2,1)S(1)}, bf16[64,128]{1,0:T(8,128)(2,1)S(1)}, bf16[64,128]{1,0:T(8,128)(2,1)S(1)}, bf16[64,128]{1,0:T(8,128)(2,1)S(1)}) fusion(bf16[4,64,128]{2,1,0:T(8,128)(2,1)S(1)} %collective-permute-done.14, f32[]{:T(128)} %bitcast.28, f32[64]{0:T(128)S(1)} %get-tuple-element.11, ...), kind=kLoop, calls=%fused_computation.23 | loop fusion | flops 196608 | bytes 197136 | tf_op jit(solution)/shard_map/convert_element_type | solution.py:397
  59.5 1.9 %collective-permute-start.15 = (bf16[64,128]{1,0:T(8,128)(2,1)S(1)}, bf16[64,128]{1,0:T(8,128)(2,1)S(1)}, u32[]{:S(2)}, u32[]{:S(2)}) collective-permute-start(bf16[64,128]{1,0:T(8,128)(2,1)S(1)} %get-tuple-element.28), channel_id=1, source_target_pairs={{0,1},{1,2},{2,3},{4,5},{5,6},{6,7},{8,9},{9,10},{10,11},{12,13},{... | collective-permute-start | bytes 49160 | tf_op jit(solution)/shard_map/ppermute | solution.py:401
  61.7 2.1 %collective-permute-start.13 = (bf16[32,64,128]{2,1,0:T(8,128)(2,1)S(1)}, bf16[32,64,128]{2,1,0:T(8,128)(2,1)S(1)}, u32[]{:S(2)}, u32[]{:S(2)}) collective-permute-start(bf16[32,64,128]{2,1,0:T(8,128)(2,1)S(1)} %shard_map.112), channel_id=1, source_target_pairs={{0,0},{1,4},{2,8},{3,12},{4,1},{5,5},{6,9},{7,13},{8,2},{9,6},{10,... | collective-permute-start | bytes 1572872 | tf_op jit(solution)/shard_map/ppermute | solution.py:352
  63.8 1.3 %collective-permute-start.10 = (bf16[16,64,128]{2,1,0:T(8,128)(2,1)S(1)}, bf16[16,64,128]{2,1,0:T(8,128)(2,1)S(1)}, u32[]{:S(2)}, u32[]{:S(2)}) collective-permute-start(bf16[16,64,128]{2,1,0:T(8,128)(2,1)S(1)} %shard_map.111), channel_id=1, source_target_pairs={{2,0},{3,1},{6,4},{7,5},{8,10},{9,11},{12,14},{13,15},{18,16},{19,... | collective-permute-start | bytes 786440 | tf_op jit(solution)/shard_map/ppermute | solution.py:352
  65.8 1.4 %collective-permute-start.7 = (bf16[16,64,128]{2,1,0:T(8,128)(2,1)S(1)}, bf16[16,64,128]{2,1,0:T(8,128)(2,1)S(1)}, u32[]{:S(2)}, u32[]{:S(2)}) collective-permute-start(bf16[16,64,128]{2,1,0:T(8,128)(2,1)S(1)} %shard_map.110), channel_id=1, source_target_pairs={{2,0},{3,1},{6,4},{7,5},{8,10},{9,11},{12,14},{13,15},{18,16},{19,... | collective-permute-start | bytes 786440 | tf_op jit(solution)/shard_map/ppermute | solution.py:352
  67.3 4.6 %collective-permute-start.16 = (bf16[64,128]{1,0:T(8,128)(2,1)S(1)}, bf16[64,128]{1,0:T(8,128)(2,1)S(1)}, u32[]{:S(2)}, u32[]{:S(2)}) collective-permute-start(bf16[64,128]{1,0:T(8,128)(2,1)S(1)} %get-tuple-element.27), channel_id=1, source_target_pairs={{1,0},{2,1},{3,2},{5,4},{6,5},{7,6},{9,8},{10,9},{11,10},{13,12},{... | collective-permute-start | bytes 49160 | tf_op jit(solution)/shard_map/ppermute | solution.py:402
  72.8 7.9 %collective-permute-start.18 = (bf16[66,128]{1,0:T(8,128)(2,1)S(1)}, bf16[66,128]{1,0:T(8,128)(2,1)S(1)}, u32[]{:S(2)}, u32[]{:S(2)}) collective-permute-start(bf16[66,128]{1,0:T(8,128)(2,1)S(1)} %pad_maximum_fusion.7), channel_id=1, source_target_pairs={{4,0},{8,4},{12,8},{5,1},{9,5},{13,9},{6,2},{10,6},{14,10},{7,3},{... | collective-permute-start | bytes 50696 | tf_op jit(solution)/shard_map/ppermute | solution.py:405
  80.7 6.3 %collective-permute-done.18 = bf16[66,128]{1,0:T(8,128)(2,1)S(1)} collective-permute-done((bf16[66,128]{1,0:T(8,128)(2,1)S(1)}, bf16[66,128]{1,0:T(8,128)(2,1)S(1)}, u32[]{:S(2)}, u32[]{:S(2)}) %collective-permute-start.18) | collective-permute-done | bytes 16928 | tf_op jit(solution)/shard_map/ppermute | solution.py:405
  87.0 1.9 %collective-permute-start.17 = (bf16[66,128]{1,0:T(8,128)(2,1)S(1)}, bf16[66,128]{1,0:T(8,128)(2,1)S(1)}, u32[]{:S(2)}, u32[]{:S(2)}) collective-permute-start(bf16[66,128]{1,0:T(8,128)(2,1)S(1)} %pad_maximum_fusion.6), channel_id=1, source_target_pairs={{0,4},{4,8},{8,12},{1,5},{5,9},{9,13},{2,6},{6,10},{10,14},{3,7},{... | collective-permute-start | bytes 50696 | tf_op jit(solution)/shard_map/ppermute | solution.py:404
  89.0 3.3 %collective-permute-done.17 = bf16[66,128]{1,0:T(8,128)(2,1)S(1)} collective-permute-done((bf16[66,128]{1,0:T(8,128)(2,1)S(1)}, bf16[66,128]{1,0:T(8,128)(2,1)S(1)}, u32[]{:S(2)}, u32[]{:S(2)}) %collective-permute-start.17) | collective-permute-done | bytes 16928 | tf_op jit(solution)/shard_map/ppermute | solution.py:404
  93.0 1.3 %collective-permute-start.11 = (bf16[16,64,128]{2,1,0:T(8,128)(2,1)S(1)}, bf16[16,64,128]{2,1,0:T(8,128)(2,1)S(1)}, u32[]{:S(2)}, u32[]{:S(2)}) collective-permute-start(bf16[16,64,128]{2,1,0:T(8,128)(2,1)S(1)} %collective-permute-done.10), channel_id=1, source_target_pairs={{0,8},{1,12},{4,9},{5,13},{10,2},{11,6},{14,3},{15,7},{16,24},{17,... | collective-permute-start | bytes 786440 | tf_op jit(solution)/shard_map/ppermute | solution.py:352
  95.7 20.6 %collective-permute-done.11.refs_2_ = bf16[16,64,128]{2,1,0:T(8,128)(2,1)S(1)} collective-permute-done((bf16[16,64,128]{2,1,0:T(8,128)(2,1)S(1)}, bf16[16,64,128]{2,1,0:T(8,128)(2,1)S(1)}, u32[]{:S(2)}, u32[]{:S(2)}) %collective-permute-start.11) | collective-permute-done | bytes 262176 | tf_op jit(solution)/shard_map/ppermute | solution.py:352
  116.3 2.8 %collective-permute-done.8.refs_0_ = bf16[16,64,128]{2,1,0:T(8,128)(2,1)S(1)} collective-permute-done((bf16[16,64,128]{2,1,0:T(8,128)(2,1)S(1)}, bf16[16,64,128]{2,1,0:T(8,128)(2,1)S(1)}, u32[]{:S(2)}, u32[]{:S(2)}) %collective-permute-start.8) | collective-permute-done | bytes 262176 | tf_op jit(solution)/shard_map/ppermute | solution.py:352
  119.2 4.2 %shard_map.113 = bf16[64,64,128]{2,1,0:T(8,128)(2,1)} custom-call(s32[64]{0:T(128)S(1)} %get-tuple-element.14.valid_i, bf16[64,64,128]{2,1,0:T(8,128)(2,1)S(1)} %bitcast.71, bf16[16,64,128]{2,1,0:T(8,128)(2,1)S(1)} %collective-permute-done.8.refs_0_, bf16[16,64,128]{2,1,0:T(8,128)(2,1)S(1)} %collective-permute-done.9.refs_1_, ...), custom_call_target="tpu_custom_call" | custom-call | flops 1207959552 | bytes 3145728 | tf_op jit(solution)/shard_map/pallas_call | solution.py:240
  (80 shorter events, 16.7 us)
Async XLA Ops:
  2.4 12.3 %copy-start.2 = (bf16[1024,128]{1,0:T(8,128)(2,1)S(1)}, bf16[1024,128]{1,0:T(8,128)(2,1)}, u32[]{:S(2)}) copy-start(bf16[1024,128]{1,0:T(8,128)(2,1)} %param.17) | copy-start | bytes 786436
  3.2 12.9 %copy-start.5 = (bf16[128,512]{1,0:T(8,128)(2,1)S(1)}, bf16[128,512]{1,0:T(8,128)(2,1)}, u32[]{:S(2)}) copy-start(bf16[128,512]{1,0:T(8,128)(2,1)} %param.18) | copy-start | bytes 393220
  3.8 12.3 %copy-start.7 = (s32[256]{0:T(256)S(1)}, s32[256]{0:T(256)}, u32[]{:S(2)}) copy-start(s32[256]{0:T(256)} %param.14) | copy-start | bytes 3076
  5.4 27.0 %copy-start.3 = (bf16[64,64,128]{2,1,0:T(8,128)(2,1)S(1)}, bf16[64,64,128]{2,1,0:T(8,128)(2,1)}, u32[]{:S(2)}) copy-start(bf16[64,64,128]{2,1,0:T(8,128)(2,1)} %param.11) | copy-start | bytes 3145732
  5.4 27.8 %collective-permute-start.4 = (bf16[32,2176]{1,0:T(8,128)(2,1)S(1)}, bf16[32,2176]{1,0:T(8,128)(2,1)S(1)}, u32[]{:S(2)}, u32[]{:S(2)}) collective-permute-start(bf16[32,2176]{1,0:T(8,128)(2,1)S(1)} %get-tuple-element.39.refs_4_), channel_id=1, source_target_pairs={{0,12},{4,0},{8,4},{12,8},{1,13},{5,1},{9,5},{13,9},{2,14},{6,2},{... | collective-permute-start | bytes 417800 | tf_op jit(solution)/shard_map/ppermute | solution.py:307
  5.5 27.7 %collective-permute-start.5 = (bf16[32,2176]{1,0:T(8,128)(2,1)S(1)}, bf16[32,2176]{1,0:T(8,128)(2,1)S(1)}, u32[]{:S(2)}, u32[]{:S(2)}) collective-permute-start(bf16[32,2176]{1,0:T(8,128)(2,1)S(1)} %get-tuple-element.39.refs_4_), channel_id=1, source_target_pairs={{0,8},{4,12},{8,0},{12,4},{1,9},{5,13},{9,1},{13,5},{2,10},{6,14},... | collective-permute-start | bytes 417800 | tf_op jit(solution)/shard_map/ppermute | solution.py:307
  8.7 24.5 %collective-permute-start.6 = (bf16[32,2176]{1,0:T(8,128)(2,1)S(1)}, bf16[32,2176]{1,0:T(8,128)(2,1)S(1)}, u32[]{:S(2)}, u32[]{:S(2)}) collective-permute-start(bf16[32,2176]{1,0:T(8,128)(2,1)S(1)} %get-tuple-element.39.refs_4_), channel_id=1, source_target_pairs={{0,4},{4,8},{8,12},{12,0},{1,5},{5,9},{9,13},{13,1},{2,6},{6,10},{... | collective-permute-start | bytes 417800 | tf_op jit(solution)/shard_map/ppermute | solution.py:307
  8.7 19.1 %collective-permute-start = (bf16[32,2176]{1,0:T(8,128)(2,1)}, bf16[32,2176]{1,0:T(8,128)(2,1)S(1)}, u32[]{:S(2)}, u32[]{:S(2)}) collective-permute-start(bf16[32,2176]{1,0:T(8,128)(2,1)} %get-tuple-element.40), channel_id=1, source_target_pairs={{0,0},{1,4},{2,8},{3,12},{4,1},{5,5},{6,9},{7,13},{8,2},{9,6},{10,... | collective-permute-start | bytes 417800 | tf_op jit(solution)/shard_map/ppermute | solution.py:304
  27.9 3.9 %collective-permute-start.1 = (bf16[32,2176]{1,0:T(8,128)(2,1)S(1)}, bf16[32,2176]{1,0:T(8,128)(2,1)S(1)}, u32[]{:S(2)}, u32[]{:S(2)}) collective-permute-start(bf16[32,2176]{1,0:T(8,128)(2,1)S(1)} %collective-permute-done.refs_0_), channel_id=1, source_target_pairs={{0,2},{2,0},{1,3},{3,1},{4,6},{6,4},{5,7},{7,5},{8,10},{10,8},{9,1... | collective-permute-start | bytes 417800 | tf_op jit(solution)/shard_map/ppermute | solution.py:311
  28.8 4.4 %collective-permute-start.2 = (bf16[32,2176]{1,0:T(8,128)(2,1)S(1)}, bf16[32,2176]{1,0:T(8,128)(2,1)S(1)}, u32[]{:S(2)}, u32[]{:S(2)}) collective-permute-start(bf16[32,2176]{1,0:T(8,128)(2,1)S(1)} %collective-permute-done.refs_0_), channel_id=1, source_target_pairs={{0,1},{1,0},{2,3},{3,2},{4,5},{5,4},{6,7},{7,6},{8,9},{9,8},{10,11... | collective-permute-start | bytes 417800 | tf_op jit(solution)/shard_map/ppermute | solution.py:315
  31.8 1.5 %collective-permute-start.3 = (bf16[32,2176]{1,0:T(8,128)(2,1)S(1)}, bf16[32,2176]{1,0:T(8,128)(2,1)S(1)}, u32[]{:S(2)}, u32[]{:S(2)}) collective-permute-start(bf16[32,2176]{1,0:T(8,128)(2,1)S(1)} %collective-permute-done.1.refs_1_), channel_id=1, source_target_pairs={{0,1},{1,0},{2,3},{3,2},{4,5},{5,4},{6,7},{7,6},{8,9},{9,8},{10,11... | collective-permute-start | bytes 417800 | tf_op jit(solution)/shard_map/ppermute | solution.py:315
  47.8 13.6 %copy-start.4 = (bf16[3,3,128,128]{3,2,1,0:T(8,128)(2,1)S(1)}, bf16[3,3,128,128]{3,2,1,0:T(8,128)(2,1)}, u32[]{:S(2)}) copy-start(bf16[3,3,128,128]{3,2,1,0:T(8,128)(2,1)} %param.21) | copy-start | bytes 884740
  48.6 8.2 %collective-permute-start.14 = (bf16[4,64,128]{2,1,0:T(8,128)(2,1)S(1)}, bf16[4,64,128]{2,1,0:T(8,128)(2,1)S(1)}, u32[]{:S(2)}, u32[]{:S(2)}) collective-permute-start(bf16[4,64,128]{2,1,0:T(8,128)(2,1)S(1)} %pad_maximum_fusion.5), channel_id=1, source_target_pairs={{0,0},{1,4},{2,8},{3,12},{4,1},{5,5},{6,9},{7,13},{8,2},{9,6},{10,... | collective-permute-start | bytes 196616 | tf_op jit(solution)/shard_map/ppermute | solution.py:352
  59.5 7.8 %collective-permute-start.15 = (bf16[64,128]{1,0:T(8,128)(2,1)S(1)}, bf16[64,128]{1,0:T(8,128)(2,1)S(1)}, u32[]{:S(2)}, u32[]{:S(2)}) collective-permute-start(bf16[64,128]{1,0:T(8,128)(2,1)S(1)} %get-tuple-element.28), channel_id=1, source_target_pairs={{0,1},{1,2},{2,3},{4,5},{5,6},{6,7},{8,9},{9,10},{10,11},{12,13},{... | collective-permute-start | bytes 49160 | tf_op jit(solution)/shard_map/ppermute | solution.py:401
  61.7 33.9 %collective-permute-start.13 = (bf16[32,64,128]{2,1,0:T(8,128)(2,1)S(1)}, bf16[32,64,128]{2,1,0:T(8,128)(2,1)S(1)}, u32[]{:S(2)}, u32[]{:S(2)}) collective-permute-start(bf16[32,64,128]{2,1,0:T(8,128)(2,1)S(1)} %shard_map.112), channel_id=1, source_target_pairs={{0,0},{1,4},{2,8},{3,12},{4,1},{5,5},{6,9},{7,13},{8,2},{9,6},{10,... | collective-permute-start | bytes 1572872 | tf_op jit(solution)/shard_map/ppermute | solution.py:352
  63.8 29.1 %collective-permute-start.10 = (bf16[16,64,128]{2,1,0:T(8,128)(2,1)S(1)}, bf16[16,64,128]{2,1,0:T(8,128)(2,1)S(1)}, u32[]{:S(2)}, u32[]{:S(2)}) collective-permute-start(bf16[16,64,128]{2,1,0:T(8,128)(2,1)S(1)} %shard_map.111), channel_id=1, source_target_pairs={{2,0},{3,1},{6,4},{7,5},{8,10},{9,11},{12,14},{13,15},{18,16},{19,... | collective-permute-start | bytes 786440 | tf_op jit(solution)/shard_map/ppermute | solution.py:352
  65.2 30.5 %collective-permute-start.12 = (bf16[16,64,128]{2,1,0:T(8,128)(2,1)S(1)}, bf16[16,64,128]{2,1,0:T(8,128)(2,1)S(1)}, u32[]{:S(2)}, u32[]{:S(2)}) collective-permute-start(bf16[16,64,128]{2,1,0:T(8,128)(2,1)S(1)} %shard_map.111), channel_id=1, source_target_pairs={{0,0},{1,4},{4,1},{5,5},{10,10},{11,14},{14,11},{15,15},{16,16},{1... | collective-permute-start | bytes 786440 | tf_op jit(solution)/shard_map/ppermute | solution.py:352
  65.8 28.4 %collective-permute-start.7 = (bf16[16,64,128]{2,1,0:T(8,128)(2,1)S(1)}, bf16[16,64,128]{2,1,0:T(8,128)(2,1)S(1)}, u32[]{:S(2)}, u32[]{:S(2)}) collective-permute-start(bf16[16,64,128]{2,1,0:T(8,128)(2,1)S(1)} %shard_map.110), channel_id=1, source_target_pairs={{2,0},{3,1},{6,4},{7,5},{8,10},{9,11},{12,14},{13,15},{18,16},{19,... | collective-permute-start | bytes 786440 | tf_op jit(solution)/shard_map/ppermute | solution.py:352
  67.3 5.5 %collective-permute-start.16 = (bf16[64,128]{1,0:T(8,128)(2,1)S(1)}, bf16[64,128]{1,0:T(8,128)(2,1)S(1)}, u32[]{:S(2)}, u32[]{:S(2)}) collective-permute-start(bf16[64,128]{1,0:T(8,128)(2,1)S(1)} %get-tuple-element.27), channel_id=1, source_target_pairs={{1,0},{2,1},{3,2},{5,4},{6,5},{7,6},{9,8},{10,9},{11,10},{13,12},{... | collective-permute-start | bytes 49160 | tf_op jit(solution)/shard_map/ppermute | solution.py:402
  72.8 14.2 %collective-permute-start.18 = (bf16[66,128]{1,0:T(8,128)(2,1)S(1)}, bf16[66,128]{1,0:T(8,128)(2,1)S(1)}, u32[]{:S(2)}, u32[]{:S(2)}) collective-permute-start(bf16[66,128]{1,0:T(8,128)(2,1)S(1)} %pad_maximum_fusion.7), channel_id=1, source_target_pairs={{4,0},{8,4},{12,8},{5,1},{9,5},{13,9},{6,2},{10,6},{14,10},{7,3},{... | collective-permute-start | bytes 50696 | tf_op jit(solution)/shard_map/ppermute | solution.py:405
  87.0 5.2 %collective-permute-start.17 = (bf16[66,128]{1,0:T(8,128)(2,1)S(1)}, bf16[66,128]{1,0:T(8,128)(2,1)S(1)}, u32[]{:S(2)}, u32[]{:S(2)}) collective-permute-start(bf16[66,128]{1,0:T(8,128)(2,1)S(1)} %pad_maximum_fusion.6), channel_id=1, source_target_pairs={{0,4},{4,8},{8,12},{1,5},{5,9},{9,13},{2,6},{6,10},{10,14},{3,7},{... | collective-permute-start | bytes 50696 | tf_op jit(solution)/shard_map/ppermute | solution.py:404
  92.3 3.4 %collective-permute-start.9 = (bf16[16,64,128]{2,1,0:T(8,128)(2,1)S(1)}, bf16[16,64,128]{2,1,0:T(8,128)(2,1)S(1)}, u32[]{:S(2)}, u32[]{:S(2)}) collective-permute-start(bf16[16,64,128]{2,1,0:T(8,128)(2,1)S(1)} %shard_map.110), channel_id=1, source_target_pairs={{0,0},{1,4},{4,1},{5,5},{10,10},{11,14},{14,11},{15,15},{16,16},{1... | collective-permute-start | bytes 786440 | tf_op jit(solution)/shard_map/ppermute | solution.py:352
  93.0 23.3 %collective-permute-start.11 = (bf16[16,64,128]{2,1,0:T(8,128)(2,1)S(1)}, bf16[16,64,128]{2,1,0:T(8,128)(2,1)S(1)}, u32[]{:S(2)}, u32[]{:S(2)}) collective-permute-start(bf16[16,64,128]{2,1,0:T(8,128)(2,1)S(1)} %collective-permute-done.10), channel_id=1, source_target_pairs={{0,8},{1,12},{4,9},{5,13},{10,2},{11,6},{14,3},{15,7},{16,24},{17,... | collective-permute-start | bytes 786440 | tf_op jit(solution)/shard_map/ppermute | solution.py:352
  94.3 24.8 %collective-permute-start.8 = (bf16[16,64,128]{2,1,0:T(8,128)(2,1)S(1)}, bf16[16,64,128]{2,1,0:T(8,128)(2,1)S(1)}, u32[]{:S(2)}, u32[]{:S(2)}) collective-permute-start(bf16[16,64,128]{2,1,0:T(8,128)(2,1)S(1)} %collective-permute-done.7), channel_id=1, source_target_pairs={{0,8},{1,12},{4,9},{5,13},{10,2},{11,6},{14,3},{15,7},{16,24},{17,... | collective-permute-start | bytes 786440 | tf_op jit(solution)/shard_map/ppermute | solution.py:352
  (3 other events, 6.5 us)

commit v3 on v2

--- a/solution.py
+++ b/solution.py
@@ -13,7 +13,7 @@
 turns = 4
 plane = ("col", "chan")
 whole = ("row", "col", "chan")
-unit = 16
+unit = 8
 
 
 def kernel_params(mib):
@@ -90,7 +90,7 @@
             pltpu.VMEM((depth, lanes), jnp.bfloat16),
         ],
         compiler_params=kernel_params(12),
-        cost_estimate=pl.CostEstimate(flops=1 << 24, bytes_accessed=4 << 20, transcendentals=0),
+        cost_estimate=pl.CostEstimate(flops=1024, bytes_accessed=1024, transcendentals=0),
     )(places, *row_side, *col_side)
 
 
@@ -145,7 +145,7 @@
             value = update[g * tokens_row : (g + 1) * tokens_row] * factor
             value = base[n].astype(jnp.float32) + value
             held[n * tokens_row : (n + 1) * tokens_row, :] = value.astype(jnp.bfloat16)
-    piece = min(16, strip)
+    piece = math.gcd(strip, 24) if strip > 24 else strip
     for first in range(0, strip, piece):
         at = slice(first * tokens_row, (first + piece) * tokens_row)
         result = transition_rows(held[at, :].astype(jnp.float32), gate_up[...], down[...])
@@ -158,7 +158,6 @@
     width = span // base.shape[0]
     start = first // strip
     fixed = lambda a: pl.BlockSpec(a.shape, lambda n, rank=a.ndim: (0,) * rank)
-    flops = 2 * count * tokens_row * (width * width * (depth + channels) + 3 * channels * 512)
     return pl.pallas_call(
         tile_kernel,
         grid=(count // strip,),
@@ -179,7 +178,7 @@
             pltpu.VMEM((strip * tokens_row, channels), jnp.bfloat16),
         ],
         compiler_params=kernel_params(40),
-        cost_estimate=pl.CostEstimate(flops=flops, bytes_accessed=4 << 20, transcendentals=0),
+        cost_estimate=pl.CostEstimate(flops=1024, bytes_accessed=1024, transcendentals=0),
     )(row_side, lane_side, scale, base, weight, gate_up, down)
 
 
@@ -286,11 +285,12 @@
 
     flat = alignment_features.reshape(local_rows * local_tokens, align_width)
     mask_rows = alignment_mask.astype(jnp.float32)
-    projected = []
-    for weight in (left_weight, right_weight):
+
+    def project(flat, weight):
         value = jnp.dot(flat, weight, preferred_element_type=jnp.float32)
         value = value.reshape(local_rows, local_tokens, width) * mask_rows[:, :, None]
-        projected.append(value.astype(jnp.bfloat16))
+        return value.astype(jnp.bfloat16)
+
     narrow_mask = alignment_mask.astype(jnp.bfloat16)
 
     def beside(side, mask):
@@ -299,9 +299,11 @@
         return jnp.concatenate([side.reshape(depth, tokens * width), room], axis=1)
 
     if square:
-        left_block, right_block = (beside(side, narrow_mask) for side in projected)
+        left_block = beside(project(flat, left_weight), narrow_mask)
+        flat, left_block = lax.optimization_barrier((flat, left_block))
         mirror_pairs = [(place_of(r, c), place_of(c, r)) for r, c in tiles]
         first = lax.ppermute(left_block, whole, mirror_pairs)
+        right_block = beside(project(flat, right_weight), narrow_mask)
         col_side, col_places = [right_block], [row_index]
         for step in range(1, row_count):
             col_side.append(lax.ppermute(right_block, "row", shifts(row_count, -step)))
@@ -318,12 +320,12 @@
                 )
         places = jnp.stack(row_places + col_places).astype(jnp.int32) * local_rows
     else:
-        left_wide = lax.all_gather(projected[0], plane, axis=1, tiled=True)
+        left_wide = lax.all_gather(project(flat, left_weight), plane, axis=1, tiled=True)
         mask_wide = lax.all_gather(narrow_mask, plane, axis=1, tiled=True)
         turn = lambda a: lax.all_to_all(a, "row", split_axis=1, concat_axis=0, tiled=True)
         gather = lambda a: lax.all_gather(a, "row", axis=0, tiled=True)
         row_side = [beside(turn(left_wide), turn(mask_wide))]
-        col_side = [beside(gather(projected[1]), gather(narrow_mask))]
+        col_side = [beside(gather(project(flat, right_weight)), gather(narrow_mask))]
         places = jnp.zeros((2,), jnp.int32)
 
     split = output_weight.reshape(width // turns, turns, width, channels)
@@ -335,14 +337,20 @@
     base = jnp.swapaxes(pair_input, 0, 1)
 
     sides = arrange(places, row_side, col_side, width, rows_dev, cols_dev)
-    run = lambda first, count, strip: tile_strips(
-        first, count, strip, *sides, base, weight, gate_up, down_weight
-    )
+
+    def run(first, count, strip, after=None):
+        row_channels = sides[0]
+        if after is not None:
+            row_channels, _ = lax.optimization_barrier((row_channels, after))
+        return tile_strips(
+            first, count, strip, row_channels, *sides[1:], base, weight, gate_up, down_weight
+        )
+
     ahead = lambda size: [(n, n + 1) for n in range(size - 1)]
     back = lambda size: [(n + 1, n) for n in range(size - 1)]
 
-    if square and cols_dev % (4 * unit) == 0 and x_count > 1:
-        part = cols_dev // 4
+    if square and cols_dev % (8 * unit) == 0 and x_count > 1:
+        part = cols_dev // 8
         host = lambda r, c: place_of(r, (r // core_count) * core_count + c % core_count)
         away = [(r, c) for r, c in tiles if r // core_count != c // core_count]
         near = [(r, c) for r, c in tiles if r // core_count == c // core_count]
@@ -350,19 +358,19 @@
         from_host = [(host(r, c), place_of(c, r)) for r, c in away]
         beside_pairs = [(place_of(r, c), place_of(c, r)) for r, c in near]
         send = lambda value, pairs: lax.ppermute(value, whole, pairs)
-        sent, mirrored = [], []
-        for n in range(2):
-            strip = run(n * part, part, part)
-            sent.append(strip)
-            mirrored.append(
-                [send(send(strip, to_host), from_host), send(strip, beside_pairs)]
-            )
-        strip = run(2 * part, 2 * part, 2 * part)
-        sent.append(strip)
-        turned = jnp.concatenate(sent, axis=0)
+        last = run(6 * part, 2 * part, 2 * part)
+        mirrored_last = send(last, mirror_pairs)
+        opening = run(0, 3 * part, 3 * part, last)
+        hosted = send(opening, to_host)
+        mirrored_near = send(opening, beside_pairs)
+        middle = run(3 * part, 3 * part, 3 * part, opening)
+        mirrored_middle = send(middle, mirror_pairs)
+        mirrored_away = send(hosted, from_host)
+        turned = jnp.concatenate([opening, middle, last], axis=0)
+        turned, _ = lax.optimization_barrier((turned, hosted))
         edges = jnp.stack([turned[0], turned[-1], turned[:, 0], turned[:, -1]])
         edges = send(edges, mirror_pairs)
-        mirrored.append([send(strip, mirror_pairs)])
+        mirrored = [[mirrored_away, mirrored_near], [mirrored_middle], [mirrored_last]]
     else:
         turned = run(0, cols_dev, math.gcd(unit, cols_dev))
         share = rows_dev // col_count
@@ -400,18 +408,30 @@
     last_side = (mean(turned[-1], edges[3]) * keep_i * keep_j[last_j]).astype(jnp.bfloat16)
     left = lax.ppermute(last_side, plane, ahead(col_count))
     right = lax.ppermute(first_side, plane, back(col_count))
-    border = lambda i, line: jnp.concatenate([left[i][None], line, right[i][None]], axis=0)
-    top = lax.ppermute(border(last_i, last_line), "row", ahead(row_count))
-    bottom = lax.ppermute(border(0, first_line), "row", back(row_count))
-    left = jnp.concatenate([top[:1], left, bottom[:1]], axis=0)
-    right = jnp.concatenate([top[-1:], right, bottom[-1:]], axis=0)
+    top = lax.ppermute(last_line, "row", ahead(row_count))
+    bottom = lax.ppermute(first_line, "row", back(row_count))
+
+    def corner(value, down, across):
+        pairs = [
+            (place_of(r, c), place_of(r + down, c + across))
+            for r, c in tiles
+            if 0 <= r + down < row_count and 0 <= c + across < col_count
+        ]
+        return lax.ppermute(jnp.broadcast_to(value, (16, channels)), whole, pairs)[:1]
+
+    top_left = corner(last_line[-1:], 1, 1)
+    top_right = corner(last_line[:1], 1, -1)
+    bottom_left = corner(first_line[-1:], -1, 1)
+    bottom_right = corner(first_line[:1], -1, -1)
+    left = jnp.concatenate([top_left, left, bottom_left], axis=0)
+    right = jnp.concatenate([top_right, right, bottom_right], axis=0)
     wide_valid = jnp.broadcast_to(keep_j, (cols_dev, channels))
     return convolve(
         pair_two,
         mirrored,
         valid_i,
         wide_valid,
-        [top[1:-1], bottom[1:-1], left, right],
+        [top, bottom, left, right],
         conv_weight,
     )
 

time: 124 us -> 137 us (1.10)
  the two profiles are of different devices: /device:TPU:21 before, /device:TPU:1 now
where the time goes in v3:
time: 137 us; the launch traced here: 135 us
  starting transfers between devices  56.9 us (42%)
  waiting for transfers between devices  33.5 us (24%)
  Pallas kernels  18.4 us (13%)
  local copies, waits for them, and re-layouts  16.1 us (12%)
  other arithmetic  7.26 us (5%)
  matrix products  1.56 us (1%)
    ppermute x4, waiting for transfers between devices, corner(): lax.ppermute(jnp.broadcast_to(value, (16, channels)), whole, pairs)[:1]  23.2 us
    ppermute x6, starting transfers between devices, on_device(): send = lambda value, pairs: lax.ppermute(value, whole, pairs)  18.9 us
    pallas_call x3, Pallas kernels, tile_strips(): pl.pallas_call(tile_kernel, grid=(count // strip,), in_specs=[fixed(row_s...  12.1 us
    unnamed x52, local copies, waits for them, and re-layouts  9.14 us
    ppermute x2, starting transfers between devices, on_device(): lax.ppermute(row_side[n], 'chan', shifts(core_count, -step))  8.08 us
    ppermute x4, starting transfers between devices, corner(): lax.ppermute(jnp.broadcast_to(value, (16, channels)), whole, pairs)[:1]  7.48 us
    ppermute x1, starting transfers between devices, on_device(): first = lax.ppermute(left_block, whole, mirror_pairs)  5.67 us
    ppermute x3, starting transfers between devices, on_device(): col_side.append(lax.ppermute(right_block, 'row', shifts(row_count, -step)))  4.66 us
  transfers between devices with their start and end apart: 21, of which 8 were waited for; matrix products, arithmetic and copies ran while one was open for 8% of the time, Pallas kernels for 3%

profile of v3, /device:TPU:1, one launch (start us, length us, event | category | flops | bytes accessed | tf_op | source)
XLA Modules:
  0.0 134.5 jit_solution(1719709027653969850)
XLA Ops:
  4.9 4.2 %collective-permute-start.4 = (bf16[32,2176]{1,0:T(8,128)(2,1)S(1)}, bf16[32,2176]{1,0:T(8,128)(2,1)S(1)}, u32[]{:S(2)}, u32[]{:S(2)}) collective-permute-start(bf16[32,2176]{1,0:T(8,128)(2,1)S(1)} %fusion.3.refs_4_), channel_id=1, source_target_pairs={{0,12},{4,0},{8,4},{12,8},{1,13},{5,1},{9,5},{13,9},{2,14},{6,2},{... | collective-permute-start | bytes 417800 | tf_op jit(solution)/shard_map/ppermute | solution.py:309
  9.6 5.7 %collective-permute-start = (bf16[32,2176]{1,0:T(8,128)(2,1)S(1)}, bf16[32,2176]{1,0:T(8,128)(2,1)S(1)}, u32[]{:S(2)}, u32[]{:S(2)}) collective-permute-start(bf16[32,2176]{1,0:T(8,128)(2,1)S(1)} %fusion.2), channel_id=1, source_target_pairs={{0,0},{1,4},{2,8},{3,12},{4,1},{5,5},{6,9},{7,13},{8,2},{9,6},{10,... | collective-permute-start | bytes 417800 | tf_op jit(solution)/shard_map/ppermute | solution.py:305
  17.7 2.5 %collective-permute-done.refs_0_ = bf16[32,2176]{1,0:T(8,128)(2,1)S(1)} collective-permute-done((bf16[32,2176]{1,0:T(8,128)(2,1)S(1)}, bf16[32,2176]{1,0:T(8,128)(2,1)S(1)}, u32[]{:S(2)}, u32[]{:S(2)}) %collective-permute-start) | collective-permute-done | bytes 139296 | tf_op jit(solution)/shard_map/ppermute | solution.py:305
  20.3 3.2 %collective-permute-start.1 = (bf16[32,2176]{1,0:T(8,128)(2,1)S(1)}, bf16[32,2176]{1,0:T(8,128)(2,1)S(1)}, u32[]{:S(2)}, u32[]{:S(2)}) collective-permute-start(bf16[32,2176]{1,0:T(8,128)(2,1)S(1)} %collective-permute-done.refs_0_), channel_id=1, source_target_pairs={{0,2},{2,0},{1,3},{3,1},{4,6},{6,4},{5,7},{7,5},{8,10},{10,8},{9,1... | collective-permute-start | bytes 417800 | tf_op jit(solution)/shard_map/ppermute | solution.py:313
  24.4 6.0 %collective-permute-start.2 = (bf16[32,2176]{1,0:T(8,128)(2,1)S(1)}, bf16[32,2176]{1,0:T(8,128)(2,1)S(1)}, u32[]{:S(2)}, u32[]{:S(2)}) collective-permute-start(bf16[32,2176]{1,0:T(8,128)(2,1)S(1)} %collective-permute-done.refs_0_), channel_id=1, source_target_pairs={{0,1},{1,0},{2,3},{3,2},{4,5},{5,4},{6,7},{7,6},{8,9},{9,8},{10,11... | collective-permute-start | bytes 417800 | tf_op jit(solution)/shard_map/ppermute | solution.py:317
  30.4 2.0 %collective-permute-start.3 = (bf16[32,2176]{1,0:T(8,128)(2,1)S(1)}, bf16[32,2176]{1,0:T(8,128)(2,1)S(1)}, u32[]{:S(2)}, u32[]{:S(2)}) collective-permute-start(bf16[32,2176]{1,0:T(8,128)(2,1)S(1)} %collective-permute-done.1.refs_1_), channel_id=1, source_target_pairs={{0,1},{1,0},{2,3},{3,2},{4,5},{5,4},{6,7},{7,6},{8,9},{9,8},{10,11... | collective-permute-start | bytes 417800 | tf_op jit(solution)/shard_map/ppermute | solution.py:317
  39.1 2.0 %shard_map.109 = (bf16[2048,128]{1,0:T(8,128)(2,1)S(1)}, bf16[4,128,2048]{2,1,0:T(8,128)(2,1)S(1)}, f32[8,64,128]{2,1,0:T(8,128)S(1)}) custom-call(s32[8]{0:T(128)S(1)} %broadcast_multiply_fusion.3.places, bf16[32,2176]{1,0:T(8,128)(2,1)S(1)} %copy-done.19, bf16[32,2176]{1,0:T(8,128)(2,1)S(1)} %collective-permute-done.1.refs_1_, ...), custom_call_target="tpu_custom_call" | custom-call | flops 1024 | bytes 1024 | tf_op jit(solution)/shard_map/pallas_call | solution.py:76
  41.2 3.1 %shard_map.110 = bf16[16,64,128]{2,1,0:T(8,128)(2,1)S(1)} custom-call(bf16[2048,128]{1,0:T(8,128)(2,1)S(1)} %get-tuple-element.19.row_side, bf16[4,128,2048]{2,1,0:T(8,128)(2,1)S(1)} %get-tuple-element.16.lane_side, f32[8,64,128]{2,1,0:T(8,128)S(1)} %get-tuple-element.17.scale, bf16[64,64,128]{2,1,0:T(8,128)(2,1)S(1)} %bitcast.75, ...), custom_call_target="tpu_custom_call" | custom-call | flops 1024 | bytes 1024 | tf_op jit(solution)/shard_map/pallas_call | solution.py:161
  44.3 4.8 %shard_map.111 = bf16[24,64,128]{2,1,0:T(8,128)(2,1)} custom-call(bf16[2048,128]{1,0:T(8,128)(2,1)S(1)} %get-tuple-element.19.row_side, bf16[4,128,2048]{2,1,0:T(8,128)(2,1)S(1)} %get-tuple-element.16.lane_side, f32[8,64,128]{2,1,0:T(8,128)S(1)} %get-tuple-element.17.scale, bf16[64,64,128]{2,1,0:T(8,128)(2,1)S(1)} %bitcast.76, ...), custom_call_target="tpu_custom_call" | custom-call | flops 1024 | bytes 1024 | tf_op jit(solution)/shard_map/pallas_call | solution.py:161
  54.8 4.2 %shard_map.112 = bf16[24,64,128]{2,1,0:T(8,128)(2,1)S(1)} custom-call(bf16[2048,128]{1,0:T(8,128)(2,1)S(1)} %get-tuple-element.19.row_side, bf16[4,128,2048]{2,1,0:T(8,128)(2,1)S(1)} %get-tuple-element.16.lane_side, f32[8,64,128]{2,1,0:T(8,128)S(1)} %copy-done.6, bf16[64,64,128]{2,1,0:T(8,128)(2,1)S(1)} %bitcast.77, bf16[4,1024,128]{2,1,0:T(8,128)(2,1)S(1)} %copy-done.4, ...), custom_call_target="tpu_custom_call" | custom-call | flops 1024 | bytes 1024 | tf_op jit(solution)/shard_map/pallas_call | solution.py:161
  62.9 3.1 %collective-permute-start.12 = (bf16[4,64,128]{2,1,0:T(8,128)(2,1)S(1)}, bf16[4,64,128]{2,1,0:T(8,128)(2,1)S(1)}, u32[]{:S(2)}, u32[]{:S(2)}) collective-permute-start(bf16[4,64,128]{2,1,0:T(8,128)(2,1)S(1)} %pad_maximum_fusion.6), channel_id=1, source_target_pairs={{0,0},{1,4},{2,8},{3,12},{4,1},{5,5},{6,9},{7,13},{8,2},{9,6},{10,... | collective-permute-start | bytes 196616 | tf_op jit(solution)/shard_map/ppermute | solution.py:360
  66.6 2.5 %collective-permute-start.10 = (bf16[24,64,128]{2,1,0:T(8,128)(2,1)S(1)}, bf16[24,64,128]{2,1,0:T(8,128)(2,1)S(1)}, u32[]{:S(2)}, u32[]{:S(2)}) collective-permute-start(bf16[24,64,128]{2,1,0:T(8,128)(2,1)S(1)} %shard_map.112), channel_id=1, source_target_pairs={{0,0},{1,4},{2,8},{3,12},{4,1},{5,5},{6,9},{7,13},{8,2},{9,6},{10,... | collective-permute-start | bytes 1179656 | tf_op jit(solution)/shard_map/ppermute | solution.py:360
  69.1 3.1 %collective-permute-start.9 = (bf16[24,64,128]{2,1,0:T(8,128)(2,1)}, bf16[24,64,128]{2,1,0:T(8,128)(2,1)S(1)}, u32[]{:S(2)}, u32[]{:S(2)}) collective-permute-start(bf16[24,64,128]{2,1,0:T(8,128)(2,1)} %shard_map.111), channel_id=1, source_target_pairs={{0,0},{1,4},{4,1},{5,5},{10,10},{11,14},{14,11},{15,15},{16,16},{1... | collective-permute-start | bytes 1179656 | tf_op jit(solution)/shard_map/ppermute | solution.py:360
  72.1 2.5 %collective-permute-start.11 = (bf16[16,64,128]{2,1,0:T(8,128)(2,1)S(1)}, bf16[16,64,128]{2,1,0:T(8,128)(2,1)S(1)}, u32[]{:S(2)}, u32[]{:S(2)}) collective-permute-start(bf16[16,64,128]{2,1,0:T(8,128)(2,1)S(1)} %copy-done.9), channel_id=1, source_target_pairs={{0,0},{1,4},{2,8},{3,12},{4,1},{5,5},{6,9},{7,13},{8,2},{9,6},{10,... | collective-permute-start | bytes 786440 | tf_op jit(solution)/shard_map/ppermute | solution.py:360
  74.6 6.3 %collective-permute-start.8 = (bf16[24,64,128]{2,1,0:T(8,128)(2,1)}, bf16[24,64,128]{2,1,0:T(8,128)(2,1)S(1)}, u32[]{:S(2)}, u32[]{:S(2)}) collective-permute-start(bf16[24,64,128]{2,1,0:T(8,128)(2,1)} %collective-permute-done.7), channel_id=1, source_target_pairs={{0,8},{1,12},{4,9},{5,13},{10,2},{11,6},{14,3},{15,7},{16,24},{17,... | collective-permute-start | bytes 1179656 | tf_op jit(solution)/shard_map/ppermute | solution.py:360
  81.0 2.5 %fusion.11 = (bf16[64,128]{1,0:T(8,128)(2,1)S(1)}, bf16[64,128]{1,0:T(8,128)(2,1)S(1)}, bf16[64,128]{1,0:T(8,128)(2,1)S(1)}, bf16[64,128]{1,0:T(8,128)(2,1)S(1)}) fusion(bf16[4,64,128]{2,1,0:T(8,128)(2,1)S(1)} %collective-permute-done.12, f32[]{:T(128)} %bitcast.31, f32[64]{0:T(128)S(1)} %get-tuple-element.45, bf16[64,64,128]{2,1,0:T(8,128)(2,1)S(1)} %copy.30, ...), kind=kLoop, calls=%fused_computation.27 | loop fusion | flops 196608 | bytes 197136 | tf_op jit(solution)/shard_map/convert_element_type | solution.py:407
  84.8 4.6 %collective-permute-done.18 = bf16[16,128]{1,0:T(8,128)(2,1)S(1)} collective-permute-done((bf16[16,128]{1,0:T(8,128)(2,1)S(1)}, bf16[16,128]{1,0:T(8,128)(2,1)S(1)}, u32[]{:S(2)}, u32[]{:S(2)}) %collective-permute-start.18) | collective-permute-done | bytes 4128 | tf_op jit(solution)/shard_map/ppermute | solution.py:420
  90.7 13.2 %collective-permute-done.20 = bf16[16,128]{1,0:T(8,128)(2,1)S(1)} collective-permute-done((bf16[16,128]{1,0:T(8,128)(2,1)S(1)}, bf16[16,128]{1,0:T(8,128)(2,1)S(1)}, u32[]{:S(2)}, u32[]{:S(2)}) %collective-permute-start.20) | collective-permute-done | bytes 4128 | tf_op jit(solution)/shard_map/ppermute | solution.py:420
  104.0 3.6 %collective-permute-start.15 = (bf16[16,128]{1,0:T(8,128)(2,1)S(1)}, bf16[16,128]{1,0:T(8,128)(2,1)S(1)}, u32[]{:S(2)}, u32[]{:S(2)}) collective-permute-start(bf16[16,128]{1,0:T(8,128)(2,1)S(1)} %broadcast_in_dim.39), channel_id=1, source_target_pairs={{0,5},{1,6},{2,7},{4,9},{5,10},{6,11},{8,13},{9,14},{10,15},{16,21... | collective-permute-start | bytes 12296 | tf_op jit(solution)/shard_map/ppermute | solution.py:420
  109.6 4.6 %collective-permute-done.17 = bf16[16,128]{1,0:T(8,128)(2,1)S(1)} collective-permute-done((bf16[16,128]{1,0:T(8,128)(2,1)S(1)}, bf16[16,128]{1,0:T(8,128)(2,1)S(1)}, u32[]{:S(2)}, u32[]{:S(2)}) %collective-permute-start.17) | collective-permute-done | bytes 4128 | tf_op jit(solution)/shard_map/ppermute | solution.py:420
  116.6 2.8 %collective-permute-done.19 = bf16[64,128]{1,0:T(8,128)(2,1)S(1)} collective-permute-done((bf16[64,128]{1,0:T(8,128)(2,1)S(1)}, bf16[64,128]{1,0:T(8,128)(2,1)S(1)}, u32[]{:S(2)}, u32[]{:S(2)}) %collective-permute-start.19) | collective-permute-done | bytes 16416 | tf_op jit(solution)/shard_map/ppermute | solution.py:410
  121.3 3.8 %collective-permute-start.13 = (bf16[64,128]{1,0:T(8,128)(2,1)S(1)}, bf16[64,128]{1,0:T(8,128)(2,1)S(1)}, u32[]{:S(2)}, u32[]{:S(2)}) collective-permute-start(bf16[64,128]{1,0:T(8,128)(2,1)S(1)} %get-tuple-element.37), channel_id=1, source_target_pairs={{0,4},{4,8},{8,12},{1,5},{5,9},{9,13},{2,6},{6,10},{10,14},{3,7},{... | collective-permute-start | bytes 49160 | tf_op jit(solution)/shard_map/ppermute | solution.py:411
  126.5 3.8 %collective-permute-done.14.refs_6_ = bf16[64,128]{1,0:T(8,128)(2,1)S(1)} collective-permute-done((bf16[64,128]{1,0:T(8,128)(2,1)S(1)}, bf16[64,128]{1,0:T(8,128)(2,1)S(1)}, u32[]{:S(2)}, u32[]{:S(2)}) %collective-permute-start.14) | collective-permute-done | bytes 16416 | tf_op jit(solution)/shard_map/ppermute | solution.py:412
  130.3 4.2 %shard_map.113 = bf16[64,64,128]{2,1,0:T(8,128)(2,1)} custom-call(s32[64]{0:T(128)S(1)} %get-tuple-element.46.valid_i, bf16[64,64,128]{2,1,0:T(8,128)(2,1)S(1)} %bitcast.78, bf16[24,64,128]{2,1,0:T(8,128)(2,1)S(1)} %collective-permute-done.8.refs_0_, bf16[24,64,128]{2,1,0:T(8,128)(2,1)S(1)} %collective-permute-done.9.refs_1_, ...), custom_call_target="tpu_custom_call" | custom-call | flops 1207959552 | bytes 3145728 | tf_op jit(solution)/shard_map/pallas_call | solution.py:239
  (125 shorter events, 35.3 us)
Async XLA Ops:
  4.9 29.3 %copy-start.10 = (bf16[32,2176]{1,0:T(8,128)(2,1)}, bf16[32,2176]{1,0:T(8,128)(2,1)S(1)}, u32[]{:S(2)}) copy-start(bf16[32,2176]{1,0:T(8,128)(2,1)S(1)} %fusion.3.refs_4_) | copy-start | bytes 417796
  4.9 28.6 %copy-start.21 = (bf16[64,64,128]{2,1,0:T(8,128)(2,1)S(1)}, bf16[64,64,128]{2,1,0:T(8,128)(2,1)}, u32[]{:S(2)}) copy-start(bf16[64,64,128]{2,1,0:T(8,128)(2,1)} %param.11) | copy-start | bytes 3145732
  4.9 29.5 %collective-permute-start.4 = (bf16[32,2176]{1,0:T(8,128)(2,1)S(1)}, bf16[32,2176]{1,0:T(8,128)(2,1)S(1)}, u32[]{:S(2)}, u32[]{:S(2)}) collective-permute-start(bf16[32,2176]{1,0:T(8,128)(2,1)S(1)} %fusion.3.refs_4_), channel_id=1, source_target_pairs={{0,12},{4,0},{8,4},{12,8},{1,13},{5,1},{9,5},{13,9},{2,14},{6,2},{... | collective-permute-start | bytes 417800 | tf_op jit(solution)/shard_map/ppermute | solution.py:309
  9.1 25.9 %collective-permute-start.5 = (bf16[32,2176]{1,0:T(8,128)(2,1)S(1)}, bf16[32,2176]{1,0:T(8,128)(2,1)S(1)}, u32[]{:S(2)}, u32[]{:S(2)}) collective-permute-start(bf16[32,2176]{1,0:T(8,128)(2,1)S(1)} %fusion.3.refs_4_), channel_id=1, source_target_pairs={{0,8},{4,12},{8,0},{12,4},{1,9},{5,13},{9,1},{13,5},{2,10},{6,14},... | collective-permute-start | bytes 417800 | tf_op jit(solution)/shard_map/ppermute | solution.py:309
  9.1 26.6 %collective-permute-start.6 = (bf16[32,2176]{1,0:T(8,128)(2,1)S(1)}, bf16[32,2176]{1,0:T(8,128)(2,1)S(1)}, u32[]{:S(2)}, u32[]{:S(2)}) collective-permute-start(bf16[32,2176]{1,0:T(8,128)(2,1)S(1)} %fusion.3.refs_4_), channel_id=1, source_target_pairs={{0,4},{4,8},{8,12},{12,0},{1,5},{5,9},{9,13},{13,1},{2,6},{6,10},{... | collective-permute-start | bytes 417800 | tf_op jit(solution)/shard_map/ppermute | solution.py:309
  9.6 10.7 %collective-permute-start = (bf16[32,2176]{1,0:T(8,128)(2,1)S(1)}, bf16[32,2176]{1,0:T(8,128)(2,1)S(1)}, u32[]{:S(2)}, u32[]{:S(2)}) collective-permute-start(bf16[32,2176]{1,0:T(8,128)(2,1)S(1)} %fusion.2), channel_id=1, source_target_pairs={{0,0},{1,4},{2,8},{3,12},{4,1},{5,5},{6,9},{7,13},{8,2},{9,6},{10,... | collective-permute-start | bytes 417800 | tf_op jit(solution)/shard_map/ppermute | solution.py:305
  20.3 10.2 %collective-permute-start.1 = (bf16[32,2176]{1,0:T(8,128)(2,1)S(1)}, bf16[32,2176]{1,0:T(8,128)(2,1)S(1)}, u32[]{:S(2)}, u32[]{:S(2)}) collective-permute-start(bf16[32,2176]{1,0:T(8,128)(2,1)S(1)} %collective-permute-done.refs_0_), channel_id=1, source_target_pairs={{0,2},{2,0},{1,3},{3,1},{4,6},{6,4},{5,7},{7,5},{8,10},{10,8},{9,1... | collective-permute-start | bytes 417800 | tf_op jit(solution)/shard_map/ppermute | solution.py:313
  24.4 12.0 %collective-permute-start.2 = (bf16[32,2176]{1,0:T(8,128)(2,1)S(1)}, bf16[32,2176]{1,0:T(8,128)(2,1)S(1)}, u32[]{:S(2)}, u32[]{:S(2)}) collective-permute-start(bf16[32,2176]{1,0:T(8,128)(2,1)S(1)} %collective-permute-done.refs_0_), channel_id=1, source_target_pairs={{0,1},{1,0},{2,3},{3,2},{4,5},{5,4},{6,7},{7,6},{8,9},{9,8},{10,11... | collective-permute-start | bytes 417800 | tf_op jit(solution)/shard_map/ppermute | solution.py:317
  30.4 5.9 %collective-permute-start.3 = (bf16[32,2176]{1,0:T(8,128)(2,1)S(1)}, bf16[32,2176]{1,0:T(8,128)(2,1)S(1)}, u32[]{:S(2)}, u32[]{:S(2)}) collective-permute-start(bf16[32,2176]{1,0:T(8,128)(2,1)S(1)} %collective-permute-done.1.refs_1_), channel_id=1, source_target_pairs={{0,1},{1,0},{2,3},{3,2},{4,5},{5,4},{6,7},{7,6},{8,9},{9,8},{10,11... | collective-permute-start | bytes 417800 | tf_op jit(solution)/shard_map/ppermute | solution.py:317
  49.2 12.9 %collective-permute-start.7 = (bf16[24,64,128]{2,1,0:T(8,128)(2,1)}, bf16[24,64,128]{2,1,0:T(8,128)(2,1)}, u32[]{:S(2)}, u32[]{:S(2)}) collective-permute-start(bf16[24,64,128]{2,1,0:T(8,128)(2,1)} %shard_map.111), channel_id=1, source_target_pairs={{2,0},{3,1},{6,4},{7,5},{8,10},{9,11},{12,14},{13,15},{18,16},{19,... | collective-permute-start | bytes 1179656 | tf_op jit(solution)/shard_map/ppermute | solution.py:360
  60.7 55.5 %copy-start.22 = (bf16[3,3,128,128]{3,2,1,0:T(8,128)(2,1)S(1)}, bf16[3,3,128,128]{3,2,1,0:T(8,128)(2,1)}, u32[]{:S(2)}) copy-start(bf16[3,3,128,128]{3,2,1,0:T(8,128)(2,1)} %param.21) | copy-start | bytes 884740
  62.9 18.1 %collective-permute-start.12 = (bf16[4,64,128]{2,1,0:T(8,128)(2,1)S(1)}, bf16[4,64,128]{2,1,0:T(8,128)(2,1)S(1)}, u32[]{:S(2)}, u32[]{:S(2)}) collective-permute-start(bf16[4,64,128]{2,1,0:T(8,128)(2,1)S(1)} %pad_maximum_fusion.6), channel_id=1, source_target_pairs={{0,0},{1,4},{2,8},{3,12},{4,1},{5,5},{6,9},{7,13},{8,2},{9,6},{10,... | collective-permute-start | bytes 196616 | tf_op jit(solution)/shard_map/ppermute | solution.py:360
  66.6 59.9 %collective-permute-start.10 = (bf16[24,64,128]{2,1,0:T(8,128)(2,1)S(1)}, bf16[24,64,128]{2,1,0:T(8,128)(2,1)S(1)}, u32[]{:S(2)}, u32[]{:S(2)}) collective-permute-start(bf16[24,64,128]{2,1,0:T(8,128)(2,1)S(1)} %shard_map.112), channel_id=1, source_target_pairs={{0,0},{1,4},{2,8},{3,12},{4,1},{5,5},{6,9},{7,13},{8,2},{9,6},{10,... | collective-permute-start | bytes 1179656 | tf_op jit(solution)/shard_map/ppermute | solution.py:360
  69.1 57.4 %collective-permute-start.9 = (bf16[24,64,128]{2,1,0:T(8,128)(2,1)}, bf16[24,64,128]{2,1,0:T(8,128)(2,1)S(1)}, u32[]{:S(2)}, u32[]{:S(2)}) collective-permute-start(bf16[24,64,128]{2,1,0:T(8,128)(2,1)} %shard_map.111), channel_id=1, source_target_pairs={{0,0},{1,4},{4,1},{5,5},{10,10},{11,14},{14,11},{15,15},{16,16},{1... | collective-permute-start | bytes 1179656 | tf_op jit(solution)/shard_map/ppermute | solution.py:360
  72.1 49.2 %collective-permute-start.11 = (bf16[16,64,128]{2,1,0:T(8,128)(2,1)S(1)}, bf16[16,64,128]{2,1,0:T(8,128)(2,1)S(1)}, u32[]{:S(2)}, u32[]{:S(2)}) collective-permute-start(bf16[16,64,128]{2,1,0:T(8,128)(2,1)S(1)} %copy-done.9), channel_id=1, source_target_pairs={{0,0},{1,4},{2,8},{3,12},{4,1},{5,5},{6,9},{7,13},{8,2},{9,6},{10,... | collective-permute-start | bytes 786440 | tf_op jit(solution)/shard_map/ppermute | solution.py:360
  74.6 55.6 %collective-permute-start.8 = (bf16[24,64,128]{2,1,0:T(8,128)(2,1)}, bf16[24,64,128]{2,1,0:T(8,128)(2,1)S(1)}, u32[]{:S(2)}, u32[]{:S(2)}) collective-permute-start(bf16[24,64,128]{2,1,0:T(8,128)(2,1)} %collective-permute-done.7), channel_id=1, source_target_pairs={{0,8},{1,12},{4,9},{5,13},{10,2},{11,6},{14,3},{15,7},{16,24},{17,... | collective-permute-start | bytes 1179656 | tf_op jit(solution)/shard_map/ppermute | solution.py:360
  83.5 5.9 %collective-permute-start.18 = (bf16[16,128]{1,0:T(8,128)(2,1)S(1)}, bf16[16,128]{1,0:T(8,128)(2,1)S(1)}, u32[]{:S(2)}, u32[]{:S(2)}) collective-permute-start(bf16[16,128]{1,0:T(8,128)(2,1)S(1)} %broadcast_in_dim.43), channel_id=1, source_target_pairs={{1,4},{2,5},{3,6},{5,8},{6,9},{7,10},{9,12},{10,13},{11,14},{17,20... | collective-permute-start | bytes 12296 | tf_op jit(solution)/shard_map/ppermute | solution.py:420
  89.4 14.5 %collective-permute-start.20 = (bf16[16,128]{1,0:T(8,128)(2,1)S(1)}, bf16[16,128]{1,0:T(8,128)(2,1)S(1)}, u32[]{:S(2)}, u32[]{:S(2)}) collective-permute-start(bf16[16,128]{1,0:T(8,128)(2,1)S(1)} %broadcast_in_dim.45), channel_id=1, source_target_pairs={{5,0},{6,1},{7,2},{9,4},{10,5},{11,6},{13,8},{14,9},{15,10},{21,16... | collective-permute-start | bytes 12296 | tf_op jit(solution)/shard_map/ppermute | solution.py:420
  104.0 4.4 %collective-permute-start.15 = (bf16[16,128]{1,0:T(8,128)(2,1)S(1)}, bf16[16,128]{1,0:T(8,128)(2,1)S(1)}, u32[]{:S(2)}, u32[]{:S(2)}) collective-permute-start(bf16[16,128]{1,0:T(8,128)(2,1)S(1)} %broadcast_in_dim.39), channel_id=1, source_target_pairs={{0,5},{1,6},{2,7},{4,9},{5,10},{6,11},{8,13},{9,14},{10,15},{16,21... | collective-permute-start | bytes 12296 | tf_op jit(solution)/shard_map/ppermute | solution.py:420
  108.3 5.9 %collective-permute-start.17 = (bf16[16,128]{1,0:T(8,128)(2,1)S(1)}, bf16[16,128]{1,0:T(8,128)(2,1)S(1)}, u32[]{:S(2)}, u32[]{:S(2)}) collective-permute-start(bf16[16,128]{1,0:T(8,128)(2,1)S(1)} %broadcast_in_dim.41), channel_id=1, source_target_pairs={{4,1},{5,2},{6,3},{8,5},{9,6},{10,7},{12,9},{13,10},{14,11},{20,17... | collective-permute-start | bytes 12296 | tf_op jit(solution)/shard_map/ppermute | solution.py:420
  114.3 5.0 %collective-permute-start.19 = (bf16[64,128]{1,0:T(8,128)(2,1)S(1)}, bf16[64,128]{1,0:T(8,128)(2,1)S(1)}, u32[]{:S(2)}, u32[]{:S(2)}) collective-permute-start(bf16[64,128]{1,0:T(8,128)(2,1)S(1)} %get-tuple-element.35), channel_id=1, source_target_pairs={{1,0},{2,1},{3,2},{5,4},{6,5},{7,6},{9,8},{10,9},{11,10},{13,12},{... | collective-permute-start | bytes 49160 | tf_op jit(solution)/shard_map/ppermute | solution.py:410
  119.3 5.8 %collective-permute-start.16 = (bf16[64,128]{1,0:T(8,128)(2,1)S(1)}, bf16[64,128]{1,0:T(8,128)(2,1)S(1)}, u32[]{:S(2)}, u32[]{:S(2)}) collective-permute-start(bf16[64,128]{1,0:T(8,128)(2,1)S(1)} %get-tuple-element.36), channel_id=1, source_target_pairs={{0,1},{1,2},{2,3},{4,5},{5,6},{6,7},{8,9},{9,10},{10,11},{12,13},{... | collective-permute-start | bytes 49160 | tf_op jit(solution)/shard_map/ppermute | solution.py:409
  121.3 5.2 %collective-permute-start.13 = (bf16[64,128]{1,0:T(8,128)(2,1)S(1)}, bf16[64,128]{1,0:T(8,128)(2,1)S(1)}, u32[]{:S(2)}, u32[]{:S(2)}) collective-permute-start(bf16[64,128]{1,0:T(8,128)(2,1)S(1)} %get-tuple-element.37), channel_id=1, source_target_pairs={{0,4},{4,8},{8,12},{1,5},{5,9},{9,13},{2,6},{6,10},{10,14},{3,7},{... | collective-permute-start | bytes 49160 | tf_op jit(solution)/shard_map/ppermute | solution.py:411
  125.1 5.1 %collective-permute-start.14 = (bf16[64,128]{1,0:T(8,128)(2,1)S(1)}, bf16[64,128]{1,0:T(8,128)(2,1)S(1)}, u32[]{:S(2)}, u32[]{:S(2)}) collective-permute-start(bf16[64,128]{1,0:T(8,128)(2,1)S(1)} %get-tuple-element.38), channel_id=1, source_target_pairs={{4,0},{8,4},{12,8},{5,1},{9,5},{13,9},{6,2},{10,6},{14,10},{7,3},{... | collective-permute-start | bytes 49160 | tf_op jit(solution)/shard_map/ppermute | solution.py:412
  (22 other events, 89.2 us)

commit v4 on v3

--- a/solution.py
+++ b/solution.py
@@ -367,9 +367,6 @@
         mirrored_middle = send(middle, mirror_pairs)
         mirrored_away = send(hosted, from_host)
         turned = jnp.concatenate([opening, middle, last], axis=0)
-        turned, _ = lax.optimization_barrier((turned, hosted))
-        edges = jnp.stack([turned[0], turned[-1], turned[:, 0], turned[:, -1]])
-        edges = send(edges, mirror_pairs)
         mirrored = [[mirrored_away, mirrored_near], [mirrored_middle], [mirrored_last]]
     else:
         turned = run(0, cols_dev, math.gcd(unit, cols_dev))
@@ -393,45 +390,37 @@
             .reshape(rows_dev, cols_dev, channels)
         )
         mirrored = [[full]]
-        edges = (full[0], full[-1], full[:, 0], full[:, -1])
 
     pair_two = jnp.swapaxes(turned, 0, 1)
     valid_i = lax.dynamic_slice_in_dim(token_valid, row_index * rows_dev, rows_dev)
     valid_j = lax.dynamic_slice_in_dim(token_valid, col_index * cols_dev, cols_dev)
     keep_i = valid_i.astype(jnp.float32)[:, None]
     keep_j = valid_j.astype(jnp.float32)[:, None]
-    mean = lambda a, b: (a.astype(jnp.float32) + b.astype(jnp.float32)) * 0.5
     last_i, last_j = rows_dev - 1, cols_dev - 1
-    first_line = (mean(turned[:, 0], edges[0]) * keep_j * keep_i[0]).astype(jnp.bfloat16)
-    last_line = (mean(turned[:, -1], edges[1]) * keep_j * keep_i[last_i]).astype(jnp.bfloat16)
-    first_side = (mean(turned[0], edges[2]) * keep_i * keep_j[0]).astype(jnp.bfloat16)
-    last_side = (mean(turned[-1], edges[3]) * keep_i * keep_j[last_j]).astype(jnp.bfloat16)
+    parts = [[a.astype(jnp.float32) for a in part] for part in mirrored]
+    along = lambda pick: jnp.concatenate([sum(pick(a) for a in part) for part in parts], axis=0)
+
+    def edge(own, other, keep):
+        return ((own.astype(jnp.float32) + other) * 0.5 * keep).astype(jnp.bfloat16)
+
+    first_line = edge(turned[:, 0], sum(a[0] for a in parts[0]), keep_j * keep_i[0])
+    last_line = edge(turned[:, -1], sum(a[-1] for a in parts[-1]), keep_j * keep_i[last_i])
+    first_side = edge(turned[0], along(lambda a: a[:, 0]), keep_i * keep_j[0])
+    last_side = edge(turned[-1], along(lambda a: a[:, -1]), keep_i * keep_j[last_j])
     left = lax.ppermute(last_side, plane, ahead(col_count))
     right = lax.ppermute(first_side, plane, back(col_count))
-    top = lax.ppermute(last_line, "row", ahead(row_count))
-    bottom = lax.ppermute(first_line, "row", back(row_count))
-
-    def corner(value, down, across):
-        pairs = [
-            (place_of(r, c), place_of(r + down, c + across))
-            for r, c in tiles
-            if 0 <= r + down < row_count and 0 <= c + across < col_count
-        ]
-        return lax.ppermute(jnp.broadcast_to(value, (16, channels)), whole, pairs)[:1]
-
-    top_left = corner(last_line[-1:], 1, 1)
-    top_right = corner(last_line[:1], 1, -1)
-    bottom_left = corner(first_line[-1:], -1, 1)
-    bottom_right = corner(first_line[:1], -1, -1)
-    left = jnp.concatenate([top_left, left, bottom_left], axis=0)
-    right = jnp.concatenate([top_right, right, bottom_right], axis=0)
+    border = lambda i, line: jnp.concatenate([left[i][None], line, right[i][None]], axis=0)
+    top = lax.ppermute(border(last_i, last_line), "row", ahead(row_count))
+    bottom = lax.ppermute(border(0, first_line), "row", back(row_count))
+    left = jnp.concatenate([top[:1], left, bottom[:1]], axis=0)
+    right = jnp.concatenate([top[-1:], right, bottom[-1:]], axis=0)
     wide_valid = jnp.broadcast_to(keep_j, (cols_dev, channels))
     return convolve(
         pair_two,
         mirrored,
         valid_i,
         wide_valid,
-        [top, bottom, left, right],
+        [top[1:-1], bottom[1:-1], left, right],
         conv_weight,
     )
 

time: 137 us -> 113 us (0.82)
  the two profiles are of different devices: /device:TPU:1 before, /device:TPU:30 now
where the time goes in v4:
time: 113 us; the launch traced here: 112 us
  starting transfers between devices  55.6 us (49%)
  waiting for transfers between devices  21.5 us (19%)
  Pallas kernels  18.1 us (16%)
  other arithmetic  7.5 us (7%)
  local copies, waits for them, and re-layouts  7.4 us (7%)
  matrix products  1.55 us (1%)
    ppermute x1, starting transfers between devices, on_device(): right = lax.ppermute(first_side, plane, back(col_count))  20.4 us
    ppermute x5, starting transfers between devices, on_device(): send = lambda value, pairs: lax.ppermute(value, whole, pairs)  15.8 us
    pallas_call x3, Pallas kernels, tile_strips(): pl.pallas_call(tile_kernel, grid=(count // strip,), in_specs=[fixed(row_s...  11.8 us
    ppermute x5, waiting for transfers between devices, on_device(): send = lambda value, pairs: lax.ppermute(value, whole, pairs)  8.8 us
    ppermute x2, starting transfers between devices, on_device(): lax.ppermute(row_side[n], 'chan', shifts(core_count, -step))  5.79 us
    ppermute x1, waiting for transfers between devices, on_device(): first = lax.ppermute(left_block, whole, mirror_pairs)  5.39 us
    pallas_call x1, Pallas kernels, convolve(): pl.pallas_call(functools.partial(conv_kernel, parts=[tuple(range(len(part...  4.28 us
    ppermute x1, waiting for transfers between devices, on_device(): top = lax.ppermute(border(last_i, last_line), 'row', ahead(row_count))  4.21 us
  transfers between devices with their start and end apart: 16, of which 6 were waited for; matrix products, arithmetic and copies ran while one was open for 9% of the time, Pallas kernels for 0%

profile of v4, /device:TPU:30, one launch (start us, length us, event | category | flops | bytes accessed | tf_op | source)
XLA Modules:
  0.0 112.2 jit_solution(15842307322519947770)
XLA Ops:
  1.1 1.3 %fusion = bf16[32,64,32]{1,2,0:T(8,128)(2,1)S(1)} fusion(bf16[32,64,64]{2,1,0:T(8,128)(2,1)S(1)} %copy-done, f32[32,64]{1,0:T(8,128)S(1)} %get-tuple-element.51, bf16[64,32]{0,1:T(8,128)(2,1)} %param.15), kind=kOutput, calls=%fused_computation.1 | convolution fusion | flops 8519680 | bytes 405504 | tf_op jit(solution)/shard_map/dot_general | solution.py:290
  6.4 3.0 %collective-permute-start.6 = (bf16[32,2176]{1,0:T(8,128)(2,1)S(1)}, bf16[32,2176]{1,0:T(8,128)(2,1)S(1)}, u32[]{:S(2)}, u32[]{:S(2)}) collective-permute-start(bf16[32,2176]{1,0:T(8,128)(2,1)S(1)} %fusion.3.refs_4_), channel_id=1, source_target_pairs={{0,4},{4,8},{8,12},{12,0},{1,5},{5,9},{9,13},{13,1},{2,6},{6,10},{... | collective-permute-start | bytes 417800 | tf_op jit(solution)/shard_map/ppermute | solution.py:309
  9.5 2.1 %collective-permute-start = (bf16[32,2176]{1,0:T(8,128)(2,1)}, bf16[32,2176]{1,0:T(8,128)(2,1)S(1)}, u32[]{:S(2)}, u32[]{:S(2)}) collective-permute-start(bf16[32,2176]{1,0:T(8,128)(2,1)} %fusion.2), channel_id=1, source_target_pairs={{0,0},{1,4},{2,8},{3,12},{4,1},{5,5},{6,9},{7,13},{8,2},{9,6},{10,... | collective-permute-start | bytes 417800 | tf_op jit(solution)/shard_map/ppermute | solution.py:305
  15.7 5.4 %collective-permute-done.refs_0_ = bf16[32,2176]{1,0:T(8,128)(2,1)S(1)} collective-permute-done((bf16[32,2176]{1,0:T(8,128)(2,1)}, bf16[32,2176]{1,0:T(8,128)(2,1)S(1)}, u32[]{:S(2)}, u32[]{:S(2)}) %collective-permute-start) | collective-permute-done | bytes 139296 | tf_op jit(solution)/shard_map/ppermute | solution.py:305
  21.1 1.3 %collective-permute-start.1 = (bf16[32,2176]{1,0:T(8,128)(2,1)S(1)}, bf16[32,2176]{1,0:T(8,128)(2,1)S(1)}, u32[]{:S(2)}, u32[]{:S(2)}) collective-permute-start(bf16[32,2176]{1,0:T(8,128)(2,1)S(1)} %collective-permute-done.refs_0_), channel_id=1, source_target_pairs={{0,2},{2,0},{1,3},{3,1},{4,6},{6,4},{5,7},{7,5},{8,10},{10,8},{9,1... | collective-permute-start | bytes 417800 | tf_op jit(solution)/shard_map/ppermute | solution.py:313
  23.8 4.9 %collective-permute-start.2 = (bf16[32,2176]{1,0:T(8,128)(2,1)S(1)}, bf16[32,2176]{1,0:T(8,128)(2,1)S(1)}, u32[]{:S(2)}, u32[]{:S(2)}) collective-permute-start(bf16[32,2176]{1,0:T(8,128)(2,1)S(1)} %collective-permute-done.refs_0_), channel_id=1, source_target_pairs={{0,1},{1,0},{2,3},{3,2},{4,5},{5,4},{6,7},{7,6},{8,9},{9,8},{10,11... | collective-permute-start | bytes 417800 | tf_op jit(solution)/shard_map/ppermute | solution.py:317
  31.1 2.0 %shard_map.109 = (bf16[2048,128]{1,0:T(8,128)(2,1)S(1)}, bf16[4,128,2048]{2,1,0:T(8,128)(2,1)S(1)}, f32[8,64,128]{2,1,0:T(8,128)S(1)}) custom-call(s32[8]{0:T(128)S(1)} %broadcast_multiply_fusion.1.places, bf16[32,2176]{1,0:T(8,128)(2,1)S(1)} %collective-permute-done.refs_0_, bf16[32,2176]{1,0:T(8,128)(2,1)S(1)} %collective-permute-done.1.refs_1_, ...), custom_call_target="tpu_custom_call" | custom-call | flops 1024 | bytes 1024 | tf_op jit(solution)/shard_map/pallas_call | solution.py:76
  33.1 3.2 %shard_map.110 = bf16[16,64,128]{2,1,0:T(8,128)(2,1)S(1)} custom-call(bf16[2048,128]{1,0:T(8,128)(2,1)S(1)} %get-tuple-element.18.row_side, bf16[4,128,2048]{2,1,0:T(8,128)(2,1)S(1)} %get-tuple-element.15.lane_side, f32[8,64,128]{2,1,0:T(8,128)S(1)} %get-tuple-element.16.scale, bf16[64,64,128]{2,1,0:T(8,128)(2,1)S(1)} %bitcast.69, ...), custom_call_target="tpu_custom_call" | custom-call | flops 1024 | bytes 1024 | tf_op jit(solution)/shard_map/pallas_call | solution.py:161
  36.4 4.1 %shard_map.111 = bf16[24,64,128]{2,1,0:T(8,128)(2,1)S(1)} custom-call(bf16[2048,128]{1,0:T(8,128)(2,1)S(1)} %get-tuple-element.18.row_side, bf16[4,128,2048]{2,1,0:T(8,128)(2,1)S(1)} %get-tuple-element.15.lane_side, f32[8,64,128]{2,1,0:T(8,128)S(1)} %get-tuple-element.16.scale, bf16[64,64,128]{2,1,0:T(8,128)(2,1)S(1)} %bitcast.70, ...), custom_call_target="tpu_custom_call" | custom-call | flops 1024 | bytes 1024 | tf_op jit(solution)/shard_map/pallas_call | solution.py:161
  40.8 4.5 %shard_map.112 = bf16[24,64,128]{2,1,0:T(8,128)(2,1)S(1)} custom-call(bf16[2048,128]{1,0:T(8,128)(2,1)S(1)} %get-tuple-element.18.row_side, bf16[4,128,2048]{2,1,0:T(8,128)(2,1)S(1)} %get-tuple-element.15.lane_side, f32[8,64,128]{2,1,0:T(8,128)S(1)} %get-tuple-element.16.scale, bf16[64,64,128]{2,1,0:T(8,128)(2,1)S(1)} %bitcast.71, ...), custom_call_target="tpu_custom_call" | custom-call | flops 1024 | bytes 1024 | tf_op jit(solution)/shard_map/pallas_call | solution.py:161
  45.9 1.3 %collective-permute-start.7 = (bf16[24,64,128]{2,0,1:T(8,128)(2,1)S(1)}, bf16[24,64,128]{2,0,1:T(8,128)(2,1)S(1)}, u32[]{:S(2)}, u32[]{:S(2)}) collective-permute-start(bf16[24,64,128]{2,0,1:T(8,128)(2,1)S(1)} %get-tuple-element.33), channel_id=1, source_target_pairs={{2,0},{3,1},{6,4},{7,5},{8,10},{9,11},{12,14},{13,15},{18,16},{19,... | collective-permute-start | bytes 1179656 | tf_op jit(solution)/shard_map/ppermute | solution.py:360
  47.2 3.0 %collective-permute-start.11 = (bf16[16,64,128]{2,0,1:T(8,128)(2,1)S(1)}, bf16[16,64,128]{2,0,1:T(8,128)(2,1)S(1)}, u32[]{:S(2)}, u32[]{:S(2)}) collective-permute-start(bf16[16,64,128]{2,0,1:T(8,128)(2,1)S(1)} %get-tuple-element.35), channel_id=1, source_target_pairs={{0,0},{1,4},{2,8},{3,12},{4,1},{5,5},{6,9},{7,13},{8,2},{9,6},{10,... | collective-permute-start | bytes 786440 | tf_op jit(solution)/shard_map/ppermute | solution.py:360
  50.2 1.2 %multiply_multiply_fusion.3 = (f32[64]{0:T(128)S(1)}, f32[64]{0:T(128)S(1)}) fusion(f32[]{:T(128)} %bitcast.21, s32[64]{0:T(128)S(1)} %get-tuple-element.22.valid_i, f32[]{:T(128)} %bitcast.29), kind=kLoop, calls=%fused_computation.51 | loop fusion | flops 320 | bytes 776 | tf_op jit(solution)/shard_map/mul | solution.py:404
  51.7 2.6 %collective-permute-start.9 = (bf16[24,64,128]{2,0,1:T(8,128)(2,1)S(1)}, bf16[24,64,128]{2,0,1:T(8,128)(2,1)S(1)}, u32[]{:S(2)}, u32[]{:S(2)}) collective-permute-start(bf16[24,64,128]{2,0,1:T(8,128)(2,1)S(1)} %get-tuple-element.33), channel_id=1, source_target_pairs={{0,0},{1,4},{4,1},{5,5},{10,10},{11,14},{14,11},{15,15},{16,16},{1... | collective-permute-start | bytes 1179656 | tf_op jit(solution)/shard_map/ppermute | solution.py:360
  54.3 3.0 %collective-permute-start.10 = (bf16[24,64,128]{2,0,1:T(8,128)(2,1)S(1)}, bf16[24,64,128]{2,0,1:T(8,128)(2,1)S(1)}, u32[]{:S(2)}, u32[]{:S(2)}) collective-permute-start(bf16[24,64,128]{2,0,1:T(8,128)(2,1)S(1)} %get-tuple-element.31), channel_id=1, source_target_pairs={{0,0},{1,4},{2,8},{3,12},{4,1},{5,5},{6,9},{7,13},{8,2},{9,6},{10,... | collective-permute-start | bytes 1179656 | tf_op jit(solution)/shard_map/ppermute | solution.py:360
  58.8 6.0 %collective-permute-start.8 = (bf16[24,64,128]{2,0,1:T(8,128)(2,1)S(1)}, bf16[24,64,128]{2,0,1:T(8,128)(2,1)S(1)}, u32[]{:S(2)}, u32[]{:S(2)}) collective-permute-start(bf16[24,64,128]{2,0,1:T(8,128)(2,1)S(1)} %collective-permute-done.7), channel_id=1, source_target_pairs={{0,8},{1,12},{4,9},{5,13},{10,2},{11,6},{14,3},{15,7},{16,24},{17,... | collective-permute-start | bytes 1179656 | tf_op jit(solution)/shard_map/ppermute | solution.py:360
  64.8 8.1 %collective-permute-done.10 = bf16[24,64,128]{2,0,1:T(8,128)(2,1)S(1)} collective-permute-done((bf16[24,64,128]{2,0,1:T(8,128)(2,1)S(1)}, bf16[24,64,128]{2,0,1:T(8,128)(2,1)S(1)}, u32[]{:S(2)}, u32[]{:S(2)}) %collective-permute-start.10) | collective-permute-done | bytes 393248 | tf_op jit(solution)/shard_map/ppermute | solution.py:360
  73.4 20.4 %collective-permute-start.13 = (bf16[64,128]{1,0:T(8,128)(2,1)S(1)}, bf16[64,128]{1,0:T(8,128)(2,1)S(1)}, u32[]{:S(2)}, u32[]{:S(2)}) collective-permute-start(bf16[64,128]{1,0:T(8,128)(2,1)S(1)} %fusion.7), channel_id=1, source_target_pairs={{1,0},{2,1},{3,2},{5,4},{6,5},{7,6},{9,8},{10,9},{11,10},{13,12},{... | collective-permute-start | bytes 49160 | tf_op jit(solution)/shard_map/ppermute | solution.py:411
  93.9 1.9 %collective-permute-start.12 = (bf16[64,128]{1,0:T(8,128)(2,1)S(1)}, bf16[64,128]{1,0:T(8,128)(2,1)S(1)}, u32[]{:S(2)}, u32[]{:S(2)}) collective-permute-start(bf16[64,128]{1,0:T(8,128)(2,1)S(1)} %fusion.5), channel_id=1, source_target_pairs={{0,1},{1,2},{2,3},{4,5},{5,6},{6,7},{8,9},{9,10},{10,11},{12,13},{... | collective-permute-start | bytes 49160 | tf_op jit(solution)/shard_map/ppermute | solution.py:410
  96.0 2.9 %collective-permute-done.12 = bf16[64,128]{1,0:T(8,128)(2,1)S(1)} collective-permute-done((bf16[64,128]{1,0:T(8,128)(2,1)S(1)}, bf16[64,128]{1,0:T(8,128)(2,1)S(1)}, u32[]{:S(2)}, u32[]{:S(2)}) %collective-permute-start.12) | collective-permute-done | bytes 16416 | tf_op jit(solution)/shard_map/ppermute | solution.py:410
  99.0 3.1 %collective-permute-start.15 = (bf16[66,128]{1,0:T(8,128)(2,1)S(1)}, bf16[66,128]{1,0:T(8,128)(2,1)S(1)}, u32[]{:S(2)}, u32[]{:S(2)}) collective-permute-start(bf16[66,128]{1,0:T(8,128)(2,1)S(1)} %pad_maximum_fusion.6), channel_id=1, source_target_pairs={{4,0},{8,4},{12,8},{5,1},{9,5},{13,9},{6,2},{10,6},{14,10},{7,3},{... | collective-permute-start | bytes 50696 | tf_op jit(solution)/shard_map/ppermute | solution.py:414
  102.2 1.3 %collective-permute-start.14 = (bf16[66,128]{1,0:T(8,128)(2,1)S(1)}, bf16[66,128]{1,0:T(8,128)(2,1)S(1)}, u32[]{:S(2)}, u32[]{:S(2)}) collective-permute-start(bf16[66,128]{1,0:T(8,128)(2,1)S(1)} %pad_maximum_fusion.5), channel_id=1, source_target_pairs={{0,4},{4,8},{8,12},{1,5},{5,9},{9,13},{2,6},{6,10},{10,14},{3,7},{... | collective-permute-start | bytes 50696 | tf_op jit(solution)/shard_map/ppermute | solution.py:413
  103.6 4.2 %collective-permute-done.14 = bf16[66,128]{1,0:T(8,128)(2,1)S(1)} collective-permute-done((bf16[66,128]{1,0:T(8,128)(2,1)S(1)}, bf16[66,128]{1,0:T(8,128)(2,1)S(1)}, u32[]{:S(2)}, u32[]{:S(2)}) %collective-permute-start.14) | collective-permute-done | bytes 16928 | tf_op jit(solution)/shard_map/ppermute | solution.py:413
  108.0 4.3 %shard_map.113 = bf16[64,64,128]{2,1,0:T(8,128)(2,1)} custom-call(s32[64]{0:T(128)S(1)} %get-tuple-element.22.valid_i, bf16[64,64,128]{2,1,0:T(8,128)(2,1)S(1)} %bitcast.73, bf16[24,64,128]{2,1,0:T(8,128)(2,1)S(1)} %copy.40.refs_0_, bf16[24,64,128]{2,1,0:T(8,128)(2,1)S(1)} %copy.41.refs_1_, bf16[24,64,128]{2,1,0:T(8,128)(2,1)S(1)} %copy.42.refs_2_, ...), custom_call_target="tpu_custom_call" | custom-call | flops 1207959552 | bytes 3145728 | tf_op jit(solution)/shard_map/pallas_call | solution.py:239
  (89 shorter events, 16.5 us)
Async XLA Ops:
  0.0 1.1 copy-start
  0.0 3.9 %copy-start.6 = (bf16[64,32]{0,1:T(8,128)(2,1)S(1)}, bf16[64,32]{0,1:T(8,128)(2,1)}, u32[]{:S(2)}) copy-start(bf16[64,32]{0,1:T(8,128)(2,1)} %param.16) | copy-start | bytes 12292
  4.2 7.4 %copy-start.2 = (bf16[1024,128]{1,0:T(8,128)(2,1)S(1)}, bf16[1024,128]{1,0:T(8,128)(2,1)}, u32[]{:S(2)}) copy-start(bf16[1024,128]{1,0:T(8,128)(2,1)} %param.17) | copy-start | bytes 786436
  5.0 8.1 %copy-start.5 = (bf16[128,512]{1,0:T(8,128)(2,1)S(1)}, bf16[128,512]{1,0:T(8,128)(2,1)}, u32[]{:S(2)}) copy-start(bf16[128,512]{1,0:T(8,128)(2,1)} %param.18) | copy-start | bytes 393220
  5.0 8.1 %copy-start.7 = (s32[256]{0:T(256)S(1)}, s32[256]{0:T(256)}, u32[]{:S(2)}) copy-start(s32[256]{0:T(256)} %param.14) | copy-start | bytes 3076
  5.6 24.6 %copy-start.3 = (bf16[64,64,128]{2,1,0:T(8,128)(2,1)S(1)}, bf16[64,64,128]{2,1,0:T(8,128)(2,1)}, u32[]{:S(2)}) copy-start(bf16[64,64,128]{2,1,0:T(8,128)(2,1)} %param.11) | copy-start | bytes 3145732
  5.6 25.5 %collective-permute-start.4 = (bf16[32,2176]{1,0:T(8,128)(2,1)S(1)}, bf16[32,2176]{1,0:T(8,128)(2,1)S(1)}, u32[]{:S(2)}, u32[]{:S(2)}) collective-permute-start(bf16[32,2176]{1,0:T(8,128)(2,1)S(1)} %fusion.3.refs_4_), channel_id=1, source_target_pairs={{0,12},{4,0},{8,4},{12,8},{1,13},{5,1},{9,5},{13,9},{2,14},{6,2},{... | collective-permute-start | bytes 417800 | tf_op jit(solution)/shard_map/ppermute | solution.py:309
  6.1 25.0 %collective-permute-start.5 = (bf16[32,2176]{1,0:T(8,128)(2,1)S(1)}, bf16[32,2176]{1,0:T(8,128)(2,1)S(1)}, u32[]{:S(2)}, u32[]{:S(2)}) collective-permute-start(bf16[32,2176]{1,0:T(8,128)(2,1)S(1)} %fusion.3.refs_4_), channel_id=1, source_target_pairs={{0,8},{4,12},{8,0},{12,4},{1,9},{5,13},{9,1},{13,5},{2,10},{6,14},... | collective-permute-start | bytes 417800 | tf_op jit(solution)/shard_map/ppermute | solution.py:309
  6.4 24.6 %collective-permute-start.6 = (bf16[32,2176]{1,0:T(8,128)(2,1)S(1)}, bf16[32,2176]{1,0:T(8,128)(2,1)S(1)}, u32[]{:S(2)}, u32[]{:S(2)}) collective-permute-start(bf16[32,2176]{1,0:T(8,128)(2,1)S(1)} %fusion.3.refs_4_), channel_id=1, source_target_pairs={{0,4},{4,8},{8,12},{12,0},{1,5},{5,9},{9,13},{13,1},{2,6},{6,10},{... | collective-permute-start | bytes 417800 | tf_op jit(solution)/shard_map/ppermute | solution.py:309
  9.5 11.6 %collective-permute-start = (bf16[32,2176]{1,0:T(8,128)(2,1)}, bf16[32,2176]{1,0:T(8,128)(2,1)S(1)}, u32[]{:S(2)}, u32[]{:S(2)}) collective-permute-start(bf16[32,2176]{1,0:T(8,128)(2,1)} %fusion.2), channel_id=1, source_target_pairs={{0,0},{1,4},{2,8},{3,12},{4,1},{5,5},{6,9},{7,13},{8,2},{9,6},{10,... | collective-permute-start | bytes 417800 | tf_op jit(solution)/shard_map/ppermute | solution.py:305
  21.1 7.7 %collective-permute-start.1 = (bf16[32,2176]{1,0:T(8,128)(2,1)S(1)}, bf16[32,2176]{1,0:T(8,128)(2,1)S(1)}, u32[]{:S(2)}, u32[]{:S(2)}) collective-permute-start(bf16[32,2176]{1,0:T(8,128)(2,1)S(1)} %collective-permute-done.refs_0_), channel_id=1, source_target_pairs={{0,2},{2,0},{1,3},{3,1},{4,6},{6,4},{5,7},{7,5},{8,10},{10,8},{9,1... | collective-permute-start | bytes 417800 | tf_op jit(solution)/shard_map/ppermute | solution.py:313
  23.8 7.2 %collective-permute-start.2 = (bf16[32,2176]{1,0:T(8,128)(2,1)S(1)}, bf16[32,2176]{1,0:T(8,128)(2,1)S(1)}, u32[]{:S(2)}, u32[]{:S(2)}) collective-permute-start(bf16[32,2176]{1,0:T(8,128)(2,1)S(1)} %collective-permute-done.refs_0_), channel_id=1, source_target_pairs={{0,1},{1,0},{2,3},{3,2},{4,5},{5,4},{6,7},{7,6},{8,9},{9,8},{10,11... | collective-permute-start | bytes 417800 | tf_op jit(solution)/shard_map/ppermute | solution.py:317
  28.8 2.3 %collective-permute-start.3 = (bf16[32,2176]{1,0:T(8,128)(2,1)S(1)}, bf16[32,2176]{1,0:T(8,128)(2,1)S(1)}, u32[]{:S(2)}, u32[]{:S(2)}) collective-permute-start(bf16[32,2176]{1,0:T(8,128)(2,1)S(1)} %collective-permute-done.1.refs_1_), channel_id=1, source_target_pairs={{0,1},{1,0},{2,3},{3,2},{4,5},{5,4},{6,7},{7,6},{8,9},{9,8},{10,11... | collective-permute-start | bytes 417800 | tf_op jit(solution)/shard_map/ppermute | solution.py:317
  30.9 2.2 %copy-start.1 = (bf16[512,128]{1,0:T(8,128)(2,1)S(1)}, bf16[512,128]{1,0:T(8,128)(2,1)}, u32[]{:S(2)}) copy-start(bf16[512,128]{1,0:T(8,128)(2,1)} %down.5) | copy-start | bytes 393220
  45.3 6.1 %copy-start.4 = (bf16[3,3,128,128]{3,2,1,0:T(8,128)(2,1)S(1)}, bf16[3,3,128,128]{3,2,1,0:T(8,128)(2,1)}, u32[]{:S(2)}) copy-start(bf16[3,3,128,128]{3,2,1,0:T(8,128)(2,1)} %param.21) | copy-start | bytes 884740
  45.9 12.9 %collective-permute-start.7 = (bf16[24,64,128]{2,0,1:T(8,128)(2,1)S(1)}, bf16[24,64,128]{2,0,1:T(8,128)(2,1)S(1)}, u32[]{:S(2)}, u32[]{:S(2)}) collective-permute-start(bf16[24,64,128]{2,0,1:T(8,128)(2,1)S(1)} %get-tuple-element.33), channel_id=1, source_target_pairs={{2,0},{3,1},{6,4},{7,5},{8,10},{9,11},{12,14},{13,15},{18,16},{19,... | collective-permute-start | bytes 1179656 | tf_op jit(solution)/shard_map/ppermute | solution.py:360
  47.2 10.8 %collective-permute-start.11 = (bf16[16,64,128]{2,0,1:T(8,128)(2,1)S(1)}, bf16[16,64,128]{2,0,1:T(8,128)(2,1)S(1)}, u32[]{:S(2)}, u32[]{:S(2)}) collective-permute-start(bf16[16,64,128]{2,0,1:T(8,128)(2,1)S(1)} %get-tuple-element.35), channel_id=1, source_target_pairs={{0,0},{1,4},{2,8},{3,12},{4,1},{5,5},{6,9},{7,13},{8,2},{9,6},{10,... | collective-permute-start | bytes 786440 | tf_op jit(solution)/shard_map/ppermute | solution.py:360
  51.7 21.3 %collective-permute-start.9 = (bf16[24,64,128]{2,0,1:T(8,128)(2,1)S(1)}, bf16[24,64,128]{2,0,1:T(8,128)(2,1)S(1)}, u32[]{:S(2)}, u32[]{:S(2)}) collective-permute-start(bf16[24,64,128]{2,0,1:T(8,128)(2,1)S(1)} %get-tuple-element.33), channel_id=1, source_target_pairs={{0,0},{1,4},{4,1},{5,5},{10,10},{11,14},{14,11},{15,15},{16,16},{1... | collective-permute-start | bytes 1179656 | tf_op jit(solution)/shard_map/ppermute | solution.py:360
  54.3 18.6 %collective-permute-start.10 = (bf16[24,64,128]{2,0,1:T(8,128)(2,1)S(1)}, bf16[24,64,128]{2,0,1:T(8,128)(2,1)S(1)}, u32[]{:S(2)}, u32[]{:S(2)}) collective-permute-start(bf16[24,64,128]{2,0,1:T(8,128)(2,1)S(1)} %get-tuple-element.31), channel_id=1, source_target_pairs={{0,0},{1,4},{2,8},{3,12},{4,1},{5,5},{6,9},{7,13},{8,2},{9,6},{10,... | collective-permute-start | bytes 1179656 | tf_op jit(solution)/shard_map/ppermute | solution.py:360
  58.8 14.4 %collective-permute-start.8 = (bf16[24,64,128]{2,0,1:T(8,128)(2,1)S(1)}, bf16[24,64,128]{2,0,1:T(8,128)(2,1)S(1)}, u32[]{:S(2)}, u32[]{:S(2)}) collective-permute-start(bf16[24,64,128]{2,0,1:T(8,128)(2,1)S(1)} %collective-permute-done.7), channel_id=1, source_target_pairs={{0,8},{1,12},{4,9},{5,13},{10,2},{11,6},{14,3},{15,7},{16,24},{17,... | collective-permute-start | bytes 1179656 | tf_op jit(solution)/shard_map/ppermute | solution.py:360
  73.4 22.6 %collective-permute-start.13 = (bf16[64,128]{1,0:T(8,128)(2,1)S(1)}, bf16[64,128]{1,0:T(8,128)(2,1)S(1)}, u32[]{:S(2)}, u32[]{:S(2)}) collective-permute-start(bf16[64,128]{1,0:T(8,128)(2,1)S(1)} %fusion.7), channel_id=1, source_target_pairs={{1,0},{2,1},{3,2},{5,4},{6,5},{7,6},{9,8},{10,9},{11,10},{13,12},{... | collective-permute-start | bytes 49160 | tf_op jit(solution)/shard_map/ppermute | solution.py:411
  93.9 5.0 %collective-permute-start.12 = (bf16[64,128]{1,0:T(8,128)(2,1)S(1)}, bf16[64,128]{1,0:T(8,128)(2,1)S(1)}, u32[]{:S(2)}, u32[]{:S(2)}) collective-permute-start(bf16[64,128]{1,0:T(8,128)(2,1)S(1)} %fusion.5), channel_id=1, source_target_pairs={{0,1},{1,2},{2,3},{4,5},{5,6},{6,7},{8,9},{9,10},{10,11},{12,13},{... | collective-permute-start | bytes 49160 | tf_op jit(solution)/shard_map/ppermute | solution.py:410
  99.0 4.6 %collective-permute-start.15 = (bf16[66,128]{1,0:T(8,128)(2,1)S(1)}, bf16[66,128]{1,0:T(8,128)(2,1)S(1)}, u32[]{:S(2)}, u32[]{:S(2)}) collective-permute-start(bf16[66,128]{1,0:T(8,128)(2,1)S(1)} %pad_maximum_fusion.6), channel_id=1, source_target_pairs={{4,0},{8,4},{12,8},{5,1},{9,5},{13,9},{6,2},{10,6},{14,10},{7,3},{... | collective-permute-start | bytes 50696 | tf_op jit(solution)/shard_map/ppermute | solution.py:414
  102.2 5.7 %collective-permute-start.14 = (bf16[66,128]{1,0:T(8,128)(2,1)S(1)}, bf16[66,128]{1,0:T(8,128)(2,1)S(1)}, u32[]{:S(2)}, u32[]{:S(2)}) collective-permute-start(bf16[66,128]{1,0:T(8,128)(2,1)S(1)} %pad_maximum_fusion.5), channel_id=1, source_target_pairs={{0,4},{4,8},{8,12},{1,5},{5,9},{9,13},{2,6},{6,10},{10,14},{3,7},{... | collective-permute-start | bytes 50696 | tf_op jit(solution)/shard_map/ppermute | solution.py:413

commit v5 on v4

--- a/solution.py
+++ b/solution.py
@@ -18,6 +18,51 @@
 
 def kernel_params(mib):
     return pltpu.CompilerParams(vmem_limit_bytes=mib * 1024 * 1024)
+
+
+def project_kernel(features, mask, left_weight, right_weight, left, right):
+    depth, tokens = mask.shape
+    inner, width = left_weight.shape
+    group = lanes // width
+
+    def chosen(rows, columns, test):
+        a = lax.broadcasted_iota(jnp.int32, (rows, columns), 0)
+        b = lax.broadcasted_iota(jnp.int32, (rows, columns), 1)
+        return jnp.where(test(a, b), 1.0, 0.0).astype(jnp.bfloat16)
+
+    dot = lambda a, b: jnp.dot(a, b, preferred_element_type=jnp.float32)
+    repeat_rows = chosen(group * inner, inner, lambda a, b: a % inner == b)
+    repeat_lanes = chosen(width, lanes, lambda a, b: a == b % width)
+    own_block = chosen(group * inner, lanes, lambda a, b: a // inner == b // width)
+    spread = []
+    for weight in (left_weight, right_weight):
+        tall = dot(repeat_rows, weight[...]).astype(jnp.bfloat16)
+        spread.append(dot(tall, repeat_lanes).astype(jnp.bfloat16) * own_block)
+    both = jnp.concatenate(spread, axis=1)
+    kept = mask[...].astype(jnp.float32).astype(jnp.bfloat16)
+    wide_mask = dot(kept, chosen(tokens, tokens * width, lambda a, b: a == b // width))
+    for g in range(tokens // group):
+        at = slice(g * lanes, (g + 1) * lanes)
+        value = dot(features[:, g * group * inner : (g + 1) * group * inner], both)
+        left[:, at] = (value[:, :lanes] * wide_mask[:, at]).astype(jnp.bfloat16)
+        right[:, at] = (value[:, lanes:] * wide_mask[:, at]).astype(jnp.bfloat16)
+    narrow = dot(kept, chosen(tokens, lanes, lambda a, b: a == b)).astype(jnp.bfloat16)
+    left[:, tokens * width :] = narrow
+    right[:, tokens * width :] = narrow
+
+
+def project_sides(features, mask, left_weight, right_weight):
+    depth, tokens = mask.shape
+    span = tokens * left_weight.shape[1] + lanes
+    in_vmem = pl.BlockSpec(memory_space=pltpu.VMEM)
+    return pl.pallas_call(
+        project_kernel,
+        in_specs=[in_vmem] * 4,
+        out_specs=[in_vmem] * 2,
+        out_shape=[jax.ShapeDtypeStruct((depth, span), jnp.bfloat16)] * 2,
+        compiler_params=kernel_params(8),
+        cost_estimate=pl.CostEstimate(flops=1024, bytes_accessed=1024, transcendentals=0),
+    )(features.reshape(depth, -1), mask, left_weight, right_weight)
 
 
 def arrange_kernel(
@@ -110,17 +155,29 @@
 
 
 def tile_kernel(
-    row_side, lane_side, scale, base, weight, gate_up, down, out, products, stacked, held
+    row_side,
+    lane_side,
+    scale,
+    base,
+    weight,
+    gate_up,
+    down,
+    out,
+    products,
+    stacked,
+    held,
+    *,
+    first,
+    width,
 ):
     strip, tokens_row, channels = out.shape
-    width = lane_side.shape[2] // strip
     high = width // turns
     groups = strip // turns
     span = high * tokens_row
     for turn in range(turns):
         products[turn] = jnp.dot(
             row_side[turn * span : (turn + 1) * span, :],
-            lane_side[turn],
+            lane_side[turn, :, first * width : (first + strip) * width],
             preferred_element_type=jnp.float32,
         ).astype(jnp.bfloat16)
     position = lax.broadcasted_iota(jnp.int32, (tokens_row, lanes), 1) // width
@@ -141,37 +198,28 @@
         update = jnp.dot(stacked[u], weight[u], preferred_element_type=jnp.float32)
         for g in range(groups):
             n = turns * g + u
-            factor = scale[n // unit][:, n % unit : n % unit + 1]
+            at = first + n
+            factor = scale[at // unit][:, at % unit : at % unit + 1]
             value = update[g * tokens_row : (g + 1) * tokens_row] * factor
-            value = base[n].astype(jnp.float32) + value
+            value = base[at].astype(jnp.float32) + value
             held[n * tokens_row : (n + 1) * tokens_row, :] = value.astype(jnp.bfloat16)
-    piece = math.gcd(strip, 24) if strip > 24 else strip
-    for first in range(0, strip, piece):
-        at = slice(first * tokens_row, (first + piece) * tokens_row)
+    piece = strip if strip <= 32 else math.gcd(strip, 24)
+    for start in range(0, strip, piece):
+        at = slice(start * tokens_row, (start + piece) * tokens_row)
         result = transition_rows(held[at, :].astype(jnp.float32), gate_up[...], down[...])
-        out[first : first + piece] = result.astype(out.dtype).reshape(piece, tokens_row, channels)
-
-
-def tile_strips(first, count, strip, row_side, lane_side, scale, base, weight, gate_up, down):
+        out[start : start + piece] = result.astype(out.dtype).reshape(piece, tokens_row, channels)
+
+
+def tile_strip(first, strip, row_side, lane_side, scale, base, weight, gate_up, down):
     tokens_row, channels = base.shape[1:]
-    turn_count, depth, span = lane_side.shape
-    width = span // base.shape[0]
-    start = first // strip
-    fixed = lambda a: pl.BlockSpec(a.shape, lambda n, rank=a.ndim: (0,) * rank)
+    width = lane_side.shape[2] // base.shape[0]
+    operands = [row_side, lane_side, scale, base, weight, gate_up, down]
+    in_vmem = pl.BlockSpec(memory_space=pltpu.VMEM)
     return pl.pallas_call(
-        tile_kernel,
-        grid=(count // strip,),
-        in_specs=[
-            fixed(row_side),
-            pl.BlockSpec((turn_count, depth, strip * width), lambda n: (0, 0, n + start)),
-            pl.BlockSpec((strip // unit, tokens_row, lanes), lambda n: (n + start, 0, 0)),
-            pl.BlockSpec((strip, tokens_row, channels), lambda n: (n + start, 0, 0)),
-            fixed(weight),
-            fixed(gate_up),
-            fixed(down),
-        ],
-        out_specs=pl.BlockSpec((strip, tokens_row, channels), lambda n: (n, 0, 0)),
-        out_shape=jax.ShapeDtypeStruct((count, tokens_row, channels), jnp.bfloat16),
+        functools.partial(tile_kernel, first=first, width=width),
+        in_specs=[in_vmem] * len(operands),
+        out_specs=in_vmem,
+        out_shape=jax.ShapeDtypeStruct((strip, tokens_row, channels), jnp.bfloat16),
         scratch_shapes=[
             pltpu.VMEM((turns, tokens_row * width // turns, strip * width), jnp.bfloat16),
             pltpu.VMEM((turns, strip // turns * tokens_row, width * width), jnp.bfloat16),
@@ -179,7 +227,7 @@
         ],
         compiler_params=kernel_params(40),
         cost_estimate=pl.CostEstimate(flops=1024, bytes_accessed=1024, transcendentals=0),
-    )(row_side, lane_side, scale, base, weight, gate_up, down)
+    )(*operands)
 
 
 def conv_kernel(
@@ -299,11 +347,11 @@
         return jnp.concatenate([side.reshape(depth, tokens * width), room], axis=1)
 
     if square:
-        left_block = beside(project(flat, left_weight), narrow_mask)
-        flat, left_block = lax.optimization_barrier((flat, left_block))
+        left_block, right_block = project_sides(
+            alignment_features, alignment_mask, left_weight, right_weight
+        )
         mirror_pairs = [(place_of(r, c), place_of(c, r)) for r, c in tiles]
         first = lax.ppermute(left_block, whole, mirror_pairs)
-        right_block = beside(project(flat, right_weight), narrow_mask)
         col_side, col_places = [right_block], [row_index]
         for step in range(1, row_count):
             col_side.append(lax.ppermute(right_block, "row", shifts(row_count, -step)))
@@ -338,12 +386,12 @@
 
     sides = arrange(places, row_side, col_side, width, rows_dev, cols_dev)
 
-    def run(first, count, strip, after=None):
+    def run(first, strip, after=None):
         row_channels = sides[0]
         if after is not None:
             row_channels, _ = lax.optimization_barrier((row_channels, after))
-        return tile_strips(
-            first, count, strip, row_channels, *sides[1:], base, weight, gate_up, down_weight
+        return tile_strip(
+            first, strip, row_channels, *sides[1:], base, weight, gate_up, down_weight
         )
 
     ahead = lambda size: [(n, n + 1) for n in range(size - 1)]
@@ -358,18 +406,16 @@
         from_host = [(host(r, c), place_of(c, r)) for r, c in away]
         beside_pairs = [(place_of(r, c), place_of(c, r)) for r, c in near]
         send = lambda value, pairs: lax.ppermute(value, whole, pairs)
-        last = run(6 * part, 2 * part, 2 * part)
-        mirrored_last = send(last, mirror_pairs)
-        opening = run(0, 3 * part, 3 * part, last)
+        opening = run(0, 3 * part)
         hosted = send(opening, to_host)
         mirrored_near = send(opening, beside_pairs)
-        middle = run(3 * part, 3 * part, 3 * part, opening)
-        mirrored_middle = send(middle, mirror_pairs)
+        rest = run(3 * part, 5 * part, opening)
+        mirrored_rest = send(rest, mirror_pairs)
         mirrored_away = send(hosted, from_host)
-        turned = jnp.concatenate([opening, middle, last], axis=0)
-        mirrored = [[mirrored_away, mirrored_near], [mirrored_middle], [mirrored_last]]
+        turned = jnp.concatenate([opening, rest], axis=0)
+        mirrored = [[mirrored_away, mirrored_near], [mirrored_rest]]
     else:
-        turned = run(0, cols_dev, math.gcd(unit, cols_dev))
+        turned = run(0, cols_dev)
         share = rows_dev // col_count
         fold = row_count // col_count
         second = lax.all_to_all(

time: 113 us -> 106 us (0.938)
  the two profiles are of different devices: /device:TPU:30 before, /device:TPU:1 now
where the time goes in v5:
time: 106 us; the launch traced here: 104 us
  starting transfers between devices  51.1 us (48%)
  Pallas kernels  19 us (18%)
  waiting for transfers between devices  17.7 us (17%)
  local copies, waits for them, and re-layouts  9.38 us (9%)
  other arithmetic  5.93 us (6%)
    ppermute x1, starting transfers between devices, on_device(): left = lax.ppermute(last_side, plane, ahead(col_count))  13.7 us
    ppermute x4, waiting for transfers between devices, on_device(): send = lambda value, pairs: lax.ppermute(value, whole, pairs)  12.1 us
    pallas_call x2, Pallas kernels, tile_strip(): pl.pallas_call(functools.partial(tile_kernel, first=first, width=width),...  11.9 us
    ppermute x4, starting transfers between devices, on_device(): send = lambda value, pairs: lax.ppermute(value, whole, pairs)  10.9 us
    ppermute x2, starting transfers between devices, on_device(): lax.ppermute(row_side[n], 'chan', shifts(core_count, -step))  5.98 us
    ppermute x1, starting transfers between devices, on_device(): first = lax.ppermute(left_block, whole, mirror_pairs)  5.49 us
    ppermute x3, starting transfers between devices, on_device(): col_side.append(lax.ppermute(right_block, 'row', shifts(row_count, -step)))  4.66 us
    unnamed x18, local copies, waits for them, and re-layouts  4.32 us
  transfers between devices with their start and end apart: 15, of which 5 were waited for; matrix products, arithmetic and copies ran while one was open for 10% of the time, Pallas kernels for 0%

profile of v5, /device:TPU:1, one launch (start us, length us, event | category | flops | bytes accessed | tf_op | source)
XLA Modules:
  0.0 103.7 jit_solution(3854635894811249258)
XLA Ops:
  0.0 1.5 %reshape.46.features = bf16[32,4096]{1,0:T(8,128)(2,1)S(1)} reshape(bf16[32,64,64]{2,1,0:T(8,128)(2,1)} %param.12) | data formatting | bytes 524288 | tf_op jit(solution)/shard_map/reshape | solution.py:65
  4.8 4.2 %collective-permute-start.4 = (bf16[32,2176]{1,0:T(8,128)(2,1)S(1)}, bf16[32,2176]{1,0:T(8,128)(2,1)S(1)}, u32[]{:S(2)}, u32[]{:S(2)}) collective-permute-start(bf16[32,2176]{1,0:T(8,128)(2,1)S(1)} %get-tuple-element.12.refs_4_), channel_id=1, source_target_pairs={{0,12},{4,0},{8,4},{12,8},{1,13},{5,1},{9,5},{13,9},{2,14},{6,2},{... | collective-permute-start | bytes 417800 | tf_op jit(solution)/shard_map/ppermute | solution.py:357
  9.4 5.5 %collective-permute-start = (bf16[32,2176]{1,0:T(8,128)(2,1)S(1)}, bf16[32,2176]{1,0:T(8,128)(2,1)S(1)}, u32[]{:S(2)}, u32[]{:S(2)}) collective-permute-start(bf16[32,2176]{1,0:T(8,128)(2,1)S(1)} %get-tuple-element.11), channel_id=1, source_target_pairs={{0,0},{1,4},{2,8},{3,12},{4,1},{5,5},{6,9},{7,13},{8,2},{9,6},{10,... | collective-permute-start | bytes 417800 | tf_op jit(solution)/shard_map/ppermute | solution.py:354
  16.0 4.1 %collective-permute-done.refs_0_ = bf16[32,2176]{1,0:T(8,128)(2,1)S(1)} collective-permute-done((bf16[32,2176]{1,0:T(8,128)(2,1)S(1)}, bf16[32,2176]{1,0:T(8,128)(2,1)S(1)}, u32[]{:S(2)}, u32[]{:S(2)}) %collective-permute-start) | collective-permute-done | bytes 139296 | tf_op jit(solution)/shard_map/ppermute | solution.py:354
  20.1 3.2 %collective-permute-start.1 = (bf16[32,2176]{1,0:T(8,128)(2,1)S(1)}, bf16[32,2176]{1,0:T(8,128)(2,1)S(1)}, u32[]{:S(2)}, u32[]{:S(2)}) collective-permute-start(bf16[32,2176]{1,0:T(8,128)(2,1)S(1)} %collective-permute-done.refs_0_), channel_id=1, source_target_pairs={{0,2},{2,0},{1,3},{3,1},{4,6},{6,4},{5,7},{7,5},{8,10},{10,8},{9,1... | collective-permute-start | bytes 417800 | tf_op jit(solution)/shard_map/ppermute | solution.py:361
  23.9 1.9 %copy.43 = bf16[64,64,128]{2,0,1:T(8,128)(2,1)S(1)} copy(bf16[64,64,128]{2,1,0:T(8,128)(2,1)} %param.11) | data formatting | bytes 2097152 | tf_op args[0]
  25.8 1.6 %pad_maximum_fusion.1 = (bf16[8,4,32,128]{3,2,1,0:T(8,128)(2,1)S(1)}, bf16[8,4,32,128]{3,2,1,0:T(8,128)(2,1)}) fusion(bf16[8,3,32,128]{3,2,1,0:T(8,128)(2,1)S(1)} %get-tuple-element.33, bf16[8,1,32,128]{3,2,1,0:T(8,128)(2,1)S(1)} %get-tuple-element.31, bf16[8,1,32,128]{3,2,1,0:T(8,128)(2,1)} %get-tuple-element.32, ...), kind=kLoop, calls=%fused_computation.3 | loop fusion | flops 262144 | bytes 1048576 | tf_op jit(solution)/shard_map/jit(_roll_static)/concatenate | solution.py:381
  27.4 6.0 %collective-permute-start.2 = (bf16[32,2176]{1,0:T(8,128)(2,1)S(1)}, bf16[32,2176]{1,0:T(8,128)(2,1)S(1)}, u32[]{:S(2)}, u32[]{:S(2)}) collective-permute-start(bf16[32,2176]{1,0:T(8,128)(2,1)S(1)} %collective-permute-done.refs_0_), channel_id=1, source_target_pairs={{0,1},{1,0},{2,3},{3,2},{4,5},{5,4},{6,7},{7,6},{8,9},{9,8},{10,11... | collective-permute-start | bytes 417800 | tf_op jit(solution)/shard_map/ppermute | solution.py:365
  33.7 1.1 %pad_maximum_fusion.weight = bf16[4,1024,128]{2,1,0:T(8,128)(2,1)S(1)} fusion(bf16[1,1024,128]{2,1,0:T(8,128)(2,1)} %bitcast.68, bf16[1,1024,128]{2,1,0:T(8,128)(2,1)S(1)} %bitcast.66, bf16[1,1024,128]{2,1,0:T(8,128)(2,1)S(1)} %bitcast.67, bf16[1,1024,128]{2,1,0:T(8,128)(2,1)S(1)} %bitcast.64), kind=kLoop, calls=%fused_computation | loop fusion | flops 1572864 | bytes 2097152 | tf_op jit(solution)/shard_map/stack | solution.py:380
  34.9 2.0 %shard_map.110 = (bf16[2048,128]{1,0:T(8,128)(2,1)S(1)}, bf16[4,128,2048]{2,1,0:T(8,128)(2,1)S(1)}, f32[8,64,128]{2,1,0:T(8,128)S(1)}) custom-call(s32[8]{0:T(128)S(1)} %broadcast_multiply_fusion.1.places, bf16[32,2176]{1,0:T(8,128)(2,1)S(1)} %collective-permute-done.refs_0_, bf16[32,2176]{1,0:T(8,128)(2,1)S(1)} %collective-permute-done.1.refs_1_, ...), custom_call_target="tpu_custom_call" | custom-call | flops 1024 | bytes 1024 | tf_op jit(solution)/shard_map/pallas_call | solution.py:121
  37.0 4.1 %shard_map.111 = bf16[24,64,128]{2,1,0:T(8,128)(2,1)S(1)} custom-call(bf16[2048,128]{1,0:T(8,128)(2,1)S(1)} %get-tuple-element.16.row_side, bf16[4,128,2048]{2,1,0:T(8,128)(2,1)S(1)} %get-tuple-element.14.lane_side, f32[8,64,128]{2,1,0:T(8,128)S(1)} %get-tuple-element.15.scale, bf16[64,64,128]{2,1,0:T(8,128)(2,1)S(1)} %bitcast.57, ...), custom_call_target="tpu_custom_call" | custom-call | flops 1024 | bytes 1024 | tf_op jit(solution)/shard_map/pallas_call | solution.py:218
  41.4 7.8 %shard_map.112 = bf16[40,64,128]{2,1,0:T(8,128)(2,1)S(1)} custom-call(bf16[2048,128]{1,0:T(8,128)(2,1)S(1)} %get-tuple-element.16.row_side, bf16[4,128,2048]{2,1,0:T(8,128)(2,1)S(1)} %get-tuple-element.14.lane_side, f32[8,64,128]{2,1,0:T(8,128)S(1)} %get-tuple-element.15.scale, bf16[64,64,128]{2,1,0:T(8,128)(2,1)S(1)} %bitcast.58, ...), custom_call_target="tpu_custom_call" | custom-call | flops 1024 | bytes 1024 | tf_op jit(solution)/shard_map/pallas_call | solution.py:218
  49.2 1.3 %collective-permute-start.7 = (bf16[24,64,128]{2,0,1:T(8,128)(2,1)S(1)}, bf16[24,64,128]{2,0,1:T(8,128)(2,1)S(1)}, u32[]{:S(2)}, u32[]{:S(2)}) collective-permute-start(bf16[24,64,128]{2,0,1:T(8,128)(2,1)S(1)} %get-tuple-element.29), channel_id=1, source_target_pairs={{2,0},{3,1},{6,4},{7,5},{8,10},{9,11},{12,14},{13,15},{18,16},{19,... | collective-permute-start | bytes 1179656 | tf_op jit(solution)/shard_map/ppermute | solution.py:408
  51.0 2.8 %collective-permute-start.10 = (bf16[40,64,128]{2,0,1:T(8,128)(2,1)S(1)}, bf16[40,64,128]{2,0,1:T(8,128)(2,1)S(1)}, u32[]{:S(2)}, u32[]{:S(2)}) collective-permute-start(bf16[40,64,128]{2,0,1:T(8,128)(2,1)S(1)} %get-tuple-element.27), channel_id=1, source_target_pairs={{0,0},{1,4},{2,8},{3,12},{4,1},{5,5},{6,9},{7,13},{8,2},{9,6},{10,... | collective-permute-start | bytes 1966088 | tf_op jit(solution)/shard_map/ppermute | solution.py:408
  55.1 2.8 %collective-permute-start.9 = (bf16[24,64,128]{2,0,1:T(8,128)(2,1)S(1)}, bf16[24,64,128]{2,0,1:T(8,128)(2,1)S(1)}, u32[]{:S(2)}, u32[]{:S(2)}) collective-permute-start(bf16[24,64,128]{2,0,1:T(8,128)(2,1)S(1)} %get-tuple-element.29), channel_id=1, source_target_pairs={{0,0},{1,4},{4,1},{5,5},{10,10},{11,14},{14,11},{15,15},{16,16},{1... | collective-permute-start | bytes 1179656 | tf_op jit(solution)/shard_map/ppermute | solution.py:408
  57.9 1.3 %multiply_multiply_fusion.3 = (f32[64]{0:T(128)S(1)}, f32[64]{0:T(128)S(1)}) fusion(f32[]{:T(128)} %bitcast.18, s32[64]{0:T(128)S(1)} %get-tuple-element.20.valid_i, f32[]{:T(128)} %bitcast.25), kind=kLoop, calls=%fused_computation.40 | loop fusion | flops 320 | bytes 776 | tf_op jit(solution)/shard_map/mul | solution.py:450
  59.2 2.1 %collective-permute-done.7 = bf16[24,64,128]{2,0,1:T(8,128)(2,1)S(1)} collective-permute-done((bf16[24,64,128]{2,0,1:T(8,128)(2,1)S(1)}, bf16[24,64,128]{2,0,1:T(8,128)(2,1)S(1)}, u32[]{:S(2)}, u32[]{:S(2)}) %collective-permute-start.7) | collective-permute-done | bytes 393248 | tf_op jit(solution)/shard_map/ppermute | solution.py:408
  61.2 4.0 %collective-permute-start.8 = (bf16[24,64,128]{2,0,1:T(8,128)(2,1)S(1)}, bf16[24,64,128]{2,0,1:T(8,128)(2,1)S(1)}, u32[]{:S(2)}, u32[]{:S(2)}) collective-permute-start(bf16[24,64,128]{2,0,1:T(8,128)(2,1)S(1)} %collective-permute-done.7), channel_id=1, source_target_pairs={{0,8},{1,12},{4,9},{5,13},{10,2},{11,6},{14,3},{15,7},{16,24},{17,... | collective-permute-start | bytes 1179656 | tf_op jit(solution)/shard_map/ppermute | solution.py:408
  65.8 10.1 %collective-permute-done.9 = bf16[24,64,128]{2,0,1:T(8,128)(2,1)S(1)} collective-permute-done((bf16[24,64,128]{2,0,1:T(8,128)(2,1)S(1)}, bf16[24,64,128]{2,0,1:T(8,128)(2,1)S(1)}, u32[]{:S(2)}, u32[]{:S(2)}) %collective-permute-start.9) | collective-permute-done | bytes 393248 | tf_op jit(solution)/shard_map/ppermute | solution.py:408
  76.6 1.9 %collective-permute-start.12 = (bf16[64,128]{1,0:T(8,128)(2,1)S(1)}, bf16[64,128]{1,0:T(8,128)(2,1)S(1)}, u32[]{:S(2)}, u32[]{:S(2)}) collective-permute-start(bf16[64,128]{1,0:T(8,128)(2,1)S(1)} %fusion.3), channel_id=1, source_target_pairs={{1,0},{2,1},{3,2},{5,4},{6,5},{7,6},{9,8},{10,9},{11,10},{13,12},{... | collective-permute-start | bytes 49160 | tf_op jit(solution)/shard_map/ppermute | solution.py:457
  78.6 13.7 %collective-permute-start.11 = (bf16[64,128]{1,0:T(8,128)(2,1)S(1)}, bf16[64,128]{1,0:T(8,128)(2,1)S(1)}, u32[]{:S(2)}, u32[]{:S(2)}) collective-permute-start(bf16[64,128]{1,0:T(8,128)(2,1)S(1)} %fusion.1), channel_id=1, source_target_pairs={{0,1},{1,2},{2,3},{4,5},{5,6},{6,7},{8,9},{9,10},{10,11},{12,13},{... | collective-permute-start | bytes 49160 | tf_op jit(solution)/shard_map/ppermute | solution.py:456
  93.2 1.3 %collective-permute-start.14 = (bf16[66,128]{1,0:T(8,128)(2,1)S(1)}, bf16[66,128]{1,0:T(8,128)(2,1)S(1)}, u32[]{:S(2)}, u32[]{:S(2)}) collective-permute-start(bf16[66,128]{1,0:T(8,128)(2,1)S(1)} %pad_maximum_fusion.6), channel_id=1, source_target_pairs={{4,0},{8,4},{12,8},{5,1},{9,5},{13,9},{6,2},{10,6},{14,10},{7,3},{... | collective-permute-start | bytes 50696 | tf_op jit(solution)/shard_map/ppermute | solution.py:460
  94.5 4.0 %collective-permute-start.13 = (bf16[66,128]{1,0:T(8,128)(2,1)S(1)}, bf16[66,128]{1,0:T(8,128)(2,1)S(1)}, u32[]{:S(2)}, u32[]{:S(2)}) collective-permute-start(bf16[66,128]{1,0:T(8,128)(2,1)S(1)} %pad_maximum_fusion.5), channel_id=1, source_target_pairs={{0,4},{4,8},{8,12},{1,5},{5,9},{9,13},{2,6},{6,10},{10,14},{3,7},{... | collective-permute-start | bytes 50696 | tf_op jit(solution)/shard_map/ppermute | solution.py:459
  99.5 4.2 %shard_map.113 = bf16[64,64,128]{2,1,0:T(8,128)(2,1)} custom-call(s32[64]{0:T(128)S(1)} %get-tuple-element.20.valid_i, bf16[64,64,128]{2,1,0:T(8,128)(2,1)S(1)} %bitcast.60, bf16[24,64,128]{2,1,0:T(8,128)(2,1)S(1)} %copy.33.refs_0_, bf16[24,64,128]{2,1,0:T(8,128)(2,1)S(1)} %copy.34.refs_1_, bf16[40,64,128]{2,1,0:T(8,128)(2,1)S(1)} %copy.35.refs_2_, ...), custom_call_target="tpu_custom_call" | custom-call | flops 1207959552 | bytes 3145728 | tf_op jit(solution)/shard_map/pallas_call | solution.py:287
  (73 shorter events, 10.6 us)
Async XLA Ops:
  0.0 15.0 %copy-start.2 = (bf16[1024,128]{1,0:T(8,128)(2,1)S(1)}, bf16[1024,128]{1,0:T(8,128)(2,1)}, u32[]{:S(2)}) copy-start(bf16[1024,128]{1,0:T(8,128)(2,1)} %param.17) | copy-start | bytes 786436
  0.0 15.8 %copy-start.4 = (bf16[128,512]{1,0:T(8,128)(2,1)S(1)}, bf16[128,512]{1,0:T(8,128)(2,1)}, u32[]{:S(2)}) copy-start(bf16[128,512]{1,0:T(8,128)(2,1)} %param.18) | copy-start | bytes 393220
  3.1 0.7 copy-start.1
  4.7 11.2 %copy-start.6 = (s32[256]{0:T(256)S(1)}, s32[256]{0:T(256)}, u32[]{:S(2)}) copy-start(s32[256]{0:T(256)} %param.14) | copy-start | bytes 3076
  4.7 11.2 %copy-start.5 = (bf16[128,512]{1,0:T(8,128)(2,1)S(1)}, bf16[128,512]{1,0:T(8,128)(2,1)}, u32[]{:S(2)}) copy-start(bf16[128,512]{1,0:T(8,128)(2,1)} %param.19) | copy-start | bytes 393220
  4.8 30.1 %collective-permute-start.4 = (bf16[32,2176]{1,0:T(8,128)(2,1)S(1)}, bf16[32,2176]{1,0:T(8,128)(2,1)S(1)}, u32[]{:S(2)}, u32[]{:S(2)}) collective-permute-start(bf16[32,2176]{1,0:T(8,128)(2,1)S(1)} %get-tuple-element.12.refs_4_), channel_id=1, source_target_pairs={{0,12},{4,0},{8,4},{12,8},{1,13},{5,1},{9,5},{13,9},{2,14},{6,2},{... | collective-permute-start | bytes 417800 | tf_op jit(solution)/shard_map/ppermute | solution.py:357
  9.0 25.9 %collective-permute-start.5 = (bf16[32,2176]{1,0:T(8,128)(2,1)S(1)}, bf16[32,2176]{1,0:T(8,128)(2,1)S(1)}, u32[]{:S(2)}, u32[]{:S(2)}) collective-permute-start(bf16[32,2176]{1,0:T(8,128)(2,1)S(1)} %get-tuple-element.12.refs_4_), channel_id=1, source_target_pairs={{0,8},{4,12},{8,0},{12,4},{1,9},{5,13},{9,1},{13,5},{2,10},{6,14},... | collective-permute-start | bytes 417800 | tf_op jit(solution)/shard_map/ppermute | solution.py:357
  9.0 25.9 %collective-permute-start.6 = (bf16[32,2176]{1,0:T(8,128)(2,1)S(1)}, bf16[32,2176]{1,0:T(8,128)(2,1)S(1)}, u32[]{:S(2)}, u32[]{:S(2)}) collective-permute-start(bf16[32,2176]{1,0:T(8,128)(2,1)S(1)} %get-tuple-element.12.refs_4_), channel_id=1, source_target_pairs={{0,4},{4,8},{8,12},{12,0},{1,5},{5,9},{9,13},{13,1},{2,6},{6,10},{... | collective-permute-start | bytes 417800 | tf_op jit(solution)/shard_map/ppermute | solution.py:357
  9.4 10.7 %collective-permute-start = (bf16[32,2176]{1,0:T(8,128)(2,1)S(1)}, bf16[32,2176]{1,0:T(8,128)(2,1)S(1)}, u32[]{:S(2)}, u32[]{:S(2)}) collective-permute-start(bf16[32,2176]{1,0:T(8,128)(2,1)S(1)} %get-tuple-element.11), channel_id=1, source_target_pairs={{0,0},{1,4},{2,8},{3,12},{4,1},{5,5},{6,9},{7,13},{8,2},{9,6},{10,... | collective-permute-start | bytes 417800 | tf_op jit(solution)/shard_map/ppermute | solution.py:354
  20.1 13.3 %collective-permute-start.1 = (bf16[32,2176]{1,0:T(8,128)(2,1)S(1)}, bf16[32,2176]{1,0:T(8,128)(2,1)S(1)}, u32[]{:S(2)}, u32[]{:S(2)}) collective-permute-start(bf16[32,2176]{1,0:T(8,128)(2,1)S(1)} %collective-permute-done.refs_0_), channel_id=1, source_target_pairs={{0,2},{2,0},{1,3},{3,1},{4,6},{6,4},{5,7},{7,5},{8,10},{10,8},{9,1... | collective-permute-start | bytes 417800 | tf_op jit(solution)/shard_map/ppermute | solution.py:361
  23.9 9.5 %copy-start.3 = (bf16[3,3,128,128]{3,2,1,0:T(8,128)(2,1)S(1)}, bf16[3,3,128,128]{3,2,1,0:T(8,128)(2,1)}, u32[]{:S(2)}) copy-start(bf16[3,3,128,128]{3,2,1,0:T(8,128)(2,1)} %param.21) | copy-start | bytes 884740
  27.4 7.5 %collective-permute-start.2 = (bf16[32,2176]{1,0:T(8,128)(2,1)S(1)}, bf16[32,2176]{1,0:T(8,128)(2,1)S(1)}, u32[]{:S(2)}, u32[]{:S(2)}) collective-permute-start(bf16[32,2176]{1,0:T(8,128)(2,1)S(1)} %collective-permute-done.refs_0_), channel_id=1, source_target_pairs={{0,1},{1,0},{2,3},{3,2},{4,5},{5,4},{6,7},{7,6},{8,9},{9,8},{10,11... | collective-permute-start | bytes 417800 | tf_op jit(solution)/shard_map/ppermute | solution.py:365
  33.4 1.5 %collective-permute-start.3 = (bf16[32,2176]{1,0:T(8,128)(2,1)S(1)}, bf16[32,2176]{1,0:T(8,128)(2,1)S(1)}, u32[]{:S(2)}, u32[]{:S(2)}) collective-permute-start(bf16[32,2176]{1,0:T(8,128)(2,1)S(1)} %collective-permute-done.1.refs_1_), channel_id=1, source_target_pairs={{0,1},{1,0},{2,3},{3,2},{4,5},{5,4},{6,7},{7,6},{8,9},{9,8},{10,11... | collective-permute-start | bytes 417800 | tf_op jit(solution)/shard_map/ppermute | solution.py:365
  33.7 3.2 %copy-start = (bf16[512,128]{1,0:T(8,128)(2,1)S(1)}, bf16[512,128]{1,0:T(8,128)(2,1)}, u32[]{:S(2)}) copy-start(bf16[512,128]{1,0:T(8,128)(2,1)} %down.3) | copy-start | bytes 393220
  49.2 12.1 %collective-permute-start.7 = (bf16[24,64,128]{2,0,1:T(8,128)(2,1)S(1)}, bf16[24,64,128]{2,0,1:T(8,128)(2,1)S(1)}, u32[]{:S(2)}, u32[]{:S(2)}) collective-permute-start(bf16[24,64,128]{2,0,1:T(8,128)(2,1)S(1)} %get-tuple-element.29), channel_id=1, source_target_pairs={{2,0},{3,1},{6,4},{7,5},{8,10},{9,11},{12,14},{13,15},{18,16},{19,... | collective-permute-start | bytes 1179656 | tf_op jit(solution)/shard_map/ppermute | solution.py:408
  51.0 25.0 %collective-permute-start.10 = (bf16[40,64,128]{2,0,1:T(8,128)(2,1)S(1)}, bf16[40,64,128]{2,0,1:T(8,128)(2,1)S(1)}, u32[]{:S(2)}, u32[]{:S(2)}) collective-permute-start(bf16[40,64,128]{2,0,1:T(8,128)(2,1)S(1)} %get-tuple-element.27), channel_id=1, source_target_pairs={{0,0},{1,4},{2,8},{3,12},{4,1},{5,5},{6,9},{7,13},{8,2},{9,6},{10,... | collective-permute-start | bytes 1966088 | tf_op jit(solution)/shard_map/ppermute | solution.py:408
  55.1 20.8 %collective-permute-start.9 = (bf16[24,64,128]{2,0,1:T(8,128)(2,1)S(1)}, bf16[24,64,128]{2,0,1:T(8,128)(2,1)S(1)}, u32[]{:S(2)}, u32[]{:S(2)}) collective-permute-start(bf16[24,64,128]{2,0,1:T(8,128)(2,1)S(1)} %get-tuple-element.29), channel_id=1, source_target_pairs={{0,0},{1,4},{4,1},{5,5},{10,10},{11,14},{14,11},{15,15},{16,16},{1... | collective-permute-start | bytes 1179656 | tf_op jit(solution)/shard_map/ppermute | solution.py:408
  61.2 15.1 %collective-permute-start.8 = (bf16[24,64,128]{2,0,1:T(8,128)(2,1)S(1)}, bf16[24,64,128]{2,0,1:T(8,128)(2,1)S(1)}, u32[]{:S(2)}, u32[]{:S(2)}) collective-permute-start(bf16[24,64,128]{2,0,1:T(8,128)(2,1)S(1)} %collective-permute-done.7), channel_id=1, source_target_pairs={{0,8},{1,12},{4,9},{5,13},{10,2},{11,6},{14,3},{15,7},{16,24},{17,... | collective-permute-start | bytes 1179656 | tf_op jit(solution)/shard_map/ppermute | solution.py:408
  76.6 15.9 %collective-permute-start.12 = (bf16[64,128]{1,0:T(8,128)(2,1)S(1)}, bf16[64,128]{1,0:T(8,128)(2,1)S(1)}, u32[]{:S(2)}, u32[]{:S(2)}) collective-permute-start(bf16[64,128]{1,0:T(8,128)(2,1)S(1)} %fusion.3), channel_id=1, source_target_pairs={{1,0},{2,1},{3,2},{5,4},{6,5},{7,6},{9,8},{10,9},{11,10},{13,12},{... | collective-permute-start | bytes 49160 | tf_op jit(solution)/shard_map/ppermute | solution.py:457
  78.6 14.6 %collective-permute-start.11 = (bf16[64,128]{1,0:T(8,128)(2,1)S(1)}, bf16[64,128]{1,0:T(8,128)(2,1)S(1)}, u32[]{:S(2)}, u32[]{:S(2)}) collective-permute-start(bf16[64,128]{1,0:T(8,128)(2,1)S(1)} %fusion.1), channel_id=1, source_target_pairs={{0,1},{1,2},{2,3},{4,5},{5,6},{6,7},{8,9},{9,10},{10,11},{12,13},{... | collective-permute-start | bytes 49160 | tf_op jit(solution)/shard_map/ppermute | solution.py:456
  93.2 5.3 %collective-permute-start.14 = (bf16[66,128]{1,0:T(8,128)(2,1)S(1)}, bf16[66,128]{1,0:T(8,128)(2,1)S(1)}, u32[]{:S(2)}, u32[]{:S(2)}) collective-permute-start(bf16[66,128]{1,0:T(8,128)(2,1)S(1)} %pad_maximum_fusion.6), channel_id=1, source_target_pairs={{4,0},{8,4},{12,8},{5,1},{9,5},{13,9},{6,2},{10,6},{14,10},{7,3},{... | collective-permute-start | bytes 50696 | tf_op jit(solution)/shard_map/ppermute | solution.py:460
  94.5 4.9 %collective-permute-start.13 = (bf16[66,128]{1,0:T(8,128)(2,1)S(1)}, bf16[66,128]{1,0:T(8,128)(2,1)S(1)}, u32[]{:S(2)}, u32[]{:S(2)}) collective-permute-start(bf16[66,128]{1,0:T(8,128)(2,1)S(1)} %pad_maximum_fusion.5), channel_id=1, source_target_pairs={{0,4},{4,8},{8,12},{1,5},{5,9},{9,13},{2,6},{6,10},{10,14},{3,7},{... | collective-permute-start | bytes 50696 | tf_op jit(solution)/shard_map/ppermute | solution.py:459

commit v6 on v5

--- a/solution.py
+++ b/solution.py
@@ -22,7 +22,7 @@
 
 def project_kernel(features, mask, left_weight, right_weight, left, right):
     depth, tokens = mask.shape
-    inner, width = left_weight.shape
+    width, inner = left_weight.shape
     group = lanes // width
 
     def chosen(rows, columns, test):
@@ -36,7 +36,12 @@
     own_block = chosen(group * inner, lanes, lambda a, b: a // inner == b // width)
     spread = []
     for weight in (left_weight, right_weight):
-        tall = dot(repeat_rows, weight[...]).astype(jnp.bfloat16)
+        tall = lax.dot_general(
+            repeat_rows,
+            weight[...],
+            (((1,), (1,)), ((), ())),
+            preferred_element_type=jnp.float32,
+        ).astype(jnp.bfloat16)
         spread.append(dot(tall, repeat_lanes).astype(jnp.bfloat16) * own_block)
     both = jnp.concatenate(spread, axis=1)
     kept = mask[...].astype(jnp.float32).astype(jnp.bfloat16)
@@ -62,7 +67,7 @@
         out_shape=[jax.ShapeDtypeStruct((depth, span), jnp.bfloat16)] * 2,
         compiler_params=kernel_params(8),
         cost_estimate=pl.CostEstimate(flops=1024, bytes_accessed=1024, transcendentals=0),
-    )(features.reshape(depth, -1), mask, left_weight, right_weight)
+    )(features.reshape(depth, -1), mask, left_weight.T, right_weight.T)
 
 
 def arrange_kernel(
@@ -203,7 +208,7 @@
             value = update[g * tokens_row : (g + 1) * tokens_row] * factor
             value = base[at].astype(jnp.float32) + value
             held[n * tokens_row : (n + 1) * tokens_row, :] = value.astype(jnp.bfloat16)
-    piece = strip if strip <= 32 else math.gcd(strip, 24)
+    piece = strip if strip <= 32 else strip // 2
     for start in range(0, strip, piece):
         at = slice(start * tokens_row, (start + piece) * tokens_row)
         result = transition_rows(held[at, :].astype(jnp.float32), gate_up[...], down[...])
@@ -353,8 +358,10 @@
         mirror_pairs = [(place_of(r, c), place_of(c, r)) for r, c in tiles]
         first = lax.ppermute(left_block, whole, mirror_pairs)
         col_side, col_places = [right_block], [row_index]
+        held_back, _ = lax.optimization_barrier((right_block, first))
         for step in range(1, row_count):
-            col_side.append(lax.ppermute(right_block, "row", shifts(row_count, -step)))
+            block = right_block if step in (1, row_count - 1) else held_back
+            col_side.append(lax.ppermute(block, "row", shifts(row_count, -step)))
             col_places.append((row_index + step) % row_count)
         row_side, row_places = [first], [col_index]
         for step in range(1, x_count):

time: 106 us -> 104 us (0.981)
  the two profiles are of different devices: /device:TPU:1 before, /device:TPU:14 now
where the time goes in v6:
time: 104 us
  waiting for transfers between devices  45.9 us (44%)
  starting transfers between devices  24.2 us (23%)
  Pallas kernels  18.1 us (17%)
  local copies, waits for them, and re-layouts  9.27 us (9%)
  other arithmetic  5.95 us (6%)
    ppermute x4, waiting for transfers between devices, on_device(): send = lambda value, pairs: lax.ppermute(value, whole, pairs)  25.1 us
    pallas_call x2, Pallas kernels, tile_strip(): pl.pallas_call(functools.partial(tile_kernel, first=first, width=width),...  11 us
    ppermute x1, waiting for transfers between devices, on_device(): first = lax.ppermute(left_block, whole, mirror_pairs)  9.89 us
    ppermute x4, starting transfers between devices, on_device(): send = lambda value, pairs: lax.ppermute(value, whole, pairs)  6.13 us
    ppermute x1, starting transfers between devices, on_device(): bottom = lax.ppermute(border(0, first_line), 'row', back(row_count))  4.87 us
    ppermute x3, waiting for transfers between devices, on_device(): col_side.append(lax.ppermute(block, 'row', shifts(row_count, -step)))  4.69 us
    pallas_call x1, Pallas kernels, convolve(): pl.pallas_call(functools.partial(conv_kernel, parts=[tuple(range(len(part...  4.21 us
    unnamed x20, local copies, waits for them, and re-layouts  4.13 us
  transfers between devices with their start and end apart: 15, of which 6 were waited for; matrix products, arithmetic and copies ran while one was open for 11% of the time, Pallas kernels for 0%

profile of v6, /device:TPU:14, one launch (start us, length us, event | category | flops | bytes accessed | tf_op | source)
XLA Modules:
  0.0 103.9 jit_solution(635725574918711126)
XLA Ops:
  0.0 1.5 %reshape.46.features = bf16[32,4096]{1,0:T(8,128)(2,1)S(1)} reshape(bf16[32,64,64]{2,1,0:T(8,128)(2,1)} %param.12) | data formatting | bytes 524288 | tf_op jit(solution)/shard_map/reshape | solution.py:70
  5.1 1.6 %collective-permute-start.6 = (bf16[32,2176]{1,0:T(8,128)(2,1)S(1)}, bf16[32,2176]{1,0:T(8,128)(2,1)S(1)}, u32[]{:S(2)}, u32[]{:S(2)}) collective-permute-start(bf16[32,2176]{1,0:T(8,128)(2,1)S(1)} %get-tuple-element.14.refs_4_), channel_id=1, source_target_pairs={{0,4},{4,8},{8,12},{12,0},{1,5},{5,9},{9,13},{13,1},{2,6},{6,10},{... | collective-permute-start | bytes 417800 | tf_op jit(solution)/shard_map/ppermute | solution.py:364
  6.6 2.3 %collective-permute-start = (bf16[32,2176]{1,0:T(8,128)(2,1)S(1)}, bf16[32,2176]{1,0:T(8,128)(2,1)S(1)}, u32[]{:S(2)}, u32[]{:S(2)}) collective-permute-start(bf16[32,2176]{1,0:T(8,128)(2,1)S(1)} %get-tuple-element.12), channel_id=1, source_target_pairs={{0,0},{1,4},{2,8},{3,12},{4,1},{5,5},{6,9},{7,13},{8,2},{9,6},{10,... | collective-permute-start | bytes 417800 | tf_op jit(solution)/shard_map/ppermute | solution.py:359
  10.1 9.9 %collective-permute-done.refs_0_ = bf16[32,2176]{1,0:T(8,128)(2,1)S(1)} collective-permute-done((bf16[32,2176]{1,0:T(8,128)(2,1)S(1)}, bf16[32,2176]{1,0:T(8,128)(2,1)S(1)}, u32[]{:S(2)}, u32[]{:S(2)}) %collective-permute-start) | collective-permute-done | bytes 139296 | tf_op jit(solution)/shard_map/ppermute | solution.py:359
  20.6 1.9 %copy.39 = bf16[64,64,128]{2,0,1:T(8,128)(2,1)S(1)} copy(bf16[64,64,128]{2,1,0:T(8,128)(2,1)} %param.11) | data formatting | bytes 2097152 | tf_op args[0]
  22.6 1.6 %pad_maximum_fusion.1 = (bf16[8,4,32,128]{3,2,1,0:T(8,128)(2,1)S(1)}, bf16[8,4,32,128]{3,2,1,0:T(8,128)(2,1)}) fusion(bf16[8,3,32,128]{3,2,1,0:T(8,128)(2,1)S(1)} %get-tuple-element.35, bf16[8,1,32,128]{3,2,1,0:T(8,128)(2,1)} %get-tuple-element.33, bf16[8,1,32,128]{3,2,1,0:T(8,128)(2,1)} %get-tuple-element.34, bf16[8,3,32,128]{3,2,1,0:T(8,128)(2,1)S(1)} %get-tuple-element.36), kind=kLoop, calls=%fused_computation.3 | loop fusion | flops 262144 | bytes 1048576 | tf_op jit(solution)/shard_map/jit(_roll_static)/concatenate | solution.py:388
  24.2 2.0 %collective-permute-start.5 = (bf16[32,2176]{1,0:T(8,128)(2,1)S(1)}, bf16[32,2176]{1,0:T(8,128)(2,1)S(1)}, u32[]{:S(2)}, u32[]{:S(2)}) collective-permute-start(bf16[32,2176]{1,0:T(8,128)(2,1)S(1)} %get-tuple-element.14.refs_4_), channel_id=1, source_target_pairs={{0,8},{4,12},{8,0},{12,4},{1,9},{5,13},{9,1},{13,5},{2,10},{6,14},... | collective-permute-start | bytes 417800 | tf_op jit(solution)/shard_map/ppermute | solution.py:364
  28.2 4.7 %collective-permute-done.5.refs_6_ = bf16[32,2176]{1,0:T(8,128)(2,1)S(1)} collective-permute-done((bf16[32,2176]{1,0:T(8,128)(2,1)S(1)}, bf16[32,2176]{1,0:T(8,128)(2,1)S(1)}, u32[]{:S(2)}, u32[]{:S(2)}) %collective-permute-start.5) | collective-permute-done | bytes 139296 | tf_op jit(solution)/shard_map/ppermute | solution.py:364
  32.9 2.0 %shard_map.110 = (bf16[2048,128]{1,0:T(8,128)(2,1)S(1)}, bf16[4,128,2048]{2,1,0:T(8,128)(2,1)S(1)}, f32[8,64,128]{2,1,0:T(8,128)S(1)}) custom-call(s32[8]{0:T(128)S(1)} %broadcast_multiply_fusion.1.places, bf16[32,2176]{1,0:T(8,128)(2,1)S(1)} %collective-permute-done.refs_0_, bf16[32,2176]{1,0:T(8,128)(2,1)S(1)} %collective-permute-done.1.refs_1_, ...), custom_call_target="tpu_custom_call" | custom-call | flops 1024 | bytes 1024 | tf_op jit(solution)/shard_map/pallas_call | solution.py:126
  34.9 4.1 %shard_map.111 = bf16[24,64,128]{2,1,0:T(8,128)(2,1)S(1)} custom-call(bf16[2048,128]{1,0:T(8,128)(2,1)S(1)} %get-tuple-element.18.row_side, bf16[4,128,2048]{2,1,0:T(8,128)(2,1)S(1)} %get-tuple-element.16.lane_side, f32[8,64,128]{2,1,0:T(8,128)S(1)} %get-tuple-element.17.scale, bf16[64,64,128]{2,1,0:T(8,128)(2,1)S(1)} %bitcast.59, ...), custom_call_target="tpu_custom_call" | custom-call | flops 1024 | bytes 1024 | tf_op jit(solution)/shard_map/pallas_call | solution.py:223
  39.3 7.0 %shard_map.112 = bf16[40,64,128]{2,1,0:T(8,128)(2,1)S(1)} custom-call(bf16[2048,128]{1,0:T(8,128)(2,1)S(1)} %get-tuple-element.18.row_side, bf16[4,128,2048]{2,1,0:T(8,128)(2,1)S(1)} %get-tuple-element.16.lane_side, f32[8,64,128]{2,1,0:T(8,128)S(1)} %get-tuple-element.17.scale, bf16[64,64,128]{2,1,0:T(8,128)(2,1)S(1)} %bitcast.60, ...), custom_call_target="tpu_custom_call" | custom-call | flops 1024 | bytes 1024 | tf_op jit(solution)/shard_map/pallas_call | solution.py:223
  46.3 2.2 %collective-permute-start.7 = (bf16[24,64,128]{2,0,1:T(8,128)(2,1)S(1)}, bf16[24,64,128]{2,0,1:T(8,128)(2,1)S(1)}, u32[]{:S(2)}, u32[]{:S(2)}) collective-permute-start(bf16[24,64,128]{2,0,1:T(8,128)(2,1)S(1)} %get-tuple-element.31), channel_id=1, source_target_pairs={{2,0},{3,1},{6,4},{7,5},{8,10},{9,11},{12,14},{13,15},{18,16},{19,... | collective-permute-start | bytes 1179656 | tf_op jit(solution)/shard_map/ppermute | solution.py:415
  49.1 2.0 %collective-permute-start.10 = (bf16[40,64,128]{2,0,1:T(8,128)(2,1)S(1)}, bf16[40,64,128]{2,0,1:T(8,128)(2,1)S(1)}, u32[]{:S(2)}, u32[]{:S(2)}) collective-permute-start(bf16[40,64,128]{2,0,1:T(8,128)(2,1)S(1)} %get-tuple-element.29), channel_id=1, source_target_pairs={{0,0},{1,4},{2,8},{3,12},{4,1},{5,5},{6,9},{7,13},{8,2},{9,6},{10,... | collective-permute-start | bytes 1966088 | tf_op jit(solution)/shard_map/ppermute | solution.py:415
  53.0 1.3 %multiply_multiply_fusion.3 = (f32[64]{0:T(128)S(1)}, f32[64]{0:T(128)S(1)}) fusion(f32[]{:T(128)} %bitcast.20, s32[64]{0:T(128)S(1)} %get-tuple-element.22.valid_i, f32[]{:T(128)} %bitcast.27), kind=kLoop, calls=%fused_computation.40 | loop fusion | flops 320 | bytes 776 | tf_op jit(solution)/shard_map/mul | solution.py:457
  54.2 2.9 %collective-permute-done.7 = bf16[24,64,128]{2,0,1:T(8,128)(2,1)S(1)} collective-permute-done((bf16[24,64,128]{2,0,1:T(8,128)(2,1)S(1)}, bf16[24,64,128]{2,0,1:T(8,128)(2,1)S(1)}, u32[]{:S(2)}, u32[]{:S(2)}) %collective-permute-start.7) | collective-permute-done | bytes 393248 | tf_op jit(solution)/shard_map/ppermute | solution.py:415
  57.1 1.3 %collective-permute-start.8 = (bf16[24,64,128]{2,0,1:T(8,128)(2,1)S(1)}, bf16[24,64,128]{2,0,1:T(8,128)(2,1)S(1)}, u32[]{:S(2)}, u32[]{:S(2)}) collective-permute-start(bf16[24,64,128]{2,0,1:T(8,128)(2,1)S(1)} %collective-permute-done.7), channel_id=1, source_target_pairs={{0,8},{1,12},{4,9},{5,13},{10,2},{11,6},{14,3},{15,7},{16,24},{17,... | collective-permute-start | bytes 1179656 | tf_op jit(solution)/shard_map/ppermute | solution.py:415
  59.2 22.3 %collective-permute-done.10 = bf16[40,64,128]{2,0,1:T(8,128)(2,1)S(1)} collective-permute-done((bf16[40,64,128]{2,0,1:T(8,128)(2,1)S(1)}, bf16[40,64,128]{2,0,1:T(8,128)(2,1)S(1)}, u32[]{:S(2)}, u32[]{:S(2)}) %collective-permute-start.10) | collective-permute-done | bytes 655392 | tf_op jit(solution)/shard_map/ppermute | solution.py:415
  81.9 1.9 %collective-permute-start.12 = (bf16[64,128]{1,0:T(8,128)(2,1)S(1)}, bf16[64,128]{1,0:T(8,128)(2,1)S(1)}, u32[]{:S(2)}, u32[]{:S(2)}) collective-permute-start(bf16[64,128]{1,0:T(8,128)(2,1)S(1)} %fusion.3), channel_id=1, source_target_pairs={{1,0},{2,1},{3,2},{5,4},{6,5},{7,6},{9,8},{10,9},{11,10},{13,12},{... | collective-permute-start | bytes 49160 | tf_op jit(solution)/shard_map/ppermute | solution.py:464
  83.9 2.4 %collective-permute-start.11 = (bf16[64,128]{1,0:T(8,128)(2,1)S(1)}, bf16[64,128]{1,0:T(8,128)(2,1)S(1)}, u32[]{:S(2)}, u32[]{:S(2)}) collective-permute-start(bf16[64,128]{1,0:T(8,128)(2,1)S(1)} %fusion.1), channel_id=1, source_target_pairs={{0,1},{1,2},{2,3},{4,5},{5,6},{6,7},{8,9},{9,10},{10,11},{12,13},{... | collective-permute-start | bytes 49160 | tf_op jit(solution)/shard_map/ppermute | solution.py:463
  86.5 2.4 %collective-permute-done.11 = bf16[64,128]{1,0:T(8,128)(2,1)S(1)} collective-permute-done((bf16[64,128]{1,0:T(8,128)(2,1)S(1)}, bf16[64,128]{1,0:T(8,128)(2,1)S(1)}, u32[]{:S(2)}, u32[]{:S(2)}) %collective-permute-start.11) | collective-permute-done | bytes 16416 | tf_op jit(solution)/shard_map/ppermute | solution.py:463
  89.0 4.9 %collective-permute-start.14 = (bf16[66,128]{1,0:T(8,128)(2,1)S(1)}, bf16[66,128]{1,0:T(8,128)(2,1)S(1)}, u32[]{:S(2)}, u32[]{:S(2)}) collective-permute-start(bf16[66,128]{1,0:T(8,128)(2,1)S(1)} %pad_maximum_fusion.6), channel_id=1, source_target_pairs={{4,0},{8,4},{12,8},{5,1},{9,5},{13,9},{6,2},{10,6},{14,10},{7,3},{... | collective-permute-start | bytes 50696 | tf_op jit(solution)/shard_map/ppermute | solution.py:467
  93.9 1.9 %collective-permute-start.13 = (bf16[66,128]{1,0:T(8,128)(2,1)S(1)}, bf16[66,128]{1,0:T(8,128)(2,1)S(1)}, u32[]{:S(2)}, u32[]{:S(2)}) collective-permute-start(bf16[66,128]{1,0:T(8,128)(2,1)S(1)} %pad_maximum_fusion.5), channel_id=1, source_target_pairs={{0,4},{4,8},{8,12},{1,5},{5,9},{9,13},{2,6},{6,10},{10,14},{3,7},{... | collective-permute-start | bytes 50696 | tf_op jit(solution)/shard_map/ppermute | solution.py:466
  95.9 3.7 %collective-permute-done.13 = bf16[66,128]{1,0:T(8,128)(2,1)S(1)} collective-permute-done((bf16[66,128]{1,0:T(8,128)(2,1)S(1)}, bf16[66,128]{1,0:T(8,128)(2,1)S(1)}, u32[]{:S(2)}, u32[]{:S(2)}) %collective-permute-start.13) | collective-permute-done | bytes 16928 | tf_op jit(solution)/shard_map/ppermute | solution.py:466
  99.7 4.2 %shard_map.113 = bf16[64,64,128]{2,1,0:T(8,128)(2,1)} custom-call(s32[64]{0:T(128)S(1)} %get-tuple-element.22.valid_i, bf16[64,64,128]{2,1,0:T(8,128)(2,1)S(1)} %bitcast.62, bf16[24,64,128]{2,1,0:T(8,128)(2,1)S(1)} %copy.29.refs_0_, bf16[24,64,128]{2,1,0:T(8,128)(2,1)S(1)} %copy.30.refs_1_, bf16[40,64,128]{2,1,0:T(8,128)(2,1)S(1)} %copy.31.refs_2_, ...), custom_call_target="tpu_custom_call" | custom-call | flops 1207959552 | bytes 3145728 | tf_op jit(solution)/shard_map/pallas_call | solution.py:292
  (75 shorter events, 11.4 us)
Async XLA Ops:
  0.0 9.0 %copy-start.4 = (bf16[1024,128]{1,0:T(8,128)(2,1)S(1)}, bf16[1024,128]{1,0:T(8,128)(2,1)}, u32[]{:S(2)}) copy-start(bf16[1024,128]{1,0:T(8,128)(2,1)} %param.17) | copy-start | bytes 786436
  0.0 9.9 %copy-start.6 = (bf16[128,512]{1,0:T(8,128)(2,1)S(1)}, bf16[128,512]{1,0:T(8,128)(2,1)}, u32[]{:S(2)}) copy-start(bf16[128,512]{1,0:T(8,128)(2,1)} %param.18) | copy-start | bytes 393220
  1.6 0.7 copy-start.1
  2.3 0.7 copy-start.2
  3.0 0.7 copy-start.3
  4.5 5.4 %copy-start.8 = (s32[256]{0:T(256)S(1)}, s32[256]{0:T(256)}, u32[]{:S(2)}) copy-start(s32[256]{0:T(256)} %param.14) | copy-start | bytes 3076
  4.6 5.5 %copy-start.7 = (bf16[128,512]{1,0:T(8,128)(2,1)S(1)}, bf16[128,512]{1,0:T(8,128)(2,1)}, u32[]{:S(2)}) copy-start(bf16[128,512]{1,0:T(8,128)(2,1)} %param.19) | copy-start | bytes 393220
  4.6 23.6 %collective-permute-start.4 = (bf16[32,2176]{1,0:T(8,128)(2,1)S(1)}, bf16[32,2176]{1,0:T(8,128)(2,1)S(1)}, u32[]{:S(2)}, u32[]{:S(2)}) collective-permute-start(bf16[32,2176]{1,0:T(8,128)(2,1)S(1)} %get-tuple-element.14.refs_4_), channel_id=1, source_target_pairs={{0,12},{4,0},{8,4},{12,8},{1,13},{5,1},{9,5},{13,9},{2,14},{6,2},{... | collective-permute-start | bytes 417800 | tf_op jit(solution)/shard_map/ppermute | solution.py:364
  5.1 23.1 %collective-permute-start.6 = (bf16[32,2176]{1,0:T(8,128)(2,1)S(1)}, bf16[32,2176]{1,0:T(8,128)(2,1)S(1)}, u32[]{:S(2)}, u32[]{:S(2)}) collective-permute-start(bf16[32,2176]{1,0:T(8,128)(2,1)S(1)} %get-tuple-element.14.refs_4_), channel_id=1, source_target_pairs={{0,4},{4,8},{8,12},{12,0},{1,5},{5,9},{9,13},{13,1},{2,6},{6,10},{... | collective-permute-start | bytes 417800 | tf_op jit(solution)/shard_map/ppermute | solution.py:364
  6.6 13.3 %collective-permute-start = (bf16[32,2176]{1,0:T(8,128)(2,1)S(1)}, bf16[32,2176]{1,0:T(8,128)(2,1)S(1)}, u32[]{:S(2)}, u32[]{:S(2)}) collective-permute-start(bf16[32,2176]{1,0:T(8,128)(2,1)S(1)} %get-tuple-element.12), channel_id=1, source_target_pairs={{0,0},{1,4},{2,8},{3,12},{4,1},{5,5},{6,9},{7,13},{8,2},{9,6},{10,... | collective-permute-start | bytes 417800 | tf_op jit(solution)/shard_map/ppermute | solution.py:359
  20.0 6.6 %collective-permute-start.1 = (bf16[32,2176]{1,0:T(8,128)(2,1)S(1)}, bf16[32,2176]{1,0:T(8,128)(2,1)S(1)}, u32[]{:S(2)}, u32[]{:S(2)}) collective-permute-start(bf16[32,2176]{1,0:T(8,128)(2,1)S(1)} %collective-permute-done.refs_0_), channel_id=1, source_target_pairs={{0,2},{2,0},{1,3},{3,1},{4,6},{6,4},{5,7},{7,5},{8,10},{10,8},{9,1... | collective-permute-start | bytes 417800 | tf_op jit(solution)/shard_map/ppermute | solution.py:368
  20.6 6.1 %copy-start.5 = (bf16[3,3,128,128]{3,2,1,0:T(8,128)(2,1)S(1)}, bf16[3,3,128,128]{3,2,1,0:T(8,128)(2,1)}, u32[]{:S(2)}) copy-start(bf16[3,3,128,128]{3,2,1,0:T(8,128)(2,1)} %param.21) | copy-start | bytes 884740
  24.2 8.7 %collective-permute-start.5 = (bf16[32,2176]{1,0:T(8,128)(2,1)S(1)}, bf16[32,2176]{1,0:T(8,128)(2,1)S(1)}, u32[]{:S(2)}, u32[]{:S(2)}) collective-permute-start(bf16[32,2176]{1,0:T(8,128)(2,1)S(1)} %get-tuple-element.14.refs_4_), channel_id=1, source_target_pairs={{0,8},{4,12},{8,0},{12,4},{1,9},{5,13},{9,1},{13,5},{2,10},{6,14},... | collective-permute-start | bytes 417800 | tf_op jit(solution)/shard_map/ppermute | solution.py:364
  26.2 2.0 %collective-permute-start.2 = (bf16[32,2176]{1,0:T(8,128)(2,1)S(1)}, bf16[32,2176]{1,0:T(8,128)(2,1)S(1)}, u32[]{:S(2)}, u32[]{:S(2)}) collective-permute-start(bf16[32,2176]{1,0:T(8,128)(2,1)S(1)} %collective-permute-done.refs_0_), channel_id=1, source_target_pairs={{0,1},{1,0},{2,3},{3,2},{4,5},{5,4},{6,7},{7,6},{8,9},{9,8},{10,11... | collective-permute-start | bytes 417800 | tf_op jit(solution)/shard_map/ppermute | solution.py:372
  26.6 6.3 %collective-permute-start.3 = (bf16[32,2176]{1,0:T(8,128)(2,1)S(1)}, bf16[32,2176]{1,0:T(8,128)(2,1)S(1)}, u32[]{:S(2)}, u32[]{:S(2)}) collective-permute-start(bf16[32,2176]{1,0:T(8,128)(2,1)S(1)} %collective-permute-done.1.refs_1_), channel_id=1, source_target_pairs={{0,1},{1,0},{2,3},{3,2},{4,5},{5,4},{6,7},{7,6},{8,9},{9,8},{10,11... | collective-permute-start | bytes 417800 | tf_op jit(solution)/shard_map/ppermute | solution.py:372
  27.0 7.9 %copy-start = (bf16[512,128]{1,0:T(8,128)(2,1)S(1)}, bf16[512,128]{1,0:T(8,128)(2,1)}, u32[]{:S(2)}) copy-start(bf16[512,128]{1,0:T(8,128)(2,1)} %down.3) | copy-start | bytes 393220
  46.3 10.8 %collective-permute-start.7 = (bf16[24,64,128]{2,0,1:T(8,128)(2,1)S(1)}, bf16[24,64,128]{2,0,1:T(8,128)(2,1)S(1)}, u32[]{:S(2)}, u32[]{:S(2)}) collective-permute-start(bf16[24,64,128]{2,0,1:T(8,128)(2,1)S(1)} %get-tuple-element.31), channel_id=1, source_target_pairs={{2,0},{3,1},{6,4},{7,5},{8,10},{9,11},{12,14},{13,15},{18,16},{19,... | collective-permute-start | bytes 1179656 | tf_op jit(solution)/shard_map/ppermute | solution.py:415
  49.1 32.4 %collective-permute-start.10 = (bf16[40,64,128]{2,0,1:T(8,128)(2,1)S(1)}, bf16[40,64,128]{2,0,1:T(8,128)(2,1)S(1)}, u32[]{:S(2)}, u32[]{:S(2)}) collective-permute-start(bf16[40,64,128]{2,0,1:T(8,128)(2,1)S(1)} %get-tuple-element.29), channel_id=1, source_target_pairs={{0,0},{1,4},{2,8},{3,12},{4,1},{5,5},{6,9},{7,13},{8,2},{9,6},{10,... | collective-permute-start | bytes 1966088 | tf_op jit(solution)/shard_map/ppermute | solution.py:415
  52.3 6.7 %collective-permute-start.9 = (bf16[24,64,128]{2,0,1:T(8,128)(2,1)S(1)}, bf16[24,64,128]{2,0,1:T(8,128)(2,1)S(1)}, u32[]{:S(2)}, u32[]{:S(2)}) collective-permute-start(bf16[24,64,128]{2,0,1:T(8,128)(2,1)S(1)} %get-tuple-element.31), channel_id=1, source_target_pairs={{0,0},{1,4},{4,1},{5,5},{10,10},{11,14},{14,11},{15,15},{16,16},{1... | collective-permute-start | bytes 1179656 | tf_op jit(solution)/shard_map/ppermute | solution.py:415
  57.1 24.6 %collective-permute-start.8 = (bf16[24,64,128]{2,0,1:T(8,128)(2,1)S(1)}, bf16[24,64,128]{2,0,1:T(8,128)(2,1)S(1)}, u32[]{:S(2)}, u32[]{:S(2)}) collective-permute-start(bf16[24,64,128]{2,0,1:T(8,128)(2,1)S(1)} %collective-permute-done.7), channel_id=1, source_target_pairs={{0,8},{1,12},{4,9},{5,13},{10,2},{11,6},{14,3},{15,7},{16,24},{17,... | collective-permute-start | bytes 1179656 | tf_op jit(solution)/shard_map/ppermute | solution.py:415
  81.9 4.6 %collective-permute-start.12 = (bf16[64,128]{1,0:T(8,128)(2,1)S(1)}, bf16[64,128]{1,0:T(8,128)(2,1)S(1)}, u32[]{:S(2)}, u32[]{:S(2)}) collective-permute-start(bf16[64,128]{1,0:T(8,128)(2,1)S(1)} %fusion.3), channel_id=1, source_target_pairs={{1,0},{2,1},{3,2},{5,4},{6,5},{7,6},{9,8},{10,9},{11,10},{13,12},{... | collective-permute-start | bytes 49160 | tf_op jit(solution)/shard_map/ppermute | solution.py:464
  83.9 5.0 %collective-permute-start.11 = (bf16[64,128]{1,0:T(8,128)(2,1)S(1)}, bf16[64,128]{1,0:T(8,128)(2,1)S(1)}, u32[]{:S(2)}, u32[]{:S(2)}) collective-permute-start(bf16[64,128]{1,0:T(8,128)(2,1)S(1)} %fusion.1), channel_id=1, source_target_pairs={{0,1},{1,2},{2,3},{4,5},{5,6},{6,7},{8,9},{9,10},{10,11},{12,13},{... | collective-permute-start | bytes 49160 | tf_op jit(solution)/shard_map/ppermute | solution.py:463
  89.0 6.8 %collective-permute-start.14 = (bf16[66,128]{1,0:T(8,128)(2,1)S(1)}, bf16[66,128]{1,0:T(8,128)(2,1)S(1)}, u32[]{:S(2)}, u32[]{:S(2)}) collective-permute-start(bf16[66,128]{1,0:T(8,128)(2,1)S(1)} %pad_maximum_fusion.6), channel_id=1, source_target_pairs={{4,0},{8,4},{12,8},{5,1},{9,5},{13,9},{6,2},{10,6},{14,10},{7,3},{... | collective-permute-start | bytes 50696 | tf_op jit(solution)/shard_map/ppermute | solution.py:467
  93.9 5.7 %collective-permute-start.13 = (bf16[66,128]{1,0:T(8,128)(2,1)S(1)}, bf16[66,128]{1,0:T(8,128)(2,1)S(1)}, u32[]{:S(2)}, u32[]{:S(2)}) collective-permute-start(bf16[66,128]{1,0:T(8,128)(2,1)S(1)} %pad_maximum_fusion.5), channel_id=1, source_target_pairs={{0,4},{4,8},{8,12},{1,5},{5,9},{9,13},{2,6},{6,10},{10,14},{3,7},{... | collective-permute-start | bytes 50696 | tf_op jit(solution)/shard_map/ppermute | solution.py:466

commit v7 on v6

--- a/solution.py
+++ b/solution.py
@@ -405,7 +405,7 @@
     back = lambda size: [(n + 1, n) for n in range(size - 1)]
 
     if square and cols_dev % (8 * unit) == 0 and x_count > 1:
-        part = cols_dev // 8
+        part = cols_dev // 16
         host = lambda r, c: place_of(r, (r // core_count) * core_count + c % core_count)
         away = [(r, c) for r, c in tiles if r // core_count != c // core_count]
         near = [(r, c) for r, c in tiles if r // core_count == c // core_count]
@@ -413,14 +413,16 @@
         from_host = [(host(r, c), place_of(c, r)) for r, c in away]
         beside_pairs = [(place_of(r, c), place_of(c, r)) for r, c in near]
         send = lambda value, pairs: lax.ppermute(value, whole, pairs)
-        opening = run(0, 3 * part)
+        opening = run(0, 7 * part)
         hosted = send(opening, to_host)
         mirrored_near = send(opening, beside_pairs)
-        rest = run(3 * part, 5 * part, opening)
-        mirrored_rest = send(rest, mirror_pairs)
+        middle = run(7 * part, 4 * part, opening)
+        mirrored_middle = send(middle, mirror_pairs)
         mirrored_away = send(hosted, from_host)
-        turned = jnp.concatenate([opening, rest], axis=0)
-        mirrored = [[mirrored_away, mirrored_near], [mirrored_rest]]
+        last = run(11 * part, 5 * part, (middle, hosted))
+        mirrored_last = send(last, mirror_pairs)
+        turned = jnp.concatenate([opening, middle, last], axis=0)
+        mirrored = [[mirrored_away, mirrored_near], [mirrored_middle], [mirrored_last]]
     else:
         turned = run(0, cols_dev)
         share = rows_dev // col_count

time: 104 us -> 114 us (1.096)
  the two profiles are of different devices: /device:TPU:14 before, /device:TPU:1 now
where the time goes in v7:
time: 114 us; the launch traced here: 111 us
  starting transfers between devices  63.3 us (56%)
  Pallas kernels  18.4 us (16%)
  waiting for transfers between devices  16.4 us (14%)
  local copies, waits for them, and re-layouts  8.36 us (7%)
  other arithmetic  4.43 us (4%)
    ppermute x5, starting transfers between devices, on_device(): send = lambda value, pairs: lax.ppermute(value, whole, pairs)  20.5 us
    ppermute x1, starting transfers between devices, on_device(): left = lax.ppermute(last_side, plane, ahead(col_count))  15.2 us
    pallas_call x3, Pallas kernels, tile_strip(): pl.pallas_call(functools.partial(tile_kernel, first=first, width=width),...  11.2 us
    ppermute x5, waiting for transfers between devices, on_device(): send = lambda value, pairs: lax.ppermute(value, whole, pairs)  10.1 us
    ppermute x3, starting transfers between devices, on_device(): col_side.append(lax.ppermute(block, 'row', shifts(row_count, -step)))  7.19 us
    ppermute x1, starting transfers between devices, on_device(): right = lax.ppermute(first_side, plane, back(col_count))  6.75 us
    ppermute x1, waiting for transfers between devices, on_device(): first = lax.ppermute(left_block, whole, mirror_pairs)  4.96 us
    pallas_call x1, Pallas kernels, convolve(): pl.pallas_call(functools.partial(conv_kernel, parts=[tuple(range(len(part...  4.21 us
  transfers between devices with their start and end apart: 16, of which 5 were waited for; matrix products, arithmetic and copies ran while one was open for 8% of the time, Pallas kernels for 6%

profile of v7, /device:TPU:1, one launch (start us, length us, event | category | flops | bytes accessed | tf_op | source)
XLA Modules:
  0.0 111.5 jit_solution(3479985241807626292)
XLA Ops:
  0.0 1.6 %reshape.46.features = bf16[32,4096]{1,0:T(8,128)(2,1)S(1)} reshape(bf16[32,64,64]{2,1,0:T(8,128)(2,1)} %param.12) | data formatting | bytes 524288 | tf_op jit(solution)/shard_map/reshape | solution.py:70
  4.6 4.2 %collective-permute-start.4 = (bf16[32,2176]{1,0:T(8,128)(2,1)S(1)}, bf16[32,2176]{1,0:T(8,128)(2,1)S(1)}, u32[]{:S(2)}, u32[]{:S(2)}) collective-permute-start(bf16[32,2176]{1,0:T(8,128)(2,1)S(1)} %get-tuple-element.15.refs_4_), channel_id=1, source_target_pairs={{0,12},{4,0},{8,4},{12,8},{1,13},{5,1},{9,5},{13,9},{2,14},{6,2},{... | collective-permute-start | bytes 417800 | tf_op jit(solution)/shard_map/ppermute | solution.py:364
  8.8 2.5 %collective-permute-start = (bf16[32,2176]{1,0:T(8,128)(2,1)S(1)}, bf16[32,2176]{1,0:T(8,128)(2,1)S(1)}, u32[]{:S(2)}, u32[]{:S(2)}) collective-permute-start(bf16[32,2176]{1,0:T(8,128)(2,1)S(1)} %get-tuple-element.13), channel_id=1, source_target_pairs={{0,0},{1,4},{2,8},{3,12},{4,1},{5,5},{6,9},{7,13},{8,2},{9,6},{10,... | collective-permute-start | bytes 417800 | tf_op jit(solution)/shard_map/ppermute | solution.py:359
  12.7 5.0 %collective-permute-done.refs_0_ = bf16[32,2176]{1,0:T(8,128)(2,1)S(1)} collective-permute-done((bf16[32,2176]{1,0:T(8,128)(2,1)S(1)}, bf16[32,2176]{1,0:T(8,128)(2,1)S(1)}, u32[]{:S(2)}, u32[]{:S(2)}) %collective-permute-start) | collective-permute-done | bytes 139296 | tf_op jit(solution)/shard_map/ppermute | solution.py:359
  17.7 2.5 %collective-permute-start.1 = (bf16[32,2176]{1,0:T(8,128)(2,1)S(1)}, bf16[32,2176]{1,0:T(8,128)(2,1)S(1)}, u32[]{:S(2)}, u32[]{:S(2)}) collective-permute-start(bf16[32,2176]{1,0:T(8,128)(2,1)S(1)} %collective-permute-done.refs_0_), channel_id=1, source_target_pairs={{0,2},{2,0},{1,3},{3,1},{4,6},{6,4},{5,7},{7,5},{8,10},{10,8},{9,1... | collective-permute-start | bytes 417800 | tf_op jit(solution)/shard_map/ppermute | solution.py:368
  20.9 3.0 %collective-permute-start.5 = (bf16[32,2176]{1,0:T(8,128)(2,1)S(1)}, bf16[32,2176]{1,0:T(8,128)(2,1)S(1)}, u32[]{:S(2)}, u32[]{:S(2)}) collective-permute-start(bf16[32,2176]{1,0:T(8,128)(2,1)S(1)} %get-tuple-element.15.refs_4_), channel_id=1, source_target_pairs={{0,8},{4,12},{8,0},{12,4},{1,9},{5,13},{9,1},{13,5},{2,10},{6,14},... | collective-permute-start | bytes 417800 | tf_op jit(solution)/shard_map/ppermute | solution.py:364
  25.0 2.3 %collective-permute-start.3 = (bf16[32,2176]{1,0:T(8,128)(2,1)S(1)}, bf16[32,2176]{1,0:T(8,128)(2,1)S(1)}, u32[]{:S(2)}, u32[]{:S(2)}) collective-permute-start(bf16[32,2176]{1,0:T(8,128)(2,1)S(1)} %collective-permute-done.1.refs_1_), channel_id=1, source_target_pairs={{0,1},{1,0},{2,3},{3,2},{4,5},{5,4},{6,7},{7,6},{8,9},{9,8},{10,11... | collective-permute-start | bytes 417800 | tf_op jit(solution)/shard_map/ppermute | solution.py:372
  28.9 2.0 %shard_map.110 = (bf16[2048,128]{1,0:T(8,128)(2,1)S(1)}, bf16[4,128,2048]{2,1,0:T(8,128)(2,1)S(1)}, f32[8,64,128]{2,1,0:T(8,128)S(1)}) custom-call(s32[8]{0:T(128)S(1)} %broadcast_multiply_fusion.1.places, bf16[32,2176]{1,0:T(8,128)(2,1)S(1)} %collective-permute-done.refs_0_, bf16[32,2176]{1,0:T(8,128)(2,1)S(1)} %collective-permute-done.1.refs_1_, ...), custom_call_target="tpu_custom_call" | custom-call | flops 1024 | bytes 1024 | tf_op jit(solution)/shard_map/pallas_call | solution.py:126
  30.9 4.6 %shard_map.111 = bf16[28,64,128]{2,1,0:T(8,128)(2,1)S(1)} custom-call(bf16[2048,128]{1,0:T(8,128)(2,1)S(1)} %get-tuple-element.20.row_side, bf16[4,128,2048]{2,1,0:T(8,128)(2,1)S(1)} %get-tuple-element.17.lane_side, f32[8,64,128]{2,1,0:T(8,128)S(1)} %get-tuple-element.18.scale, bf16[64,64,128]{2,1,0:T(8,128)(2,1)S(1)} %bitcast.64, ...), custom_call_target="tpu_custom_call" | custom-call | flops 1024 | bytes 1024 | tf_op jit(solution)/shard_map/pallas_call | solution.py:223
  35.9 1.3 %collective-permute-start.7 = (bf16[28,64,128]{2,0,1:T(8,128)(2,1)S(1)}, bf16[28,64,128]{2,0,1:T(8,128)(2,1)S(1)}, u32[]{:S(2)}, u32[]{:S(2)}) collective-permute-start(bf16[28,64,128]{2,0,1:T(8,128)(2,1)S(1)} %copy.27), channel_id=1, source_target_pairs={{2,0},{3,1},{6,4},{7,5},{8,10},{9,11},{12,14},{13,15},{18,16},{19,... | collective-permute-start | bytes 1376264 | tf_op jit(solution)/shard_map/ppermute | solution.py:415
  37.8 5.1 %collective-permute-start.9 = (bf16[28,64,128]{2,0,1:T(8,128)(2,1)S(1)}, bf16[28,64,128]{2,0,1:T(8,128)(2,1)S(1)}, u32[]{:S(2)}, u32[]{:S(2)}) collective-permute-start(bf16[28,64,128]{2,0,1:T(8,128)(2,1)S(1)} %copy.27), channel_id=1, source_target_pairs={{0,0},{1,4},{4,1},{5,5},{10,10},{11,14},{14,11},{15,15},{16,16},{1... | collective-permute-start | bytes 1376264 | tf_op jit(solution)/shard_map/ppermute | solution.py:415
  43.0 3.1 %shard_map.112 = bf16[16,64,128]{2,1,0:T(8,128)(2,1)S(1)} custom-call(bf16[2048,128]{1,0:T(8,128)(2,1)S(1)} %get-tuple-element.20.row_side, bf16[4,128,2048]{2,1,0:T(8,128)(2,1)S(1)} %get-tuple-element.17.lane_side, f32[8,64,128]{2,1,0:T(8,128)S(1)} %get-tuple-element.18.scale, bf16[64,64,128]{2,1,0:T(8,128)(2,1)S(1)} %bitcast.65, ...), custom_call_target="tpu_custom_call" | custom-call | flops 1024 | bytes 1024 | tf_op jit(solution)/shard_map/pallas_call | solution.py:223
  46.3 1.9 %collective-permute-start.10 = (bf16[16,64,128]{2,0,1:T(8,128)(2,1)S(1)}, bf16[16,64,128]{2,0,1:T(8,128)(2,1)S(1)}, u32[]{:S(2)}, u32[]{:S(2)}) collective-permute-start(bf16[16,64,128]{2,0,1:T(8,128)(2,1)S(1)} %copy.28), channel_id=1, source_target_pairs={{0,0},{1,4},{2,8},{3,12},{4,1},{5,5},{6,9},{7,13},{8,2},{9,6},{10,... | collective-permute-start | bytes 786440 | tf_op jit(solution)/shard_map/ppermute | solution.py:415
  49.1 1.3 %multiply_multiply_fusion.3 = (f32[64]{0:T(128)S(1)}, f32[64]{0:T(128)S(1)}) fusion(f32[]{:T(128)} %bitcast.21, s32[64]{0:T(128)S(1)} %get-tuple-element.24.valid_i, f32[]{:T(128)} %bitcast.29), kind=kLoop, calls=%fused_computation.41 | loop fusion | flops 320 | bytes 776 | tf_op jit(solution)/shard_map/mul | solution.py:459
  50.4 4.1 %collective-permute-done.10 = bf16[16,64,128]{2,0,1:T(8,128)(2,1)S(1)} collective-permute-done((bf16[16,64,128]{2,0,1:T(8,128)(2,1)S(1)}, bf16[16,64,128]{2,0,1:T(8,128)(2,1)S(1)}, u32[]{:S(2)}, u32[]{:S(2)}) %collective-permute-start.10) | collective-permute-done | bytes 262176 | tf_op jit(solution)/shard_map/ppermute | solution.py:415
  54.5 3.5 %shard_map.113 = bf16[20,64,128]{2,1,0:T(8,128)(2,1)S(1)} custom-call(bf16[2048,128]{1,0:T(8,128)(2,1)S(1)} %get-tuple-element.20.row_side, bf16[4,128,2048]{2,1,0:T(8,128)(2,1)S(1)} %get-tuple-element.17.lane_side, f32[8,64,128]{2,1,0:T(8,128)S(1)} %get-tuple-element.18.scale, bf16[64,64,128]{2,1,0:T(8,128)(2,1)S(1)} %bitcast.66, ...), custom_call_target="tpu_custom_call" | custom-call | flops 1024 | bytes 1024 | tf_op jit(solution)/shard_map/pallas_call | solution.py:223
  58.3 2.0 %collective-permute-start.11 = (bf16[20,64,128]{2,0,1:T(8,128)(2,1)S(1)}, bf16[20,64,128]{2,0,1:T(8,128)(2,1)S(1)}, u32[]{:S(2)}, u32[]{:S(2)}) collective-permute-start(bf16[20,64,128]{2,0,1:T(8,128)(2,1)S(1)} %copy.29), channel_id=1, source_target_pairs={{0,0},{1,4},{2,8},{3,12},{4,1},{5,5},{6,9},{7,13},{8,2},{9,6},{10,... | collective-permute-start | bytes 983048 | tf_op jit(solution)/shard_map/ppermute | solution.py:415
  60.4 10.1 %collective-permute-start.8 = (bf16[28,64,128]{2,0,1:T(8,128)(2,1)S(1)}, bf16[28,64,128]{2,0,1:T(8,128)(2,1)S(1)}, u32[]{:S(2)}, u32[]{:S(2)}) collective-permute-start(bf16[28,64,128]{2,0,1:T(8,128)(2,1)S(1)} %collective-permute-done.7), channel_id=1, source_target_pairs={{0,8},{1,12},{4,9},{5,13},{10,2},{11,6},{14,3},{15,7},{16,24},{17,... | collective-permute-start | bytes 1376264 | tf_op jit(solution)/shard_map/ppermute | solution.py:415
  71.7 6.0 %collective-permute-done.8 = bf16[28,64,128]{2,0,1:T(8,128)(2,1)S(1)} collective-permute-done((bf16[28,64,128]{2,0,1:T(8,128)(2,1)S(1)}, bf16[28,64,128]{2,0,1:T(8,128)(2,1)S(1)}, u32[]{:S(2)}, u32[]{:S(2)}) %collective-permute-start.8) | collective-permute-done | bytes 458784 | tf_op jit(solution)/shard_map/ppermute | solution.py:415
  78.0 6.8 %collective-permute-start.13 = (bf16[64,128]{1,0:T(8,128)(2,1)S(1)}, bf16[64,128]{1,0:T(8,128)(2,1)S(1)}, u32[]{:S(2)}, u32[]{:S(2)}) collective-permute-start(bf16[64,128]{1,0:T(8,128)(2,1)S(1)} %fusion.3), channel_id=1, source_target_pairs={{1,0},{2,1},{3,2},{5,4},{6,5},{7,6},{9,8},{10,9},{11,10},{13,12},{... | collective-permute-start | bytes 49160 | tf_op jit(solution)/shard_map/ppermute | solution.py:466
  84.9 15.2 %collective-permute-start.12 = (bf16[64,128]{1,0:T(8,128)(2,1)S(1)}, bf16[64,128]{1,0:T(8,128)(2,1)S(1)}, u32[]{:S(2)}, u32[]{:S(2)}) collective-permute-start(bf16[64,128]{1,0:T(8,128)(2,1)S(1)} %fusion.1), channel_id=1, source_target_pairs={{0,1},{1,2},{2,3},{4,5},{5,6},{6,7},{8,9},{9,10},{10,11},{12,13},{... | collective-permute-start | bytes 49160 | tf_op jit(solution)/shard_map/ppermute | solution.py:465
  101.0 1.3 %collective-permute-start.15 = (bf16[66,128]{1,0:T(8,128)(2,1)S(1)}, bf16[66,128]{1,0:T(8,128)(2,1)S(1)}, u32[]{:S(2)}, u32[]{:S(2)}) collective-permute-start(bf16[66,128]{1,0:T(8,128)(2,1)S(1)} %pad_maximum_fusion.7), channel_id=1, source_target_pairs={{4,0},{8,4},{12,8},{5,1},{9,5},{13,9},{6,2},{10,6},{14,10},{7,3},{... | collective-permute-start | bytes 50696 | tf_op jit(solution)/shard_map/ppermute | solution.py:469
  102.3 4.0 %collective-permute-start.14 = (bf16[66,128]{1,0:T(8,128)(2,1)S(1)}, bf16[66,128]{1,0:T(8,128)(2,1)S(1)}, u32[]{:S(2)}, u32[]{:S(2)}) collective-permute-start(bf16[66,128]{1,0:T(8,128)(2,1)S(1)} %pad_maximum_fusion.6), channel_id=1, source_target_pairs={{0,4},{4,8},{8,12},{1,5},{5,9},{9,13},{2,6},{6,10},{10,14},{3,7},{... | collective-permute-start | bytes 50696 | tf_op jit(solution)/shard_map/ppermute | solution.py:468
  107.3 4.2 %shard_map.114 = bf16[64,64,128]{2,1,0:T(8,128)(2,1)} custom-call(s32[64]{0:T(128)S(1)} %get-tuple-element.24.valid_i, bf16[64,64,128]{2,1,0:T(8,128)(2,1)S(1)} %fusion.20.pair_two, bf16[28,64,128]{2,1,0:T(8,128)(2,1)S(1)} %copy.34.refs_0_, bf16[28,64,128]{2,1,0:T(8,128)(2,1)S(1)} %copy.35.refs_1_, bf16[16,64,128]{2,1,0:T(8,128)(2,1)S(1)} %copy.36.refs_2_, ...), custom_call_target="tpu_custom_call" | custom-call | flops 1207959552 | bytes 3145728 | tf_op jit(solution)/shard_map/pallas_call | solution.py:292
  (86 shorter events, 13.4 us)
Async XLA Ops:
  0.0 12.4 %copy-start.4 = (bf16[1024,128]{1,0:T(8,128)(2,1)S(1)}, bf16[1024,128]{1,0:T(8,128)(2,1)}, u32[]{:S(2)}) copy-start(bf16[1024,128]{1,0:T(8,128)(2,1)} %param.17) | copy-start | bytes 786436
  0.0 12.6 %copy-start.7 = (bf16[128,512]{1,0:T(8,128)(2,1)S(1)}, bf16[128,512]{1,0:T(8,128)(2,1)}, u32[]{:S(2)}) copy-start(bf16[128,512]{1,0:T(8,128)(2,1)} %param.18) | copy-start | bytes 393220
  0.0 12.6 %copy-start.9 = (s32[256]{0:T(256)S(1)}, s32[256]{0:T(256)}, u32[]{:S(2)}) copy-start(s32[256]{0:T(256)} %param.14) | copy-start | bytes 3076
  0.0 12.7 %copy-start.8 = (bf16[128,512]{1,0:T(8,128)(2,1)S(1)}, bf16[128,512]{1,0:T(8,128)(2,1)}, u32[]{:S(2)}) copy-start(bf16[128,512]{1,0:T(8,128)(2,1)} %param.19) | copy-start | bytes 393220
  1.6 0.7 copy-start.1
  4.6 23.4 %copy-start.5 = (bf16[64,64,128]{2,1,0:T(8,128)(2,1)S(1)}, bf16[64,64,128]{2,1,0:T(8,128)(2,1)}, u32[]{:S(2)}) copy-start(bf16[64,64,128]{2,1,0:T(8,128)(2,1)} %param.11) | copy-start | bytes 3145732
  4.6 24.3 %collective-permute-start.4 = (bf16[32,2176]{1,0:T(8,128)(2,1)S(1)}, bf16[32,2176]{1,0:T(8,128)(2,1)S(1)}, u32[]{:S(2)}, u32[]{:S(2)}) collective-permute-start(bf16[32,2176]{1,0:T(8,128)(2,1)S(1)} %get-tuple-element.15.refs_4_), channel_id=1, source_target_pairs={{0,12},{4,0},{8,4},{12,8},{1,13},{5,1},{9,5},{13,9},{2,14},{6,2},{... | collective-permute-start | bytes 417800 | tf_op jit(solution)/shard_map/ppermute | solution.py:364
  8.8 20.1 %collective-permute-start.6 = (bf16[32,2176]{1,0:T(8,128)(2,1)S(1)}, bf16[32,2176]{1,0:T(8,128)(2,1)S(1)}, u32[]{:S(2)}, u32[]{:S(2)}) collective-permute-start(bf16[32,2176]{1,0:T(8,128)(2,1)S(1)} %get-tuple-element.15.refs_4_), channel_id=1, source_target_pairs={{0,4},{4,8},{8,12},{12,0},{1,5},{5,9},{9,13},{13,1},{2,6},{6,10},{... | collective-permute-start | bytes 417800 | tf_op jit(solution)/shard_map/ppermute | solution.py:364
  8.8 8.9 %collective-permute-start = (bf16[32,2176]{1,0:T(8,128)(2,1)S(1)}, bf16[32,2176]{1,0:T(8,128)(2,1)S(1)}, u32[]{:S(2)}, u32[]{:S(2)}) collective-permute-start(bf16[32,2176]{1,0:T(8,128)(2,1)S(1)} %get-tuple-element.13), channel_id=1, source_target_pairs={{0,0},{1,4},{2,8},{3,12},{4,1},{5,5},{6,9},{7,13},{8,2},{9,6},{10,... | collective-permute-start | bytes 417800 | tf_op jit(solution)/shard_map/ppermute | solution.py:359
  17.7 7.3 %collective-permute-start.1 = (bf16[32,2176]{1,0:T(8,128)(2,1)S(1)}, bf16[32,2176]{1,0:T(8,128)(2,1)S(1)}, u32[]{:S(2)}, u32[]{:S(2)}) collective-permute-start(bf16[32,2176]{1,0:T(8,128)(2,1)S(1)} %collective-permute-done.refs_0_), channel_id=1, source_target_pairs={{0,2},{2,0},{1,3},{3,1},{4,6},{6,4},{5,7},{7,5},{8,10},{10,8},{9,1... | collective-permute-start | bytes 417800 | tf_op jit(solution)/shard_map/ppermute | solution.py:368
  20.9 8.0 %collective-permute-start.5 = (bf16[32,2176]{1,0:T(8,128)(2,1)S(1)}, bf16[32,2176]{1,0:T(8,128)(2,1)S(1)}, u32[]{:S(2)}, u32[]{:S(2)}) collective-permute-start(bf16[32,2176]{1,0:T(8,128)(2,1)S(1)} %get-tuple-element.15.refs_4_), channel_id=1, source_target_pairs={{0,8},{4,12},{8,0},{12,4},{1,9},{5,13},{9,1},{13,5},{2,10},{6,14},... | collective-permute-start | bytes 417800 | tf_op jit(solution)/shard_map/ppermute | solution.py:364
  23.9 5.0 %collective-permute-start.2 = (bf16[32,2176]{1,0:T(8,128)(2,1)S(1)}, bf16[32,2176]{1,0:T(8,128)(2,1)S(1)}, u32[]{:S(2)}, u32[]{:S(2)}) collective-permute-start(bf16[32,2176]{1,0:T(8,128)(2,1)S(1)} %collective-permute-done.refs_0_), channel_id=1, source_target_pairs={{0,1},{1,0},{2,3},{3,2},{4,5},{5,4},{6,7},{7,6},{8,9},{9,8},{10,11... | collective-permute-start | bytes 417800 | tf_op jit(solution)/shard_map/ppermute | solution.py:372
  25.0 3.9 %collective-permute-start.3 = (bf16[32,2176]{1,0:T(8,128)(2,1)S(1)}, bf16[32,2176]{1,0:T(8,128)(2,1)S(1)}, u32[]{:S(2)}, u32[]{:S(2)}) collective-permute-start(bf16[32,2176]{1,0:T(8,128)(2,1)S(1)} %collective-permute-done.1.refs_1_), channel_id=1, source_target_pairs={{0,1},{1,0},{2,3},{3,2},{4,5},{5,4},{6,7},{7,6},{8,9},{9,8},{10,11... | collective-permute-start | bytes 417800 | tf_op jit(solution)/shard_map/ppermute | solution.py:372
  28.7 2.2 %copy-start = (bf16[512,128]{1,0:T(8,128)(2,1)S(1)}, bf16[512,128]{1,0:T(8,128)(2,1)}, u32[]{:S(2)}) copy-start(bf16[512,128]{1,0:T(8,128)(2,1)} %down.5) | copy-start | bytes 393220
  35.9 18.6 %collective-permute-start.7 = (bf16[28,64,128]{2,0,1:T(8,128)(2,1)S(1)}, bf16[28,64,128]{2,0,1:T(8,128)(2,1)S(1)}, u32[]{:S(2)}, u32[]{:S(2)}) collective-permute-start(bf16[28,64,128]{2,0,1:T(8,128)(2,1)S(1)} %copy.27), channel_id=1, source_target_pairs={{2,0},{3,1},{6,4},{7,5},{8,10},{9,11},{12,14},{13,15},{18,16},{19,... | collective-permute-start | bytes 1376264 | tf_op jit(solution)/shard_map/ppermute | solution.py:415
  37.8 11.0 %copy-start.6 = (bf16[3,3,128,128]{3,2,1,0:T(8,128)(2,1)S(1)}, bf16[3,3,128,128]{3,2,1,0:T(8,128)(2,1)}, u32[]{:S(2)}) copy-start(bf16[3,3,128,128]{3,2,1,0:T(8,128)(2,1)} %param.21) | copy-start | bytes 884740
  37.8 32.6 %collective-permute-start.9 = (bf16[28,64,128]{2,0,1:T(8,128)(2,1)S(1)}, bf16[28,64,128]{2,0,1:T(8,128)(2,1)S(1)}, u32[]{:S(2)}, u32[]{:S(2)}) collective-permute-start(bf16[28,64,128]{2,0,1:T(8,128)(2,1)S(1)} %copy.27), channel_id=1, source_target_pairs={{0,0},{1,4},{4,1},{5,5},{10,10},{11,14},{14,11},{15,15},{16,16},{1... | collective-permute-start | bytes 1376264 | tf_op jit(solution)/shard_map/ppermute | solution.py:415
  46.3 8.2 %collective-permute-start.10 = (bf16[16,64,128]{2,0,1:T(8,128)(2,1)S(1)}, bf16[16,64,128]{2,0,1:T(8,128)(2,1)S(1)}, u32[]{:S(2)}, u32[]{:S(2)}) collective-permute-start(bf16[16,64,128]{2,0,1:T(8,128)(2,1)S(1)} %copy.28), channel_id=1, source_target_pairs={{0,0},{1,4},{2,8},{3,12},{4,1},{5,5},{6,9},{7,13},{8,2},{9,6},{10,... | collective-permute-start | bytes 786440 | tf_op jit(solution)/shard_map/ppermute | solution.py:415
  58.3 13.3 %collective-permute-start.11 = (bf16[20,64,128]{2,0,1:T(8,128)(2,1)S(1)}, bf16[20,64,128]{2,0,1:T(8,128)(2,1)S(1)}, u32[]{:S(2)}, u32[]{:S(2)}) collective-permute-start(bf16[20,64,128]{2,0,1:T(8,128)(2,1)S(1)} %copy.29), channel_id=1, source_target_pairs={{0,0},{1,4},{2,8},{3,12},{4,1},{5,5},{6,9},{7,13},{8,2},{9,6},{10,... | collective-permute-start | bytes 983048 | tf_op jit(solution)/shard_map/ppermute | solution.py:415
  60.4 17.4 %collective-permute-start.8 = (bf16[28,64,128]{2,0,1:T(8,128)(2,1)S(1)}, bf16[28,64,128]{2,0,1:T(8,128)(2,1)S(1)}, u32[]{:S(2)}, u32[]{:S(2)}) collective-permute-start(bf16[28,64,128]{2,0,1:T(8,128)(2,1)S(1)} %collective-permute-done.7), channel_id=1, source_target_pairs={{0,8},{1,12},{4,9},{5,13},{10,2},{11,6},{14,3},{15,7},{16,24},{17,... | collective-permute-start | bytes 1376264 | tf_op jit(solution)/shard_map/ppermute | solution.py:415
  78.0 22.3 %collective-permute-start.13 = (bf16[64,128]{1,0:T(8,128)(2,1)S(1)}, bf16[64,128]{1,0:T(8,128)(2,1)S(1)}, u32[]{:S(2)}, u32[]{:S(2)}) collective-permute-start(bf16[64,128]{1,0:T(8,128)(2,1)S(1)} %fusion.3), channel_id=1, source_target_pairs={{1,0},{2,1},{3,2},{5,4},{6,5},{7,6},{9,8},{10,9},{11,10},{13,12},{... | collective-permute-start | bytes 49160 | tf_op jit(solution)/shard_map/ppermute | solution.py:466
  84.9 16.1 %collective-permute-start.12 = (bf16[64,128]{1,0:T(8,128)(2,1)S(1)}, bf16[64,128]{1,0:T(8,128)(2,1)S(1)}, u32[]{:S(2)}, u32[]{:S(2)}) collective-permute-start(bf16[64,128]{1,0:T(8,128)(2,1)S(1)} %fusion.1), channel_id=1, source_target_pairs={{0,1},{1,2},{2,3},{4,5},{5,6},{6,7},{8,9},{9,10},{10,11},{12,13},{... | collective-permute-start | bytes 49160 | tf_op jit(solution)/shard_map/ppermute | solution.py:465
  101.0 5.3 %collective-permute-start.15 = (bf16[66,128]{1,0:T(8,128)(2,1)S(1)}, bf16[66,128]{1,0:T(8,128)(2,1)S(1)}, u32[]{:S(2)}, u32[]{:S(2)}) collective-permute-start(bf16[66,128]{1,0:T(8,128)(2,1)S(1)} %pad_maximum_fusion.7), channel_id=1, source_target_pairs={{4,0},{8,4},{12,8},{5,1},{9,5},{13,9},{6,2},{10,6},{14,10},{7,3},{... | collective-permute-start | bytes 50696 | tf_op jit(solution)/shard_map/ppermute | solution.py:469
  102.3 4.9 %collective-permute-start.14 = (bf16[66,128]{1,0:T(8,128)(2,1)S(1)}, bf16[66,128]{1,0:T(8,128)(2,1)S(1)}, u32[]{:S(2)}, u32[]{:S(2)}) collective-permute-start(bf16[66,128]{1,0:T(8,128)(2,1)S(1)} %pad_maximum_fusion.6), channel_id=1, source_target_pairs={{0,4},{4,8},{8,12},{1,5},{5,9},{9,13},{2,6},{6,10},{10,14},{3,7},{... | collective-permute-start | bytes 50696 | tf_op jit(solution)/shard_map/ppermute | solution.py:468
  (2 other events, 1.4 us)

commit v8 on v6

--- a/solution.py
+++ b/solution.py
@@ -405,7 +405,7 @@
     back = lambda size: [(n + 1, n) for n in range(size - 1)]
 
     if square and cols_dev % (8 * unit) == 0 and x_count > 1:
-        part = cols_dev // 8
+        part = cols_dev // 16
         host = lambda r, c: place_of(r, (r // core_count) * core_count + c % core_count)
         away = [(r, c) for r, c in tiles if r // core_count != c // core_count]
         near = [(r, c) for r, c in tiles if r // core_count == c // core_count]
@@ -413,10 +413,10 @@
         from_host = [(host(r, c), place_of(c, r)) for r, c in away]
         beside_pairs = [(place_of(r, c), place_of(c, r)) for r, c in near]
         send = lambda value, pairs: lax.ppermute(value, whole, pairs)
-        opening = run(0, 3 * part)
+        opening = run(0, 7 * part)
         hosted = send(opening, to_host)
         mirrored_near = send(opening, beside_pairs)
-        rest = run(3 * part, 5 * part, opening)
+        rest = run(7 * part, 9 * part, opening)
         mirrored_rest = send(rest, mirror_pairs)
         mirrored_away = send(hosted, from_host)
         turned = jnp.concatenate([opening, rest], axis=0)

time: 104 us -> 111 us (1.067)
  the two profiles are of different devices: /device:TPU:14 before, /device:TPU:1 now
where the time goes in v8:
time: 111 us; the launch traced here: 110 us
  starting transfers between devices  45.8 us (41%)
  waiting for transfers between devices  31.6 us (28%)
  Pallas kernels  17.8 us (16%)
  local copies, waits for them, and re-layouts  9.07 us (8%)
  other arithmetic  5.19 us (5%)
    ppermute x4, waiting for transfers between devices, on_device(): send = lambda value, pairs: lax.ppermute(value, whole, pairs)  23.9 us
    ppermute x1, starting transfers between devices, on_device(): left = lax.ppermute(last_side, plane, ahead(col_count))  11.9 us
    pallas_call x2, Pallas kernels, tile_strip(): pl.pallas_call(functools.partial(tile_kernel, first=first, width=width),...  10.7 us
    ppermute x4, starting transfers between devices, on_device(): send = lambda value, pairs: lax.ppermute(value, whole, pairs)  10.4 us
    ppermute x3, starting transfers between devices, on_device(): col_side.append(lax.ppermute(block, 'row', shifts(row_count, -step)))  7.38 us
    ppermute x1, starting transfers between devices, on_device(): top = lax.ppermute(border(last_i, last_line), 'row', ahead(row_count))  4.33 us
    pallas_call x1, Pallas kernels, convolve(): pl.pallas_call(functools.partial(conv_kernel, parts=[tuple(range(len(part...  4.21 us
    ppermute x1, starting transfers between devices, on_device(): row_side.append(lax.ppermute(first, 'col', shifts(x_count, -step)))  3.36 us
  transfers between devices with their start and end apart: 15, of which 6 were waited for; matrix products, arithmetic and copies ran while one was open for 9% of the time, Pallas kernels for 0%

profile of v8, /device:TPU:1, one launch (start us, length us, event | category | flops | bytes accessed | tf_op | source)
XLA Modules:
  0.0 110.1 jit_solution(14148309743562681581)
XLA Ops:
  0.0 1.6 %reshape.46.features = bf16[32,4096]{1,0:T(8,128)(2,1)S(1)} reshape(bf16[32,64,64]{2,1,0:T(8,128)(2,1)} %param.12) | data formatting | bytes 524288 | tf_op jit(solution)/shard_map/reshape | solution.py:70
  4.6 2.2 %collective-permute-start.6 = (bf16[32,2176]{1,0:T(8,128)(2,1)S(1)}, bf16[32,2176]{1,0:T(8,128)(2,1)S(1)}, u32[]{:S(2)}, u32[]{:S(2)}) collective-permute-start(bf16[32,2176]{1,0:T(8,128)(2,1)S(1)} %get-tuple-element.14.refs_4_), channel_id=1, source_target_pairs={{0,4},{4,8},{8,12},{12,0},{1,5},{5,9},{9,13},{13,1},{2,6},{6,10},{... | collective-permute-start | bytes 417800 | tf_op jit(solution)/shard_map/ppermute | solution.py:364
  6.8 2.1 %collective-permute-start.4 = (bf16[32,2176]{1,0:T(8,128)(2,1)S(1)}, bf16[32,2176]{1,0:T(8,128)(2,1)S(1)}, u32[]{:S(2)}, u32[]{:S(2)}) collective-permute-start(bf16[32,2176]{1,0:T(8,128)(2,1)S(1)} %get-tuple-element.14.refs_4_), channel_id=1, source_target_pairs={{0,12},{4,0},{8,4},{12,8},{1,13},{5,1},{9,5},{13,9},{2,14},{6,2},{... | collective-permute-start | bytes 417800 | tf_op jit(solution)/shard_map/ppermute | solution.py:364
  8.8 2.4 %collective-permute-start = (bf16[32,2176]{1,0:T(8,128)(2,1)S(1)}, bf16[32,2176]{1,0:T(8,128)(2,1)S(1)}, u32[]{:S(2)}, u32[]{:S(2)}) collective-permute-start(bf16[32,2176]{1,0:T(8,128)(2,1)S(1)} %get-tuple-element.12), channel_id=1, source_target_pairs={{0,0},{1,4},{2,8},{3,12},{4,1},{5,5},{6,9},{7,13},{8,2},{9,6},{10,... | collective-permute-start | bytes 417800 | tf_op jit(solution)/shard_map/ppermute | solution.py:359
  15.1 1.5 %collective-permute-done.refs_0_ = bf16[32,2176]{1,0:T(8,128)(2,1)S(1)} collective-permute-done((bf16[32,2176]{1,0:T(8,128)(2,1)S(1)}, bf16[32,2176]{1,0:T(8,128)(2,1)S(1)}, u32[]{:S(2)}, u32[]{:S(2)}) %collective-permute-start) | collective-permute-done | bytes 139296 | tf_op jit(solution)/shard_map/ppermute | solution.py:359
  16.6 3.4 %collective-permute-start.1 = (bf16[32,2176]{1,0:T(8,128)(2,1)S(1)}, bf16[32,2176]{1,0:T(8,128)(2,1)S(1)}, u32[]{:S(2)}, u32[]{:S(2)}) collective-permute-start(bf16[32,2176]{1,0:T(8,128)(2,1)S(1)} %collective-permute-done.refs_0_), channel_id=1, source_target_pairs={{0,2},{2,0},{1,3},{3,1},{4,6},{6,4},{5,7},{7,5},{8,10},{10,8},{9,1... | collective-permute-start | bytes 417800 | tf_op jit(solution)/shard_map/ppermute | solution.py:368
  21.0 3.1 %collective-permute-start.5 = (bf16[32,2176]{1,0:T(8,128)(2,1)S(1)}, bf16[32,2176]{1,0:T(8,128)(2,1)S(1)}, u32[]{:S(2)}, u32[]{:S(2)}) collective-permute-start(bf16[32,2176]{1,0:T(8,128)(2,1)S(1)} %get-tuple-element.14.refs_4_), channel_id=1, source_target_pairs={{0,8},{4,12},{8,0},{12,4},{1,9},{5,13},{9,1},{13,5},{2,10},{6,14},... | collective-permute-start | bytes 417800 | tf_op jit(solution)/shard_map/ppermute | solution.py:364
  25.0 1.9 %collective-permute-start.3 = (bf16[32,2176]{1,0:T(8,128)(2,1)S(1)}, bf16[32,2176]{1,0:T(8,128)(2,1)S(1)}, u32[]{:S(2)}, u32[]{:S(2)}) collective-permute-start(bf16[32,2176]{1,0:T(8,128)(2,1)S(1)} %collective-permute-done.1.refs_1_), channel_id=1, source_target_pairs={{0,1},{1,0},{2,3},{3,2},{4,5},{5,4},{6,7},{7,6},{8,9},{9,8},{10,11... | collective-permute-start | bytes 417800 | tf_op jit(solution)/shard_map/ppermute | solution.py:372
  28.0 2.0 %shard_map.110 = (bf16[2048,128]{1,0:T(8,128)(2,1)S(1)}, bf16[4,128,2048]{2,1,0:T(8,128)(2,1)S(1)}, f32[8,64,128]{2,1,0:T(8,128)S(1)}) custom-call(s32[8]{0:T(128)S(1)} %broadcast_multiply_fusion.1.places, bf16[32,2176]{1,0:T(8,128)(2,1)S(1)} %collective-permute-done.refs_0_, bf16[32,2176]{1,0:T(8,128)(2,1)S(1)} %collective-permute-done.1.refs_1_, ...), custom_call_target="tpu_custom_call" | custom-call | flops 1024 | bytes 1024 | tf_op jit(solution)/shard_map/pallas_call | solution.py:126
  30.1 4.6 %shard_map.111 = bf16[28,64,128]{2,1,0:T(8,128)(2,1)S(1)} custom-call(bf16[2048,128]{1,0:T(8,128)(2,1)S(1)} %get-tuple-element.18.row_side, bf16[4,128,2048]{2,1,0:T(8,128)(2,1)S(1)} %get-tuple-element.16.lane_side, f32[8,64,128]{2,1,0:T(8,128)S(1)} %get-tuple-element.17.scale, bf16[64,64,128]{2,1,0:T(8,128)(2,1)S(1)} %bitcast.56, ...), custom_call_target="tpu_custom_call" | custom-call | flops 1024 | bytes 1024 | tf_op jit(solution)/shard_map/pallas_call | solution.py:223
  34.7 6.1 %shard_map.112 = bf16[36,64,128]{2,1,0:T(8,128)(2,1)S(1)} custom-call(bf16[2048,128]{1,0:T(8,128)(2,1)S(1)} %get-tuple-element.18.row_side, bf16[4,128,2048]{2,1,0:T(8,128)(2,1)S(1)} %get-tuple-element.16.lane_side, f32[8,64,128]{2,1,0:T(8,128)S(1)} %get-tuple-element.17.scale, bf16[64,64,128]{2,1,0:T(8,128)(2,1)S(1)} %bitcast.57, ...), custom_call_target="tpu_custom_call" | custom-call | flops 1024 | bytes 1024 | tf_op jit(solution)/shard_map/pallas_call | solution.py:223
  40.8 5.8 %collective-permute-start.10 = (bf16[36,64,128]{2,1,0:T(8,128)(2,1)S(1)}, bf16[36,64,128]{2,1,0:T(8,128)(2,1)S(1)}, u32[]{:S(2)}, u32[]{:S(2)}) collective-permute-start(bf16[36,64,128]{2,1,0:T(8,128)(2,1)S(1)} %shard_map.112), channel_id=1, source_target_pairs={{0,0},{1,4},{2,8},{3,12},{4,1},{5,5},{6,9},{7,13},{8,2},{9,6},{10,... | collective-permute-start | bytes 1769480 | tf_op jit(solution)/shard_map/ppermute | solution.py:415
  47.6 1.9 %collective-permute-start.9 = (bf16[28,64,128]{2,0,1:T(8,128)(2,1)S(1)}, bf16[28,64,128]{2,0,1:T(8,128)(2,1)S(1)}, u32[]{:S(2)}, u32[]{:S(2)}) collective-permute-start(bf16[28,64,128]{2,0,1:T(8,128)(2,1)S(1)} %copy.33), channel_id=1, source_target_pairs={{0,0},{1,4},{4,1},{5,5},{10,10},{11,14},{14,11},{15,15},{16,16},{1... | collective-permute-start | bytes 1376264 | tf_op jit(solution)/shard_map/ppermute | solution.py:415
  49.5 1.3 %collective-permute-start.7 = (bf16[28,64,128]{2,0,1:T(8,128)(2,1)S(1)}, bf16[28,64,128]{2,0,1:T(8,128)(2,1)S(1)}, u32[]{:S(2)}, u32[]{:S(2)}) collective-permute-start(bf16[28,64,128]{2,0,1:T(8,128)(2,1)S(1)} %copy.33), channel_id=1, source_target_pairs={{2,0},{3,1},{6,4},{7,5},{8,10},{9,11},{12,14},{13,15},{18,16},{19,... | collective-permute-start | bytes 1376264 | tf_op jit(solution)/shard_map/ppermute | solution.py:415
  53.5 15.8 %collective-permute-done.9 = bf16[28,64,128]{2,0,1:T(8,128)(2,1)S(1)} collective-permute-done((bf16[28,64,128]{2,0,1:T(8,128)(2,1)S(1)}, bf16[28,64,128]{2,0,1:T(8,128)(2,1)S(1)}, u32[]{:S(2)}, u32[]{:S(2)}) %collective-permute-start.9) | collective-permute-done | bytes 458784 | tf_op jit(solution)/shard_map/ppermute | solution.py:415
  69.6 1.3 %collective-permute-start.8 = (bf16[28,64,128]{2,0,1:T(8,128)(2,1)S(1)}, bf16[28,64,128]{2,0,1:T(8,128)(2,1)S(1)}, u32[]{:S(2)}, u32[]{:S(2)}) collective-permute-start(bf16[28,64,128]{2,0,1:T(8,128)(2,1)S(1)} %collective-permute-done.7), channel_id=1, source_target_pairs={{0,8},{1,12},{4,9},{5,13},{10,2},{11,6},{14,3},{15,7},{16,24},{17,... | collective-permute-start | bytes 1376264 | tf_op jit(solution)/shard_map/ppermute | solution.py:415
  71.4 8.1 %collective-permute-done.8 = bf16[28,64,128]{2,0,1:T(8,128)(2,1)S(1)} collective-permute-done((bf16[28,64,128]{2,0,1:T(8,128)(2,1)S(1)}, bf16[28,64,128]{2,0,1:T(8,128)(2,1)S(1)}, u32[]{:S(2)}, u32[]{:S(2)}) %collective-permute-start.8) | collective-permute-done | bytes 458784 | tf_op jit(solution)/shard_map/ppermute | solution.py:415
  79.8 11.9 %collective-permute-start.11 = (bf16[64,128]{1,0:T(8,128)(2,1)S(1)}, bf16[64,128]{1,0:T(8,128)(2,1)S(1)}, u32[]{:S(2)}, u32[]{:S(2)}) collective-permute-start(bf16[64,128]{1,0:T(8,128)(2,1)S(1)} %fusion.2), channel_id=1, source_target_pairs={{0,1},{1,2},{2,3},{4,5},{5,6},{6,7},{8,9},{9,10},{10,11},{12,13},{... | collective-permute-start | bytes 49160 | tf_op jit(solution)/shard_map/ppermute | solution.py:463
  91.8 1.9 %collective-permute-start.12 = (bf16[64,128]{1,0:T(8,128)(2,1)S(1)}, bf16[64,128]{1,0:T(8,128)(2,1)S(1)}, u32[]{:S(2)}, u32[]{:S(2)}) collective-permute-start(bf16[64,128]{1,0:T(8,128)(2,1)S(1)} %fusion.4), channel_id=1, source_target_pairs={{1,0},{2,1},{3,2},{5,4},{6,5},{7,6},{9,8},{10,9},{11,10},{13,12},{... | collective-permute-start | bytes 49160 | tf_op jit(solution)/shard_map/ppermute | solution.py:464
  94.0 2.8 %collective-permute-done.12 = bf16[64,128]{1,0:T(8,128)(2,1)S(1)} collective-permute-done((bf16[64,128]{1,0:T(8,128)(2,1)S(1)}, bf16[64,128]{1,0:T(8,128)(2,1)S(1)}, u32[]{:S(2)}, u32[]{:S(2)}) %collective-permute-start.12) | collective-permute-done | bytes 16416 | tf_op jit(solution)/shard_map/ppermute | solution.py:464
  96.9 4.3 %collective-permute-start.13 = (bf16[66,128]{1,0:T(8,128)(2,1)S(1)}, bf16[66,128]{1,0:T(8,128)(2,1)S(1)}, u32[]{:S(2)}, u32[]{:S(2)}) collective-permute-start(bf16[66,128]{1,0:T(8,128)(2,1)S(1)} %pad_maximum_fusion.6), channel_id=1, source_target_pairs={{0,4},{4,8},{8,12},{1,5},{5,9},{9,13},{2,6},{6,10},{10,14},{3,7},{... | collective-permute-start | bytes 50696 | tf_op jit(solution)/shard_map/ppermute | solution.py:466
  101.2 1.3 %collective-permute-start.14 = (bf16[66,128]{1,0:T(8,128)(2,1)S(1)}, bf16[66,128]{1,0:T(8,128)(2,1)S(1)}, u32[]{:S(2)}, u32[]{:S(2)}) collective-permute-start(bf16[66,128]{1,0:T(8,128)(2,1)S(1)} %pad_maximum_fusion.7), channel_id=1, source_target_pairs={{4,0},{8,4},{12,8},{5,1},{9,5},{13,9},{6,2},{10,6},{14,10},{7,3},{... | collective-permute-start | bytes 50696 | tf_op jit(solution)/shard_map/ppermute | solution.py:467
  102.5 3.2 %collective-permute-done.14 = bf16[66,128]{1,0:T(8,128)(2,1)S(1)} collective-permute-done((bf16[66,128]{1,0:T(8,128)(2,1)S(1)}, bf16[66,128]{1,0:T(8,128)(2,1)S(1)}, u32[]{:S(2)}, u32[]{:S(2)}) %collective-permute-start.14) | collective-permute-done | bytes 16928 | tf_op jit(solution)/shard_map/ppermute | solution.py:467
  105.8 4.2 %shard_map.113 = bf16[64,64,128]{2,1,0:T(8,128)(2,1)} custom-call(s32[64]{0:T(128)S(1)} %get-tuple-element.22.valid_i, bf16[64,64,128]{2,1,0:T(8,128)(2,1)S(1)} %fusion.pair_two, bf16[28,64,128]{2,1,0:T(8,128)(2,1)S(1)} %copy.39.refs_0_, bf16[28,64,128]{2,1,0:T(8,128)(2,1)S(1)} %copy.40.refs_1_, bf16[36,64,128]{2,1,0:T(8,128)(2,1)S(1)} %collective-permute-done.10.refs_2_, ...), custom_call_target="tpu_custom_call" | custom-call | flops 1207959552 | bytes 3145728 | tf_op jit(solution)/shard_map/pallas_call | solution.py:292
  (75 shorter events, 14.7 us)
Async XLA Ops:
  0.0 13.2 %copy-start.4 = (bf16[1024,128]{1,0:T(8,128)(2,1)S(1)}, bf16[1024,128]{1,0:T(8,128)(2,1)}, u32[]{:S(2)}) copy-start(bf16[1024,128]{1,0:T(8,128)(2,1)} %param.17) | copy-start | bytes 786436
  0.0 13.4 %copy-start.7 = (bf16[128,512]{1,0:T(8,128)(2,1)S(1)}, bf16[128,512]{1,0:T(8,128)(2,1)}, u32[]{:S(2)}) copy-start(bf16[128,512]{1,0:T(8,128)(2,1)} %param.18) | copy-start | bytes 393220
  0.0 13.4 %copy-start.8 = (s32[256]{0:T(256)S(1)}, s32[256]{0:T(256)}, u32[]{:S(2)}) copy-start(s32[256]{0:T(256)} %param.14) | copy-start | bytes 3076
  0.0 20.6 %copy-start.6 = (bf16[3,3,128,128]{3,2,1,0:T(8,128)(2,1)S(1)}, bf16[3,3,128,128]{3,2,1,0:T(8,128)(2,1)}, u32[]{:S(2)}) copy-start(bf16[3,3,128,128]{3,2,1,0:T(8,128)(2,1)} %param.21) | copy-start | bytes 884740
  1.6 0.7 copy-start.1
  2.3 0.7 copy-start.2
  3.0 0.7 copy-start.3
  4.6 23.3 %collective-permute-start.6 = (bf16[32,2176]{1,0:T(8,128)(2,1)S(1)}, bf16[32,2176]{1,0:T(8,128)(2,1)S(1)}, u32[]{:S(2)}, u32[]{:S(2)}) collective-permute-start(bf16[32,2176]{1,0:T(8,128)(2,1)S(1)} %get-tuple-element.14.refs_4_), channel_id=1, source_target_pairs={{0,4},{4,8},{8,12},{12,0},{1,5},{5,9},{9,13},{13,1},{2,6},{6,10},{... | collective-permute-start | bytes 417800 | tf_op jit(solution)/shard_map/ppermute | solution.py:364
  6.8 21.1 %collective-permute-start.4 = (bf16[32,2176]{1,0:T(8,128)(2,1)S(1)}, bf16[32,2176]{1,0:T(8,128)(2,1)S(1)}, u32[]{:S(2)}, u32[]{:S(2)}) collective-permute-start(bf16[32,2176]{1,0:T(8,128)(2,1)S(1)} %get-tuple-element.14.refs_4_), channel_id=1, source_target_pairs={{0,12},{4,0},{8,4},{12,8},{1,13},{5,1},{9,5},{13,9},{2,14},{6,2},{... | collective-permute-start | bytes 417800 | tf_op jit(solution)/shard_map/ppermute | solution.py:364
  8.8 7.8 %collective-permute-start = (bf16[32,2176]{1,0:T(8,128)(2,1)S(1)}, bf16[32,2176]{1,0:T(8,128)(2,1)S(1)}, u32[]{:S(2)}, u32[]{:S(2)}) collective-permute-start(bf16[32,2176]{1,0:T(8,128)(2,1)S(1)} %get-tuple-element.12), channel_id=1, source_target_pairs={{0,0},{1,4},{2,8},{3,12},{4,1},{5,5},{6,9},{7,13},{8,2},{9,6},{10,... | collective-permute-start | bytes 417800 | tf_op jit(solution)/shard_map/ppermute | solution.py:359
  13.2 13.8 %copy-start.5 = (bf16[64,64,128]{2,1,0:T(8,128)(2,1)S(1)}, bf16[64,64,128]{2,1,0:T(8,128)(2,1)}, u32[]{:S(2)}) copy-start(bf16[64,64,128]{2,1,0:T(8,128)(2,1)} %param.11) | copy-start | bytes 3145732
  16.6 8.4 %collective-permute-start.1 = (bf16[32,2176]{1,0:T(8,128)(2,1)S(1)}, bf16[32,2176]{1,0:T(8,128)(2,1)S(1)}, u32[]{:S(2)}, u32[]{:S(2)}) collective-permute-start(bf16[32,2176]{1,0:T(8,128)(2,1)S(1)} %collective-permute-done.refs_0_), channel_id=1, source_target_pairs={{0,2},{2,0},{1,3},{3,1},{4,6},{6,4},{5,7},{7,5},{8,10},{10,8},{9,1... | collective-permute-start | bytes 417800 | tf_op jit(solution)/shard_map/ppermute | solution.py:368
  21.0 7.1 %collective-permute-start.5 = (bf16[32,2176]{1,0:T(8,128)(2,1)S(1)}, bf16[32,2176]{1,0:T(8,128)(2,1)S(1)}, u32[]{:S(2)}, u32[]{:S(2)}) collective-permute-start(bf16[32,2176]{1,0:T(8,128)(2,1)S(1)} %get-tuple-element.14.refs_4_), channel_id=1, source_target_pairs={{0,8},{4,12},{8,0},{12,4},{1,9},{5,13},{9,1},{13,5},{2,10},{6,14},... | collective-permute-start | bytes 417800 | tf_op jit(solution)/shard_map/ppermute | solution.py:364
  24.1 3.9 %collective-permute-start.2 = (bf16[32,2176]{1,0:T(8,128)(2,1)S(1)}, bf16[32,2176]{1,0:T(8,128)(2,1)S(1)}, u32[]{:S(2)}, u32[]{:S(2)}) collective-permute-start(bf16[32,2176]{1,0:T(8,128)(2,1)S(1)} %collective-permute-done.refs_0_), channel_id=1, source_target_pairs={{0,1},{1,0},{2,3},{3,2},{4,5},{5,4},{6,7},{7,6},{8,9},{9,8},{10,11... | collective-permute-start | bytes 417800 | tf_op jit(solution)/shard_map/ppermute | solution.py:372
  25.0 3.0 %collective-permute-start.3 = (bf16[32,2176]{1,0:T(8,128)(2,1)S(1)}, bf16[32,2176]{1,0:T(8,128)(2,1)S(1)}, u32[]{:S(2)}, u32[]{:S(2)}) collective-permute-start(bf16[32,2176]{1,0:T(8,128)(2,1)S(1)} %collective-permute-done.1.refs_1_), channel_id=1, source_target_pairs={{0,1},{1,0},{2,3},{3,2},{4,5},{5,4},{6,7},{7,6},{8,9},{9,8},{10,11... | collective-permute-start | bytes 417800 | tf_op jit(solution)/shard_map/ppermute | solution.py:372
  27.7 2.4 %copy-start = (bf16[512,128]{1,0:T(8,128)(2,1)S(1)}, bf16[512,128]{1,0:T(8,128)(2,1)}, u32[]{:S(2)}) copy-start(bf16[512,128]{1,0:T(8,128)(2,1)} %down.3) | copy-start | bytes 393220
  40.8 30.2 %collective-permute-start.10 = (bf16[36,64,128]{2,1,0:T(8,128)(2,1)S(1)}, bf16[36,64,128]{2,1,0:T(8,128)(2,1)S(1)}, u32[]{:S(2)}, u32[]{:S(2)}) collective-permute-start(bf16[36,64,128]{2,1,0:T(8,128)(2,1)S(1)} %shard_map.112), channel_id=1, source_target_pairs={{0,0},{1,4},{2,8},{3,12},{4,1},{5,5},{6,9},{7,13},{8,2},{9,6},{10,... | collective-permute-start | bytes 1769480 | tf_op jit(solution)/shard_map/ppermute | solution.py:415
  47.6 21.7 %collective-permute-start.9 = (bf16[28,64,128]{2,0,1:T(8,128)(2,1)S(1)}, bf16[28,64,128]{2,0,1:T(8,128)(2,1)S(1)}, u32[]{:S(2)}, u32[]{:S(2)}) collective-permute-start(bf16[28,64,128]{2,0,1:T(8,128)(2,1)S(1)} %copy.33), channel_id=1, source_target_pairs={{0,0},{1,4},{4,1},{5,5},{10,10},{11,14},{14,11},{15,15},{16,16},{1... | collective-permute-start | bytes 1376264 | tf_op jit(solution)/shard_map/ppermute | solution.py:415
  49.5 20.1 %collective-permute-start.7 = (bf16[28,64,128]{2,0,1:T(8,128)(2,1)S(1)}, bf16[28,64,128]{2,0,1:T(8,128)(2,1)S(1)}, u32[]{:S(2)}, u32[]{:S(2)}) collective-permute-start(bf16[28,64,128]{2,0,1:T(8,128)(2,1)S(1)} %copy.33), channel_id=1, source_target_pairs={{2,0},{3,1},{6,4},{7,5},{8,10},{9,11},{12,14},{13,15},{18,16},{19,... | collective-permute-start | bytes 1376264 | tf_op jit(solution)/shard_map/ppermute | solution.py:415
  69.6 9.8 %collective-permute-start.8 = (bf16[28,64,128]{2,0,1:T(8,128)(2,1)S(1)}, bf16[28,64,128]{2,0,1:T(8,128)(2,1)S(1)}, u32[]{:S(2)}, u32[]{:S(2)}) collective-permute-start(bf16[28,64,128]{2,0,1:T(8,128)(2,1)S(1)} %collective-permute-done.7), channel_id=1, source_target_pairs={{0,8},{1,12},{4,9},{5,13},{10,2},{11,6},{14,3},{15,7},{16,24},{17,... | collective-permute-start | bytes 1376264 | tf_op jit(solution)/shard_map/ppermute | solution.py:415
  79.8 14.2 %collective-permute-start.11 = (bf16[64,128]{1,0:T(8,128)(2,1)S(1)}, bf16[64,128]{1,0:T(8,128)(2,1)S(1)}, u32[]{:S(2)}, u32[]{:S(2)}) collective-permute-start(bf16[64,128]{1,0:T(8,128)(2,1)S(1)} %fusion.2), channel_id=1, source_target_pairs={{0,1},{1,2},{2,3},{4,5},{5,6},{6,7},{8,9},{9,10},{10,11},{12,13},{... | collective-permute-start | bytes 49160 | tf_op jit(solution)/shard_map/ppermute | solution.py:463
  91.8 5.0 %collective-permute-start.12 = (bf16[64,128]{1,0:T(8,128)(2,1)S(1)}, bf16[64,128]{1,0:T(8,128)(2,1)S(1)}, u32[]{:S(2)}, u32[]{:S(2)}) collective-permute-start(bf16[64,128]{1,0:T(8,128)(2,1)S(1)} %fusion.4), channel_id=1, source_target_pairs={{1,0},{2,1},{3,2},{5,4},{6,5},{7,6},{9,8},{10,9},{11,10},{13,12},{... | collective-permute-start | bytes 49160 | tf_op jit(solution)/shard_map/ppermute | solution.py:464
  96.9 5.7 %collective-permute-start.13 = (bf16[66,128]{1,0:T(8,128)(2,1)S(1)}, bf16[66,128]{1,0:T(8,128)(2,1)S(1)}, u32[]{:S(2)}, u32[]{:S(2)}) collective-permute-start(bf16[66,128]{1,0:T(8,128)(2,1)S(1)} %pad_maximum_fusion.6), channel_id=1, source_target_pairs={{0,4},{4,8},{8,12},{1,5},{5,9},{9,13},{2,6},{6,10},{10,14},{3,7},{... | collective-permute-start | bytes 50696 | tf_op jit(solution)/shard_map/ppermute | solution.py:466
  101.2 4.5 %collective-permute-start.14 = (bf16[66,128]{1,0:T(8,128)(2,1)S(1)}, bf16[66,128]{1,0:T(8,128)(2,1)S(1)}, u32[]{:S(2)}, u32[]{:S(2)}) collective-permute-start(bf16[66,128]{1,0:T(8,128)(2,1)S(1)} %pad_maximum_fusion.7), channel_id=1, source_target_pairs={{4,0},{8,4},{12,8},{5,1},{9,5},{13,9},{6,2},{10,6},{14,10},{7,3},{... | collective-permute-start | bytes 50696 | tf_op jit(solution)/shard_map/ppermute | solution.py:467
